TPU v7x, 32 devices: a whole 2x2x4 slice. The times are simulated.
32 devices in a mesh: group: 2 (over x), expert: 16 (over z, y, core).
Axes of the slice: x: 2, y: 2, z: 4, core: 2. Of those that a mesh axis runs over, the one named last changes fastest.
Arguments:
- hidden: bfloat16 [4096, 4096], P(('group', 'expert')), parts along dimension 0, may hold values from -6 to 6
- norm_gain: bfloat16 [4096], replicated, may hold values from 0.25 to 1.75
- router_weight: bfloat16 [4096, 128], replicated, may hold values from -0.03125 to 0.03125
- expert_ids: int32 [4096, 8], P(('group', 'expert')), parts along dimension 0, may hold values from 0 to 127, all different within a row; in each aligned block of 128 rows (0 to 127, 128 to 255, ...) at most 16 rows name the same one
- gate_weight: bfloat16 [16, 4096, 384], P('expert'), may hold values from -0.09375 to 0.09375
- up_weight: bfloat16 [16, 4096, 384], P('expert'), may hold values from -0.09375 to 0.09375
- down_weight: bfloat16 [16, 384, 4096], P('expert'), may hold values from -0.625 to 0.625
Outputs:
- moe_out: bfloat16 [4096, 4096], P(('group', 'expert')), parts along dimension 0
There are 2 independent parts, one for each index of `group`. A program takes and returns all parts, laid end to end along the dimension named above; an argument that names none is the same for every part. Nothing has to cross between parts.
Inputs may be any that keep to these rules, and one draw needn't show every extreme that they name: `expert_ids`: each row names 8 different experts; in each aligned block of 128 rows (the rows of one device) no expert is named by more than 16 rows.
All inputs are finite; a program needn't handle non-finite values.
Results may differ from a plain program's by a relative error of at most 0.0077.
Values may be sent and summed in bfloat16 or wider, within the bound.
No kernel may reach another device: no remote copies, remote signals or barrier semaphores. Data moves between devices by JAX's collectives and lax.ppermute only.
A program may use at most 128 MiB of HBM per device.

v0:
```python
import jax
import jax.numpy as jnp
from jax import lax
from jax.sharding import PartitionSpec as P

SPLIT = 4
CAP = 16


def expert_rows(row_block, gate_weight, up_weight, down_weight):
    gate_act = jnp.dot(row_block, gate_weight[0], preferred_element_type=jnp.float32)
    up_act = jnp.dot(row_block, up_weight[0], preferred_element_type=jnp.float32)
    hidden_act = (jax.nn.silu(gate_act) * up_act).astype(jnp.bfloat16)
    return jnp.dot(hidden_act, down_weight[0], preferred_element_type=jnp.float32).astype(
        jnp.bfloat16
    )


def shards(hidden, norm_gain, router_weight, expert_ids, gate_weight, up_weight, down_weight):
    devices = lax.axis_size("expert")
    flight = devices // SPLIT
    tok_rows = hidden.shape[0]
    model_width = hidden.shape[1]
    pick_count = expert_ids.shape[1]
    widened = hidden.astype(jnp.float32)
    inv_rms = lax.rsqrt(jnp.mean(widened * widened, axis=-1, keepdims=True) + 1e-06)
    normed = (widened * inv_rms * norm_gain.astype(jnp.float32)).astype(jnp.bfloat16)
    logits = jnp.dot(normed, router_weight, preferred_element_type=jnp.float32)
    router_probs = jax.nn.softmax(logits, axis=-1)
    picked = jnp.take_along_axis(router_probs, expert_ids, axis=1)
    gate_share = picked / jnp.sum(picked, axis=1, keepdims=True)
    flat_ids = expert_ids.reshape(-1)
    onehot = (flat_ids[:, None] == jnp.arange(flight, dtype=jnp.int32)[None, :]).astype(jnp.int32)
    before = jnp.cumsum(onehot, axis=0) - onehot
    slot_index = jnp.sum(before * onehot, axis=1)
    is_live = jnp.sum(onehot, axis=1) > 0
    owner = jnp.where(is_live, flat_ids, 0)
    column = owner * CAP + slot_index
    select = (column[:, None] == jnp.arange(flight * CAP, dtype=jnp.int32)[None, :]) & is_live[
        :, None
    ]
    select = select.reshape(tok_rows, pick_count, flight * CAP)
    dispatch = jnp.any(select, axis=1).astype(jnp.bfloat16)
    outgoing = jnp.einsum("tc,td->cd", dispatch, normed, preferred_element_type=jnp.float32).astype(
        jnp.bfloat16
    )
    sending = jnp.tile(outgoing.reshape(flight, CAP, model_width), (SPLIT, 1, 1))
    arrived = lax.all_to_all(sending, "expert", split_axis=0, concat_axis=0, tiled=True)
    row_count = arrived.shape[1]
    partial_value = expert_rows(
        arrived.reshape(-1, model_width), gate_weight, up_weight, down_weight
    )
    partial_value = partial_value.reshape(devices, row_count, model_width)
    returned = lax.all_to_all(partial_value, "expert", split_axis=0, concat_axis=0, tiled=True)
    summed = jnp.sum(
        returned.reshape(SPLIT, flight, row_count, model_width).astype(jnp.float32), axis=0
    )
    results = summed.astype(jnp.bfloat16)
    results = results.reshape(flight * CAP, model_width)
    pick_rows = jnp.take(results, column, axis=0).reshape(tok_rows, pick_count, model_width)
    pick_weight = jnp.where(is_live, gate_share.reshape(-1), 0.0).reshape(tok_rows, pick_count)
    moe_out = jnp.zeros((tok_rows, model_width), jnp.float32)
    for pick in range(pick_count):
        moe_out = moe_out + pick_weight[:, pick][:, None] * pick_rows[:, pick].astype(jnp.float32)
    return moe_out.astype(jnp.bfloat16)


def solution(mesh):
    in_specs = (
        P(("group", "expert"), None),
        P(),
        P(),
        P(("group", "expert"), None),
        P("expert", None, None),
        P("expert", None, None),
        P("expert", None, None),
    )
    out_specs = P(("group", "expert"), None)
    return jax.shard_map(shards, mesh=mesh, in_specs=in_specs, out_specs=out_specs, check_vma=False)
```

profile of v0, /device:TPU:15, one launch (start us, length us, event | category | flops | bytes accessed | tf_op | source)
XLA Modules:
  0.0 165.2 jit_solution(15530889888116270357)
XLA Ops:
  0.0 0.0 copy-start
  0.0 0.9 copy.46
  0.9 0.1 eq.43
  1.0 0.1 eq.39
  1.1 1.5 fusion.5
  2.7 0.7 convert_element_type.81
  3.4 1.1 reduce-window.6
  4.5 0.2 slice_reduce_fusion
  4.7 0.2 reduce-window.9
  4.9 0.1 add_bitcast_fusion
  5.0 0.1 gt.35
  5.1 0.1 copy.49
  5.2 0.1 reduce_sum.66
  5.3 0.7 compare_and_fusion
  6.1 1.7 %convolution_convert_fusion.1 = bf16[64,4096]{1,0:T(8,128)(2,1)S(1)} fusion(pred[128,64]{0,1:T(8,128)(4,1)S(1)} %fusion.33, bf16[128,4096]{1,0:T(8,128)(2,1)} %param.7, f32[4096]{0:T(1024)S(1)} %convert_element_type.81, f32[128]{0:T(128)S(1)} %add_rsqrt_fusion), kind=kOutput, calls=%fused_computation.4 | convolution fusion | flops 69468160 | bytes 1597952 | tf_op jit(solution)/shard_map/tc,td->cd/dot_general | solution.py:44
  7.8 0.2 tile.11
  8.1 0.0 copy-start.3
  8.1 53.9 %all_to_all.10 = bf16[16,16,4096]{2,1,0:T(8,128)(2,1)S(1)} all-to-all(bf16[16,16,4096]{2,1,0:T(8,128)(2,1)S(1)} %bitcast.101), channel_id=1, replica_groups=mesh['group'=2,'expert'=16] {'expert'}, dimensions={0} | all-to-all | bytes 4194304 | tf_op jit(solution)/shard_map/all_to_all | solution.py:48
  62.0 0.0 copy-start.1
  62.0 1.3 copy-done.1
  63.3 0.0 copy-done.3
  63.3 2.1 %fusion.3 = f32[256,384]{1,0:T(8,128)} fusion(bf16[256,4096]{1,0:T(8,128)(2,1)S(1)} %bitcast.103, bf16[1,4096,384]{2,1,0:T(8,128)(2,1)S(1)} %copy-done.3), kind=kOutput, calls=%fused_computation.8 | convolution fusion | flops 805306368 | bytes 5636096 | tf_op jit(solution)/shard_map/dot_general | solution.py:11
  65.4 0.0 copy-done
  65.4 6.4 %convolution_convert_fusion = bf16[256,4096]{1,0:T(8,128)(2,1)} fusion(bf16[1,384,4096]{2,1,0:T(8,128)(2,1)S(1)} %copy-done, bf16[256,4096]{1,0:T(8,128)(2,1)} %bitcast.104, bf16[1,4096,384]{2,1,0:T(8,128)(2,1)} %param.12, f32[256,384]{1,0:T(8,128)} %fusion.3), kind=kOutput, calls=%fused_computation.3 | convolution fusion | flops 1612251136 | bytes 10878976 | tf_op jit(solution)/shard_map/dot_general | solution.py:14
  71.8 0.0 copy-start.2
  71.8 5.3 %all-to-all-start.1 = ((bf16[16,16,4096]{2,1,0:T(8,128)(2,1)}), bf16[16,16,4096]{2,1,0:T(8,128)(2,1)}, u32[]{:S(2)}, u32[]{:S(2)}) async-start(bf16[16,16,4096]{2,1,0:T(8,128)(2,1)} %bitcast.102), calls=%async_computation.1 | async-start | bytes 4194304 | tf_op jit(solution)/shard_map/all_to_all | solution.py:54
  77.0 0.1 reshape.168
  77.1 0.0 copy-done.2
  77.2 0.1 copy.47
  77.3 0.1 reshape.185
  77.4 2.2 %fusion.44 = (f32[128]{0:T(128)S(1)}, f32[128,128]{0,1:T(8,128)S(1)}) fusion(bf16[4096,128]{1,0:T(8,128)(2,1)} %param.9, bf16[128,4096]{1,0:T(8,128)(2,1)} %param.7, f32[4096]{0:T(1024)S(1)} %convert_element_type.81, f32[128]{0:T(128)S(1)} %add_rsqrt_fusion), kind=kOutput, calls=%fused_computation.88 | convolution fusion | flops 136331136 | bytes 2180096 | tf_op jit(solution)/shard_map/dot_general | solution.py:28
  79.6 7.0 %gather_fusion.1 = f32[1024]{0:T(1024)S(1)} fusion(f32[128,128]{0,1:T(8,128)S(1)} %fusion.35, s32[1024]{0:T(1024)S(1)} %reshape.185), kind=kCustom, calls=%fused_computation.1 | custom fusion | bytes 16384 | tf_op jit(solution)/shard_map/jit(take_along_axis)/gather | solution.py:30
  86.6 0.1 reshape.188
  86.9 37.7 %all-to-all-done.1 = bf16[16,16,4096]{2,1,0:T(8,128)(2,1)} async-done(((bf16[16,16,4096]{2,1,0:T(8,128)(2,1)}), bf16[16,16,4096]{2,1,0:T(8,128)(2,1)}, u32[]{:S(2)}, u32[]{:S(2)}) %all-to-all-start.1) | async-done | bytes 2097184 | tf_op jit(solution)/shard_map/all_to_all | solution.py:54
  124.6 2.9 %reduce_sum.67 = bf16[4,16,4096]{2,1,0:T(8,128)(2,1)} reduce(bf16[4,4,16,4096]{3,2,1,0:T(8,128)(2,1)} %bitcast.10, bf16[]{:T(256)} %constant.54.clone.1), dimensions={0}, to_apply=%region_9.10 | reduce | flops 786432 | bytes 2621442 | tf_op jit(solution)/shard_map/reduce_sum | solution.py:55
  127.4 16.2 %gather_fusion = bf16[1024,4096]{1,0:T(8,128)(2,1)} fusion(bf16[64,4096]{1,0:T(8,128)(2,1)} %bitcast.99, s32[1024]{0:T(1024)S(1)} %broadcast_clamp_fusion), kind=kCustom, calls=%fused_computation | custom fusion | bytes 16781312 | tf_op jit(solution)/shard_map/jit(_take)/gather | solution.py:60
  143.6 16.3 %copy_select_fusion = bf16[128,8,4096]{2,0,1:T(8,128)(2,1)} fusion(bf16[128,8,4096]{2,1,0:T(8,128)(2,1)} %bitcast.100, pred[128,8]{0,1:T(8,128)(4,1)S(1)} %get-tuple-element.7), kind=kLoop, calls=%fused_computation.2 | loop fusion | flops 4194304 | bytes 16778240 | tf_op jit(solution)/shard_map/jit(_take)/select_n | solution.py:60
  159.9 5.3 %fusion.9 = bf16[128,4096]{1,0:T(8,128)(2,1)} fusion(bf16[128,8,4096]{2,0,1:T(8,128)(2,1)} %copy_select_fusion, f32[128]{0:T(128)S(1)} %get-tuple-element.10, f32[128]{0:T(128)S(1)} %get-tuple-element.11, f32[128]{0:T(128)S(1)} %get-tuple-element.12, f32[128]{0:T(128)S(1)} %get-tuple-element.13, f32[128]{0:T(128)S(1)} %get-tuple-element.14, ...), kind=kLoop, calls=%fused_computation.17 | loop fusion | flops 12582912 | bytes 9441280 | tf_op jit(solution)/shard_map/convert_element_type | solution.py:65
  (15 shorter events, 0.3 us)
Async XLA Ops:
  0.0 65.4 %copy-start = (bf16[1,384,4096]{2,1,0:T(8,128)(2,1)S(1)}, bf16[1,384,4096]{2,1,0:T(8,128)(2,1)}, u32[]{:S(2)}) copy-start(bf16[1,384,4096]{2,1,0:T(8,128)(2,1)} %param.13) | copy-start | bytes 9437188
  8.1 55.2 %copy-start.3 = (bf16[1,4096,384]{2,1,0:T(8,128)(2,1)S(1)}, bf16[1,4096,384]{2,1,0:T(8,128)(2,1)}, u32[]{:S(2)}) copy-start(bf16[1,4096,384]{2,1,0:T(8,128)(2,1)} %param.11) | copy-start | bytes 9437188
  62.0 1.3 copy-start.1
  71.8 5.4 %copy-start.2 = (s32[128,8]{0,1:T(8,128)S(1)}, s32[128,8]{0,1:T(8,128)}, u32[]{:S(2)}) copy-start(s32[128,8]{0,1:T(8,128)} %param.10) | copy-start | bytes 12292
  71.8 52.8 %all-to-all-start.1 = ((bf16[16,16,4096]{2,1,0:T(8,128)(2,1)}), bf16[16,16,4096]{2,1,0:T(8,128)(2,1)}, u32[]{:S(2)}, u32[]{:S(2)}) async-start(bf16[16,16,4096]{2,1,0:T(8,128)(2,1)} %bitcast.102), calls=%async_computation.1 | async-start | bytes 4194304 | tf_op jit(solution)/shard_map/all_to_all | solution.py:54
where the time goes:
time: 166 us; the launch traced here: 165 us
  blocking collectives  53.9 us (32%)
  waiting for transfers between devices  37.7 us (23%)
  other arithmetic  29 us (17%)
  local copies, waits for them, and re-layouts  26.8 us (16%)
  matrix products  12.3 us (7%)
  starting transfers between devices  5.27 us (3%)
    all_to_all x1, blocking collectives, shards(): lax.all_to_all(sending, 'expert', split_axis=0, concat_axis=0, tiled=True)  53.9 us
    all_to_all x1, waiting for transfers between devices, shards(): lax.all_to_all(partial_value, 'expert', split_axis=0, concat_axis=0, tile...  37.7 us
    select_n x2, other arithmetic, shards(): jnp.take(results, column, axis=0).reshape(tok_rows, pick_count, model_width)  16.4 us
    gather x1, local copies, waits for them, and re-layouts, shards(): jnp.take(results, column, axis=0).reshape(tok_rows, pick_count, model_width)  16.2 us
    gather x5, local copies, waits for them, and re-layouts, shards(): picked = jnp.take_along_axis(router_probs, expert_ids, axis=1)  7.34 us
    dot_general x1, matrix products, expert_rows(): jnp.dot(hidden_act, down_weight[0], preferred_element_type=jnp.float32)  6.35 us
    all_to_all x1, starting transfers between devices, shards(): lax.all_to_all(partial_value, 'expert', split_axis=0, concat_axis=0, tile...  5.27 us
    convert_element_type x1, other arithmetic, shards(): return moe_out.astype(jnp.bfloat16)  5.26 us
  transfers between devices with their start and end apart: 1, of which 1 were waited for; matrix products, arithmetic and copies ran while one was open for 6% of the time, Pallas kernels for 0%

commit v1 on v0

v1 whole, which is shorter than its diff:
```python
import functools

import jax
import jax.numpy as jnp
from jax import lax
from jax.experimental import pallas as pl
from jax.experimental.pallas import tpu as pltpu
from jax.sharding import PartitionSpec as P

SPLIT = 4
CAP = 16
EPS = 1e-06


def slots_of(ids, flight):
    tokens = ids.shape[1]
    named = jnp.concatenate(
        [
            jnp.max((ids == e).astype(jnp.float32), axis=0, keepdims=True)
            for e in range(flight)
        ],
        axis=0,
    )
    earlier = lax.broadcasted_iota(jnp.int32, (tokens, tokens), 0) < lax.broadcasted_iota(
        jnp.int32, (tokens, tokens), 1
    )
    place = jnp.dot(
        named.astype(jnp.bfloat16),
        earlier.astype(jnp.float32).astype(jnp.bfloat16),
        preferred_element_type=jnp.float32,
    )
    return named, place


def spread(named, place, value, flight):
    slot = lax.broadcasted_iota(jnp.int32, (CAP, named.shape[1]), 0).astype(jnp.float32)
    return jnp.concatenate(
        [
            jnp.where(
                (place[e : e + 1] == slot) & (named[e : e + 1] > 0.0), value[e : e + 1], 0.0
            )
            for e in range(flight)
        ],
        axis=0,
    )


def inv_rms_of(hidden_ref):
    rows, width = hidden_ref.shape
    piece = min(width, 512)

    def add(i, total):
        x = hidden_ref[:, pl.ds(pl.multiple_of(i * piece, piece), piece)].astype(jnp.float32)
        return total + jnp.sum(x * x, axis=1, keepdims=True)

    total = lax.fori_loop(0, width // piece, add, jnp.zeros((rows, 1), jnp.float32), unroll=True)
    return lax.rsqrt(total / width + EPS)


def dispatch_kernel(flight, hidden_ref, gain_ref, ids_ref, out_ref):
    width = hidden_ref.shape[1]
    piece = min(width, 512)
    inv_rms = inv_rms_of(hidden_ref)
    named, place = slots_of(ids_ref[...], flight)
    select = spread(named, place, named, flight).astype(jnp.bfloat16)
    for i in range(width // piece):
        cols = pl.ds(i * piece, piece)
        x = hidden_ref[:, cols].astype(jnp.float32)
        normed = (x * inv_rms * gain_ref[:, cols].astype(jnp.float32)).astype(jnp.bfloat16)
        out_ref[:, cols] = jnp.dot(select, normed, preferred_element_type=jnp.float32).astype(
            jnp.bfloat16
        )


def shares_kernel(flight, hidden_ref, gain_ref, ids_ref, router_ref, out_ref):
    width = hidden_ref.shape[1]
    experts = router_ref.shape[1]
    piece = min(width, 512)
    inv_rms = inv_rms_of(hidden_ref)
    logits = jnp.zeros((hidden_ref.shape[0], experts), jnp.float32)
    for i in range(width // piece):
        cols = pl.ds(i * piece, piece)
        x = hidden_ref[:, cols].astype(jnp.float32)
        normed = (x * inv_rms * gain_ref[:, cols].astype(jnp.float32)).astype(jnp.bfloat16)
        logits += jnp.dot(normed, router_ref[cols, :], preferred_element_type=jnp.float32)
    logits = logits.T
    raised = jnp.exp(logits - jnp.max(logits, axis=0, keepdims=True))
    probs = raised / jnp.sum(raised, axis=0, keepdims=True)
    ids = ids_ref[...]
    expert = lax.broadcasted_iota(jnp.int32, probs.shape, 0)
    picked = jnp.zeros(probs.shape, jnp.float32)
    for k in range(ids.shape[0]):
        picked = jnp.where(ids[k : k + 1] == expert, probs, picked)
    share = probs[:flight] / jnp.sum(picked, axis=0, keepdims=True)
    named, place = slots_of(ids, flight)
    weight = spread(named, place, share, flight).T
    high = weight.astype(jnp.bfloat16)
    low = (weight - high.astype(jnp.float32)).astype(jnp.bfloat16)
    out_ref[...] = jnp.concatenate([high, low], axis=1)


def combine_kernel(weight_ref, *refs):
    *parts, out_ref = refs
    total = parts[0][...].astype(jnp.float32)
    for part in parts[1:]:
        total = total + part[...].astype(jnp.float32)
    rows = total.astype(jnp.bfloat16)
    out_ref[...] = jnp.dot(
        weight_ref[...], jnp.concatenate([rows, rows], axis=0), preferred_element_type=jnp.float32
    ).astype(jnp.bfloat16)


def vmem(count):
    return [pl.BlockSpec(memory_space=pltpu.VMEM)] * count


def dispatch(hidden, gain, ids, flight):
    return pl.pallas_call(
        functools.partial(dispatch_kernel, flight),
        out_shape=jax.ShapeDtypeStruct((flight * CAP, hidden.shape[1]), jnp.bfloat16),
        in_specs=vmem(3),
        out_specs=vmem(1)[0],
        name="dispatch",
    )(hidden, gain, ids)


def shares(hidden, gain, ids, router, flight):
    rows, width = hidden.shape
    return pl.pallas_call(
        functools.partial(shares_kernel, flight),
        out_shape=jax.ShapeDtypeStruct((rows, 2 * flight * CAP), jnp.bfloat16),
        in_specs=vmem(4),
        out_specs=vmem(1)[0],
        cost_estimate=pl.CostEstimate(
            flops=2 * rows * width * router.shape[1],
            bytes_accessed=2 * (hidden.size + router.size),
            transcendentals=rows * router.shape[1],
        ),
        name="shares",
    )(hidden, gain, ids, router)


def combine(weight, parts):
    rows = weight.shape[0]
    depth, width = parts[0].shape
    piece = min(width, 1024)
    block = pl.BlockSpec((depth, piece), lambda i: (0, i))
    return pl.pallas_call(
        combine_kernel,
        out_shape=jax.ShapeDtypeStruct((rows, width), jnp.bfloat16),
        grid=(width // piece,),
        in_specs=[pl.BlockSpec(weight.shape, lambda i: (0, 0))] + [block] * len(parts),
        out_specs=pl.BlockSpec((rows, piece), lambda i: (0, i)),
        name="combine",
    )(weight, *parts)


def expert_rows(rows, gate_weight, up_weight, down_weight):
    gate_act = jnp.dot(rows, gate_weight, preferred_element_type=jnp.float32)
    up_act = jnp.dot(rows, up_weight, preferred_element_type=jnp.float32)
    hidden_act = (jax.nn.silu(gate_act) * up_act).astype(jnp.bfloat16)
    return jnp.dot(hidden_act, down_weight, preferred_element_type=jnp.float32).astype(
        jnp.bfloat16
    )


def shards(hidden, norm_gain, router_weight, expert_ids, gate_weight, up_weight, down_weight):
    devices = lax.axis_size("expert")
    flight = devices // SPLIT
    width = hidden.shape[1]
    gain = norm_gain[None, :]
    ids = expert_ids.T
    outgoing = dispatch(hidden, gain, ids, flight)
    sending = jnp.tile(outgoing.reshape(flight, CAP, width), (SPLIT, 1, 1))
    arrived = lax.all_to_all(sending, "expert", split_axis=0, concat_axis=0, tiled=True)
    weight = shares(hidden, gain, ids, router_weight, flight)
    partial = expert_rows(
        arrived.reshape(-1, width), gate_weight[0], up_weight[0], down_weight[0]
    )
    returned = lax.all_to_all(
        partial.reshape(devices, CAP, width), "expert", split_axis=0, concat_axis=0, tiled=True
    )
    returned = returned.reshape(SPLIT, flight * CAP, width)
    return combine(weight, [returned[m] for m in range(SPLIT)])


def solution(mesh):
    tokens = P(("group", "expert"), None)
    sliced = P("expert", None, None)
    return jax.shard_map(
        shards,
        mesh=mesh,
        in_specs=(tokens, P(), P(), tokens, sliced, sliced, sliced),
        out_specs=tokens,
        check_vma=False,
    )
```

time: 166 us -> 128 us (0.77)
  the two profiles are of different devices: /device:TPU:15 before, /device:TPU:13 now
where the time goes in v1:
time: 128 us
  blocking collectives  53.7 us (42%)
  waiting for transfers between devices  44.3 us (35%)
  Pallas kernels  10 us (8%)
  matrix products  7.58 us (6%)
  local copies, waits for them, and re-layouts  7.1 us (6%)
  starting transfers between devices  5.12 us (4%)
    all_to_all x1, blocking collectives, shards(): lax.all_to_all(sending, 'expert', split_axis=0, concat_axis=0, tiled=True)  53.7 us
    all_to_all x1, waiting for transfers between devices, shards(): lax.all_to_all(partial.reshape(devices, CAP, width), 'expert', split_axis...  44.3 us
    dot_general x1, matrix products, expert_rows(): jnp.dot(hidden_act, down_weight, preferred_element_type=jnp.float32)  6.26 us
    all_to_all x1, starting transfers between devices, shards(): lax.all_to_all(partial.reshape(devices, CAP, width), 'expert', split_axis...  5.12 us
    pallas_call x1, Pallas kernels, combine(): pl.pallas_call(combine_kernel, out_shape=jax.ShapeDtypeStruct((rows, widt...  4.07 us
    pallas_call x1, Pallas kernels, shares(): pl.pallas_call(functools.partial(shares_kernel, flight), out_shape=jax.Sh...  3.23 us
    slice x1, local copies, waits for them, and re-layouts, shards(): return combine(weight, [returned[m] for m in range(SPLIT)])  2.88 us
    pallas_call x1, Pallas kernels, dispatch(): pl.pallas_call(functools.partial(dispatch_kernel, flight), out_shape=jax....  2.72 us
  transfers between devices with their start and end apart: 1, of which 1 were waited for; matrix products, arithmetic and copies ran while one was open for 0% of the time, Pallas kernels for 3%

profile of v1, /device:TPU:13, one launch (start us, length us, event | category | flops | bytes accessed | tf_op | source)
XLA Modules:
  0.0 127.8 jit_solution(15222555897297220664)
XLA Ops:
  0.0 0.0 copy-start
  0.0 1.5 %broadcast_in_dim.3.gain_ref = bf16[1,4096]{1,0:T(2,128)(2,1)} reshape(bf16[4096]{0:T(1024)(128)(2,1)} %param.8) | data formatting | bytes 16384 | tf_op jit(solution)/shard_map/broadcast_in_dim | solution.py:171
  1.5 2.7 %dispatch.1 = bf16[64,4096]{1,0:T(8,128)(2,1)} custom-call(bf16[128,4096]{1,0:T(8,128)(2,1)} %hidden_ref.3, bf16[1,4096]{1,0:T(2,128)(2,1)} %broadcast_in_dim.3.gain_ref, s32[8,128]{1,0:T(8,128)} %bitcast.35), custom_call_target="tpu_custom_call" | custom-call | tf_op jit(solution)/shard_map/dispatch/pallas_call | solution.py:118
  4.2 0.0 copy-start.2
  4.2 1.4 %tile.11 = bf16[4,4,16,4096]{3,2,1,0:T(8,128)(2,1)S(1)} broadcast(bf16[4,16,4096]{2,1,0:T(8,128)(2,1)} %bitcast.27), dimensions={1,2,3} | broadcast | bytes 2621440 | tf_op jit(solution)/shard_map/tile | solution.py:174
  5.6 53.7 %all_to_all.10 = bf16[16,16,4096]{2,1,0:T(8,128)(2,1)S(1)} all-to-all(bf16[16,16,4096]{2,1,0:T(8,128)(2,1)S(1)} %bitcast.26), channel_id=1, replica_groups=mesh['group'=2,'expert'=16] {'expert'}, dimensions={0} | all-to-all | bytes 4194304 | tf_op jit(solution)/shard_map/all_to_all | solution.py:175
  59.3 0.0 copy-start.1
  59.3 1.3 %copy-done.1 = bf16[16,16,4096]{2,1,0:T(8,128)(2,1)} copy-done((bf16[16,16,4096]{2,1,0:T(8,128)(2,1)}, bf16[16,16,4096]{2,1,0:T(8,128)(2,1)S(1)}, u32[]{:S(2)}) %copy-start.1) | copy-done | bytes 2097176
  60.6 0.0 copy-done.2
  60.6 1.3 %fusion.3 = f32[256,384]{1,0:T(8,128)S(1)} fusion(bf16[256,4096]{1,0:T(8,128)(2,1)S(1)} %bitcast.29, bf16[1,4096,384]{2,1,0:T(8,128)(2,1)S(1)} %copy-done.2), kind=kOutput, calls=%fused_computation.4 | convolution fusion | flops 805306368 | bytes 5636096 | tf_op jit(solution)/shard_map/dot_general | solution.py:159
  61.9 0.0 copy-done
  61.9 6.3 %convolution_convert_fusion = bf16[256,4096]{1,0:T(8,128)(2,1)} fusion(bf16[1,384,4096]{2,1,0:T(8,128)(2,1)S(1)} %copy-done, bf16[256,4096]{1,0:T(8,128)(2,1)} %bitcast.30, bf16[1,4096,384]{2,1,0:T(8,128)(2,1)} %param.12, f32[256,384]{1,0:T(8,128)S(1)} %fusion.3), kind=kOutput, calls=%fused_computation | convolution fusion | flops 1612251136 | bytes 10878976 | tf_op jit(solution)/shard_map/dot_general | solution.py:162
  68.2 5.1 %all-to-all-start.1 = ((bf16[16,16,4096]{2,1,0:T(8,128)(2,1)}), bf16[16,16,4096]{2,1,0:T(8,128)(2,1)}, u32[]{:S(2)}, u32[]{:S(2)}) async-start(bf16[16,16,4096]{2,1,0:T(8,128)(2,1)} %bitcast.28), calls=%async_computation.1 | async-start | bytes 4194304 | tf_op jit(solution)/shard_map/all_to_all | solution.py:180
  73.3 3.2 %shares.1.weight_ref = bf16[128,128]{1,0:T(8,128)(2,1)} custom-call(bf16[128,4096]{1,0:T(8,128)(2,1)} %hidden_ref.3, bf16[1,4096]{1,0:T(2,128)(2,1)} %broadcast_in_dim.3.gain_ref, s32[8,128]{1,0:T(8,128)} %bitcast.36, bf16[4096,128]{1,0:T(8,128)(2,1)} %router_ref.1), custom_call_target="tpu_custom_call" | custom-call | flops 134217728 | bytes 2097152 | tf_op jit(solution)/shard_map/shares/pallas_call | solution.py:129
  76.6 44.3 %all-to-all-done.1 = bf16[16,16,4096]{2,1,0:T(8,128)(2,1)} async-done(((bf16[16,16,4096]{2,1,0:T(8,128)(2,1)}), bf16[16,16,4096]{2,1,0:T(8,128)(2,1)}, u32[]{:S(2)}, u32[]{:S(2)}) %all-to-all-start.1) | async-done | bytes 2097184 | tf_op jit(solution)/shard_map/all_to_all | solution.py:180
  120.9 2.9 %fusion.20 = (bf16[4,16,4096]{2,1,0:T(8,128)(2,1)}, bf16[4,16,4096]{2,1,0:T(8,128)(2,1)}, bf16[4,16,4096]{2,1,0:T(8,128)(2,1)}, bf16[4,16,4096]{2,1,0:T(8,128)(2,1)}) fusion(bf16[16,16,4096]{2,1,0:T(8,128)(2,1)} %all-to-all-done.1), kind=kLoop, calls=%fused_computation.15 | loop fusion | bytes 4194304 | tf_op jit(solution)/shard_map/slice | solution.py:184
  123.7 4.1 %combine.1 = bf16[128,4096]{1,0:T(8,128)(2,1)} custom-call(bf16[128,128]{1,0:T(8,128)(2,1)} %shares.1.weight_ref, bf16[64,4096]{1,0:T(8,128)(2,1)} %bitcast.34, bf16[64,4096]{1,0:T(8,128)(2,1)} %bitcast.33, bf16[64,4096]{1,0:T(8,128)(2,1)} %bitcast.32, bf16[64,4096]{1,0:T(8,128)(2,1)} %bitcast.31), custom_call_target="tpu_custom_call" | custom-call | tf_op jit(solution)/shard_map/combine/pallas_call | solution.py:148
Async XLA Ops:
  0.0 61.9 %copy-start = (bf16[1,384,4096]{2,1,0:T(8,128)(2,1)S(1)}, bf16[1,384,4096]{2,1,0:T(8,128)(2,1)}, u32[]{:S(2)}) copy-start(bf16[1,384,4096]{2,1,0:T(8,128)(2,1)} %param.13) | copy-start | bytes 9437188
  4.2 56.4 %copy-start.2 = (bf16[1,4096,384]{2,1,0:T(8,128)(2,1)S(1)}, bf16[1,4096,384]{2,1,0:T(8,128)(2,1)}, u32[]{:S(2)}) copy-start(bf16[1,4096,384]{2,1,0:T(8,128)(2,1)} %param.11) | copy-start | bytes 9437188
  59.3 1.3 %copy-start.1 = (bf16[16,16,4096]{2,1,0:T(8,128)(2,1)}, bf16[16,16,4096]{2,1,0:T(8,128)(2,1)S(1)}, u32[]{:S(2)}) copy-start(bf16[16,16,4096]{2,1,0:T(8,128)(2,1)S(1)} %all_to_all.10) | copy-start | bytes 6291460
  68.2 52.6 %all-to-all-start.1 = ((bf16[16,16,4096]{2,1,0:T(8,128)(2,1)}), bf16[16,16,4096]{2,1,0:T(8,128)(2,1)}, u32[]{:S(2)}, u32[]{:S(2)}) async-start(bf16[16,16,4096]{2,1,0:T(8,128)(2,1)} %bitcast.28), calls=%async_computation.1 | async-start | bytes 4194304 | tf_op jit(solution)/shard_map/all_to_all | solution.py:180

commit v2 on v1

v2 whole, which is shorter than its diff:
```python
import functools

import jax
import jax.numpy as jnp
from jax import lax
from jax.experimental import pallas as pl
from jax.experimental.pallas import tpu as pltpu
from jax.sharding import PartitionSpec as P

SPLIT = 4
CAP = 16
CHUNKS = 2
EPS = 1e-06
VMEM_LIMIT = 16 * 1024 * 1024
PIECE = 512


def slots_of(ids, me, flight):
    tokens = ids.shape[1]
    named = jnp.concatenate(
        [
            jnp.max((ids == (me ^ k)).astype(jnp.float32), axis=0, keepdims=True)
            for k in range(flight)
        ],
        axis=0,
    )
    earlier = lax.broadcasted_iota(jnp.int32, (tokens, tokens), 0) < lax.broadcasted_iota(
        jnp.int32, (tokens, tokens), 1
    )
    place = jnp.dot(
        named.astype(jnp.bfloat16),
        earlier.astype(jnp.float32).astype(jnp.bfloat16),
        preferred_element_type=jnp.float32,
    )
    return named, place


def spread(named, place, value, flight):
    size = CAP // CHUNKS
    slot = lax.broadcasted_iota(jnp.int32, (size, named.shape[1]), 0)
    return jnp.concatenate(
        [
            jnp.where(
                (place[k : k + 1] == (slot + c * size).astype(jnp.float32))
                & (named[k : k + 1] > 0.0),
                value[k : k + 1],
                0.0,
            )
            for c in range(CHUNKS)
            for k in range(flight)
        ],
        axis=0,
    )


def inv_rms_of(hidden_ref):
    rows, width = hidden_ref.shape
    piece = min(width, PIECE)
    total = jnp.zeros((rows, 1), jnp.float32)
    for i in range(width // piece):
        x = hidden_ref[:, i * piece : (i + 1) * piece].astype(jnp.float32)
        total = total + jnp.sum(x * x, axis=1, keepdims=True)
    return lax.rsqrt(total / width + EPS)


def normed_piece(hidden_ref, gain_ref, inv_rms, cols):
    x = hidden_ref[:, cols].astype(jnp.float32)
    return (x * inv_rms * gain_ref[:, cols].astype(jnp.float32)).astype(jnp.bfloat16)


def dispatch_kernel(flight, me_ref, hidden_ref, gain_ref, ids_ref, *out_refs):
    width = hidden_ref.shape[1]
    piece = min(width, PIECE)
    inv_rms = inv_rms_of(hidden_ref)
    named, place = slots_of(ids_ref[...], me_ref[0], flight)
    select = spread(named, place, named, flight).astype(jnp.bfloat16)
    size = CAP // CHUNKS
    for i in range(width // piece):
        cols = pl.ds(i * piece, piece)
        normed = normed_piece(hidden_ref, gain_ref, inv_rms, cols)
        rows = jnp.dot(select, normed, preferred_element_type=jnp.float32)
        for at, out_ref in enumerate(out_refs):
            out_ref[:, cols] = rows[at * size : (at + 1) * size].astype(jnp.bfloat16)


def shares_kernel(flight, me_ref, hidden_ref, gain_ref, ids_ref, router_ref, out_ref):
    width = hidden_ref.shape[1]
    experts = router_ref.shape[1]
    piece = min(width, PIECE)
    inv_rms = inv_rms_of(hidden_ref)
    logits = jnp.zeros((hidden_ref.shape[0], experts), jnp.float32)
    for i in range(width // piece):
        cols = pl.ds(i * piece, piece)
        normed = normed_piece(hidden_ref, gain_ref, inv_rms, cols)
        logits += jnp.dot(normed, router_ref[cols, :], preferred_element_type=jnp.float32)
    logits = logits.T
    raised = jnp.exp(logits - jnp.max(logits, axis=0, keepdims=True))
    probs = raised / jnp.sum(raised, axis=0, keepdims=True)
    ids = ids_ref[...]
    expert = lax.broadcasted_iota(jnp.int32, probs.shape, 0)
    picked = jnp.zeros(probs.shape, jnp.float32)
    for k in range(ids.shape[0]):
        picked = jnp.where(ids[k : k + 1] == expert, probs, picked)
    me = me_ref[0]
    named, place = slots_of(ids, me, flight)
    flying = jnp.concatenate(
        [
            jnp.sum(jnp.where(expert == (me ^ k), probs, 0.0), axis=0, keepdims=True)
            for k in range(flight)
        ],
        axis=0,
    )
    share = flying / jnp.sum(picked, axis=0, keepdims=True)
    weight = spread(named, place, share, flight).T
    high = weight.astype(jnp.bfloat16)
    low = (weight - high.astype(jnp.float32)).astype(jnp.bfloat16)
    out_ref[...] = jnp.concatenate([high, low], axis=1)


def expert_kernel(rows_ref, gate_ref, up_ref, down_ref, out_ref):
    rows = rows_ref[...]
    gate_act = jnp.dot(rows, gate_ref[0], preferred_element_type=jnp.float32)
    up_act = jnp.dot(rows, up_ref[0], preferred_element_type=jnp.float32)
    hidden_act = (jax.nn.silu(gate_act) * up_act).astype(jnp.bfloat16)
    width = out_ref.shape[1]
    piece = min(width, PIECE)
    for i in range(width // piece):
        cols = pl.ds(i * piece, piece)
        out_ref[:, cols] = jnp.dot(
            hidden_act, down_ref[0, :, cols], preferred_element_type=jnp.float32
        ).astype(jnp.bfloat16)


def combine_kernel(weight_ref, *refs):
    *parts, out_ref = refs
    rows = jnp.concatenate([part[...].astype(jnp.float32) for part in parts], axis=0)
    rows = rows.astype(jnp.bfloat16)
    out_ref[...] = jnp.dot(
        weight_ref[...], jnp.concatenate([rows, rows], axis=0), preferred_element_type=jnp.float32
    ).astype(jnp.bfloat16)


def vmem(count):
    return [pl.BlockSpec(memory_space=pltpu.VMEM)] * count


def params():
    return pltpu.CompilerParams(vmem_limit_bytes=VMEM_LIMIT)


def dispatch(me, hidden, gain, ids, flight):
    shape = jax.ShapeDtypeStruct((CAP // CHUNKS, hidden.shape[1]), jnp.bfloat16)
    count = CHUNKS * flight
    out = pl.pallas_call(
        functools.partial(dispatch_kernel, flight),
        out_shape=[shape] * count,
        in_specs=[pl.BlockSpec(memory_space=pltpu.SMEM)] + vmem(3),
        out_specs=vmem(count),
        compiler_params=params(),
        name="dispatch",
    )(me, hidden, gain, ids)
    return [out[c * flight : (c + 1) * flight] for c in range(CHUNKS)]


def shares(me, hidden, gain, ids, router, flight):
    rows, width = hidden.shape
    return pl.pallas_call(
        functools.partial(shares_kernel, flight),
        out_shape=jax.ShapeDtypeStruct((rows, 2 * flight * CAP), jnp.bfloat16),
        in_specs=[pl.BlockSpec(memory_space=pltpu.SMEM)] + vmem(4),
        out_specs=vmem(1)[0],
        compiler_params=params(),
        cost_estimate=pl.CostEstimate(
            flops=2 * rows * width * router.shape[1],
            bytes_accessed=2 * (hidden.size + router.size),
            transcendentals=rows * router.shape[1],
        ),
        name="shares",
    )(me, hidden, gain, ids, router)


def expert(rows, gate_weight, up_weight, down_weight):
    count = gate_weight.size + up_weight.size + down_weight.size
    return pl.pallas_call(
        expert_kernel,
        out_shape=jax.ShapeDtypeStruct(rows.shape, jnp.bfloat16),
        in_specs=vmem(4),
        out_specs=vmem(1)[0],
        compiler_params=params(),
        cost_estimate=pl.CostEstimate(
            flops=2 * rows.shape[0] * count, bytes_accessed=2 * count, transcendentals=0
        ),
        name="expert",
    )(rows, gate_weight, up_weight, down_weight)


def combine(weight, parts):
    rows = weight.shape[0]
    width = parts[0].shape[1]
    piece = min(width, 1024)
    return pl.pallas_call(
        combine_kernel,
        out_shape=jax.ShapeDtypeStruct((rows, width), jnp.bfloat16),
        grid=(width // piece,),
        in_specs=[pl.BlockSpec(weight.shape, lambda i: (0, 0))]
        + [pl.BlockSpec((part.shape[0], piece), lambda i: (0, i)) for part in parts],
        out_specs=pl.BlockSpec((rows, piece), lambda i: (0, i)),
        compiler_params=params(),
        name="combine",
    )(weight, *parts)


def in_plane(blocks, flight):
    got = list(blocks)
    for k in reversed(range(1, flight)):
        pairs = [
            (m * flight + e, m * flight + (e ^ k)) for m in range(SPLIT) for e in range(flight)
        ]
        got[k] = lax.ppermute(blocks[k], "expert", pairs)
    return got


def end_pair(rows, flight, sides=(0, 1, 2, 3)):
    pairs = [(m * flight + e, (m ^ 1) * flight + e) for m in sides for e in range(flight)]
    return lax.ppermute(rows, "expert", pairs)


def middle_pair(rows, flight):
    pairs = [(m * flight + e, (3 - m) * flight + e) for m in (1, 2) for e in range(flight)]
    return lax.ppermute(rows, "expert", pairs)


def plus(*terms):
    total = terms[0].astype(jnp.float32)
    for term in terms[1:]:
        total = total + term.astype(jnp.float32)
    return total.astype(jnp.bfloat16)


def shards(hidden, norm_gain, router_weight, expert_ids, gate_weight, up_weight, down_weight):
    devices = lax.axis_size("expert")
    flight = devices // SPLIT
    gain = norm_gain[None, :]
    ids = expert_ids.T
    index = lax.axis_index("expert")
    member = index // flight
    outer = (member == 0) | (member == SPLIT - 1)
    me = (index % flight).astype(jnp.int32)[None]

    def partial(rows):
        return expert(rows, gate_weight, up_weight, down_weight)

    sent = dispatch(me, hidden, gain, ids, flight)
    own = [jnp.concatenate(in_plane(blocks, flight), axis=0) for blocks in sent]
    near = [end_pair(x, flight) for x in own]
    far_in = [middle_pair(x, flight) for x in own]
    last_in = [middle_pair(x, flight) for x in near]
    near_part = [partial(x) for x in near]
    two = [
        end_pair(jnp.where(outer, n, f), flight) for n, f in zip(near_part, far_in)
    ]
    far_part = [partial(jnp.where(outer, t, f)) for t, f in zip(two, far_in)]
    three = [
        end_pair(jnp.where(outer, f, x), flight) for f, x in zip(far_part, last_in)
    ]
    last_part = [partial(jnp.where(outer, t, x)) for t, x in zip(three, last_in)]
    mid = [middle_pair(plus(f, t), flight) for f, t in zip(far_part, three)]
    four = [end_pair(x, flight, (0, 3)) for x in last_part]
    mid2 = [middle_pair(plus(x, f), flight) for x, f in zip(last_part, four)]
    five = [end_pair(plus(n, x), flight, (1, 2)) for n, x in zip(near_part, mid2)]
    own_part = partial(jnp.concatenate(own, axis=0))
    weight = shares(me, hidden, gain, ids, router_weight, flight)
    back = []
    depth = own[0].shape[0]
    size = depth // flight
    for c in range(CHUNKS):
        mine = own_part[c * depth : (c + 1) * depth]
        done = jnp.where(outer, plus(mine, five[c]), plus(mine, two[c], mid[c]))
        back += in_plane([done[k * size : (k + 1) * size] for k in range(flight)], flight)
    return combine(weight, back)


def solution(mesh):
    tokens = P(("group", "expert"), None)
    sliced = P("expert", None, None)
    return jax.shard_map(
        shards,
        mesh=mesh,
        in_specs=(tokens, P(), P(), tokens, sliced, sliced, sliced),
        out_specs=tokens,
        check_vma=False,
    )
```

time: 128 us -> 98.6 us (0.77)
  the two profiles are of different devices: /device:TPU:13 before, /device:TPU:0 now
where the time goes in v2:
time: 98.6 us; the launch traced here: 98 us
  starting transfers between devices  40.7 us (41%)
  waiting for transfers between devices  31.9 us (32%)
  Pallas kernels  15.5 us (16%)
  local copies, waits for them, and re-layouts  8.42 us (9%)
    ppermute x10, waiting for transfers between devices, end_pair(): return lax.ppermute(rows, 'expert', pairs)  26.3 us
    ppermute x10, starting transfers between devices, end_pair(): return lax.ppermute(rows, 'expert', pairs)  26.1 us
    pallas_call x7, Pallas kernels, expert(): pl.pallas_call(expert_kernel, out_shape=jax.ShapeDtypeStruct(rows.shape,...  11.6 us
    ppermute x12, starting transfers between devices, in_plane(): got[k] = lax.ppermute(blocks[k], 'expert', pairs)  9.22 us
    unnamed x25, local copies, waits for them, and re-layouts  7.67 us
    ppermute x12, waiting for transfers between devices, in_plane(): got[k] = lax.ppermute(blocks[k], 'expert', pairs)  5.62 us
    ppermute x8, starting transfers between devices, middle_pair(): return lax.ppermute(rows, 'expert', pairs)  5.38 us
    pallas_call x1, Pallas kernels, combine(): pl.pallas_call(combine_kernel, out_shape=jax.ShapeDtypeStruct((rows, widt...  2.06 us
  transfers between devices with their start and end apart: 30, of which 12 were waited for; matrix products, arithmetic and copies ran while one was open for 1% of the time, Pallas kernels for 13%

profile of v2, /device:TPU:0, one launch (start us, length us, event | category | flops | bytes accessed | tf_op | source)
XLA Modules:
  0.0 98.0 jit_solution(9308251107776200740)
XLA Ops:
  0.0 0.7 broadcast_in_dim.7.gain_ref
  0.7 1.2 %copy-done.4 = bf16[128,4096]{1,0:T(8,128)(2,1)S(1)} copy-done((bf16[128,4096]{1,0:T(8,128)(2,1)S(1)}, bf16[128,4096]{1,0:T(8,128)(2,1)}, u32[]{:S(2)}) %copy-start.4) | copy-done | bytes 1048600
  2.0 0.7 copy-done.7
  2.6 0.7 dispatch.1
  3.3 0.5 collective-permute-start
  3.8 2.6 %collective-permute-start.1 = (bf16[8,4096]{1,0:T(8,128)(2,1)S(1)}, bf16[8,4096]{1,0:T(8,128)(2,1)S(1)}, u32[]{:S(2)}, u32[]{:S(2)}) collective-permute-start(bf16[8,4096]{1,0:T(8,128)(2,1)S(1)} %get-tuple-element.15), channel_id=1, source_target_pairs={{0,2},{1,3},{2,0},{3,1},{4,6},{5,7},{6,4},{7,5},{8,10},{9,11},{10,... | collective-permute-start | bytes 196616 | tf_op jit(solution)/shard_map/ppermute | solution.py:219
  6.4 0.1 collective-permute-start.2
  6.5 0.1 collective-permute-start.3
  6.6 1.9 %collective-permute-start.4 = (bf16[8,4096]{1,0:T(8,128)(2,1)S(1)}, bf16[8,4096]{1,0:T(8,128)(2,1)S(1)}, u32[]{:S(2)}, u32[]{:S(2)}) collective-permute-start(bf16[8,4096]{1,0:T(8,128)(2,1)S(1)} %get-tuple-element.19), channel_id=1, source_target_pairs={{0,2},{1,3},{2,0},{3,1},{4,6},{5,7},{6,4},{7,5},{8,10},{9,11},{10,... | collective-permute-start | bytes 196616 | tf_op jit(solution)/shard_map/ppermute | solution.py:219
  8.6 0.1 collective-permute-start.5
  8.7 0.4 collective-permute-done.1
  9.1 1.3 %collective-permute-done.2 = bf16[8,4096]{1,0:T(8,128)(2,1)S(1)} collective-permute-done((bf16[8,4096]{1,0:T(8,128)(2,1)S(1)}, bf16[8,4096]{1,0:T(8,128)(2,1)S(1)}, u32[]{:S(2)}, u32[]{:S(2)}) %collective-permute-start.2) | collective-permute-done | bytes 65568 | tf_op jit(solution)/shard_map/ppermute | solution.py:219
  10.5 1.6 %collective-permute-start.6 = (bf16[32,4096]{1,0:T(8,128)(2,1)S(1)}, bf16[32,4096]{1,0:T(8,128)(2,1)S(1)}, u32[]{:S(2)}, u32[]{:S(2)}) collective-permute-start(bf16[32,4096]{1,0:T(8,128)(2,1)S(1)} %get-tuple-element.40), channel_id=1, source_target_pairs={{0,4},{1,5},{2,6},{3,7},{4,0},{5,1},{6,2},{7,3},{8,12},{9,13},{10,... | collective-permute-start | bytes 786440 | tf_op jit(solution)/shard_map/ppermute | solution.py:225
  12.1 0.7 collective-permute-start.7
  12.9 0.4 collective-permute-done.5
  13.3 4.1 %collective-permute-start.18 = (bf16[32,4096]{1,0:T(8,128)(2,1)S(1)}, bf16[32,4096]{1,0:T(8,128)(2,1)S(1)}, u32[]{:S(2)}, u32[]{:S(2)}) collective-permute-start(bf16[32,4096]{1,0:T(8,128)(2,1)S(1)} %get-tuple-element.31), channel_id=1, source_target_pairs={{0,4},{1,5},{2,6},{3,7},{4,0},{5,1},{6,2},{7,3},{8,12},{9,13},{10,... | collective-permute-start | bytes 786440 | tf_op jit(solution)/shard_map/ppermute | solution.py:225
  17.4 0.7 collective-permute-start.19
  18.0 1.6 %collective-permute-done.6.rows_ref = bf16[32,4096]{1,0:T(8,128)(2,1)S(1)} collective-permute-done((bf16[32,4096]{1,0:T(8,128)(2,1)S(1)}, bf16[32,4096]{1,0:T(8,128)(2,1)S(1)}, u32[]{:S(2)}, u32[]{:S(2)}) %collective-permute-start.6) | collective-permute-done | bytes 262176 | tf_op jit(solution)/shard_map/ppermute | solution.py:225
  19.7 1.9 %copy-done = bf16[1,4096,384]{2,1,0:T(8,128)(2,1)S(1)} copy-done((bf16[1,4096,384]{2,1,0:T(8,128)(2,1)S(1)}, bf16[1,4096,384]{2,1,0:T(8,128)(2,1)}, u32[]{:S(2)}) %copy-start) | copy-done | bytes 3145752
  21.6 1.9 %copy-done.2 = bf16[1,4096,384]{2,1,0:T(8,128)(2,1)S(1)} copy-done((bf16[1,4096,384]{2,1,0:T(8,128)(2,1)S(1)}, bf16[1,4096,384]{2,1,0:T(8,128)(2,1)}, u32[]{:S(2)}) %copy-start.2) | copy-done | bytes 3145752
  23.4 1.9 %copy-done.3 = bf16[1,384,4096]{2,1,0:T(8,128)(2,1)S(1)} copy-done((bf16[1,384,4096]{2,1,0:T(8,128)(2,1)S(1)}, bf16[1,384,4096]{2,1,0:T(8,128)(2,1)}, u32[]{:S(2)}) %copy-start.3) | copy-done | bytes 3145752
  25.3 1.6 %expert.8 = bf16[32,4096]{1,0:T(8,128)(2,1)S(1)} custom-call(bf16[32,4096]{1,0:T(8,128)(2,1)S(1)} %collective-permute-done.6.rows_ref, bf16[1,4096,384]{2,1,0:T(8,128)(2,1)S(1)} %copy-done, bf16[1,4096,384]{2,1,0:T(8,128)(2,1)S(1)} %copy-done.2, bf16[1,384,4096]{2,1,0:T(8,128)(2,1)S(1)} %copy-done.3), custom_call_target="tpu_custom_call" | custom-call | flops 301989888 | bytes 9437184 | tf_op jit(solution)/shard_map/expert/pallas_call | solution.py:184
  27.0 1.6 %collective-permute-start.8 = (bf16[32,4096]{1,0:T(8,128)(2,1)S(1)}, bf16[32,4096]{1,0:T(8,128)(2,1)S(1)}, u32[]{:S(2)}, u32[]{:S(2)}) collective-permute-start(bf16[32,4096]{1,0:T(8,128)(2,1)S(1)} %broadcast_select_fusion.7), channel_id=1, source_target_pairs={{0,4},{1,5},{2,6},{3,7},{4,0},{5,1},{6,2},{7,3},{8,12},{9,13},{10,... | collective-permute-start | bytes 786440 | tf_op jit(solution)/shard_map/ppermute | solution.py:225
  28.7 1.6 %expert.11 = bf16[32,4096]{1,0:T(8,128)(2,1)S(1)} custom-call(bf16[32,4096]{1,0:T(8,128)(2,1)S(1)} %collective-permute-done.18.rows_ref, bf16[1,4096,384]{2,1,0:T(8,128)(2,1)S(1)} %copy-done.1, bf16[1,4096,384]{2,1,0:T(8,128)(2,1)S(1)} %copy-done.2, bf16[1,384,4096]{2,1,0:T(8,128)(2,1)S(1)} %copy-done.3), custom_call_target="tpu_custom_call" | custom-call | flops 301989888 | bytes 9437184 | tf_op jit(solution)/shard_map/expert/pallas_call | solution.py:184
  30.4 0.5 collective-permute-start.20
  30.9 0.7 collective-permute-start.9
  31.6 0.7 collective-permute-start.21
  32.3 4.1 %collective-permute-done.8 = bf16[32,4096]{1,0:T(8,128)(2,1)S(1)} collective-permute-done((bf16[32,4096]{1,0:T(8,128)(2,1)S(1)}, bf16[32,4096]{1,0:T(8,128)(2,1)S(1)}, u32[]{:S(2)}, u32[]{:S(2)}) %collective-permute-start.8) | collective-permute-done | bytes 262176 | tf_op jit(solution)/shard_map/ppermute | solution.py:225
  36.4 1.6 %expert.9 = bf16[32,4096]{1,0:T(8,128)(2,1)S(1)} custom-call(bf16[32,4096]{1,0:T(8,128)(2,1)S(1)} %broadcast_select_fusion.6.rows_ref, bf16[1,4096,384]{2,1,0:T(8,128)(2,1)S(1)} %copy-done.1, bf16[1,4096,384]{2,1,0:T(8,128)(2,1)S(1)} %copy-done.2, bf16[1,384,4096]{2,1,0:T(8,128)(2,1)S(1)} %copy-done.3), custom_call_target="tpu_custom_call" | custom-call | flops 301989888 | bytes 9437184 | tf_op jit(solution)/shard_map/expert/pallas_call | solution.py:184
  38.1 5.6 %collective-permute-start.10 = (bf16[32,4096]{1,0:T(8,128)(2,1)S(1)}, bf16[32,4096]{1,0:T(8,128)(2,1)S(1)}, u32[]{:S(2)}, u32[]{:S(2)}) collective-permute-start(bf16[32,4096]{1,0:T(8,128)(2,1)S(1)} %broadcast_select_fusion.5), channel_id=1, source_target_pairs={{0,4},{1,5},{2,6},{3,7},{4,0},{5,1},{6,2},{7,3},{8,12},{9,13},{10,... | collective-permute-start | bytes 786440 | tf_op jit(solution)/shard_map/ppermute | solution.py:225
  43.7 1.6 %expert.12 = bf16[32,4096]{1,0:T(8,128)(2,1)S(1)} custom-call(bf16[32,4096]{1,0:T(8,128)(2,1)S(1)} %broadcast_select_fusion.2.rows_ref, bf16[1,4096,384]{2,1,0:T(8,128)(2,1)S(1)} %copy-done.1, bf16[1,4096,384]{2,1,0:T(8,128)(2,1)S(1)} %copy-done.2, bf16[1,384,4096]{2,1,0:T(8,128)(2,1)S(1)} %copy-done.3), custom_call_target="tpu_custom_call" | custom-call | flops 301989888 | bytes 9437184 | tf_op jit(solution)/shard_map/expert/pallas_call | solution.py:184
  45.4 1.6 %collective-permute-start.22 = (bf16[32,4096]{1,0:T(8,128)(2,1)S(1)}, bf16[32,4096]{1,0:T(8,128)(2,1)S(1)}, u32[]{:S(2)}, u32[]{:S(2)}) collective-permute-start(bf16[32,4096]{1,0:T(8,128)(2,1)S(1)} %broadcast_select_fusion.1), channel_id=1, source_target_pairs={{0,4},{1,5},{2,6},{3,7},{4,0},{5,1},{6,2},{7,3},{8,12},{9,13},{10,... | collective-permute-start | bytes 786440 | tf_op jit(solution)/shard_map/ppermute | solution.py:225
  47.1 3.3 %collective-permute-done.10 = bf16[32,4096]{1,0:T(8,128)(2,1)S(1)} collective-permute-done((bf16[32,4096]{1,0:T(8,128)(2,1)S(1)}, bf16[32,4096]{1,0:T(8,128)(2,1)S(1)}, u32[]{:S(2)}, u32[]{:S(2)}) %collective-permute-start.10) | collective-permute-done | bytes 262176 | tf_op jit(solution)/shard_map/ppermute | solution.py:225
  50.4 1.6 %expert.10 = bf16[32,4096]{1,0:T(8,128)(2,1)S(1)} custom-call(bf16[32,4096]{1,0:T(8,128)(2,1)S(1)} %broadcast_select_fusion.4.rows_ref, bf16[1,4096,384]{2,1,0:T(8,128)(2,1)S(1)} %copy-done.1, bf16[1,4096,384]{2,1,0:T(8,128)(2,1)S(1)} %copy-done.2, bf16[1,384,4096]{2,1,0:T(8,128)(2,1)S(1)} %copy-done.3), custom_call_target="tpu_custom_call" | custom-call | flops 301989888 | bytes 9437184 | tf_op jit(solution)/shard_map/expert/pallas_call | solution.py:184
  52.1 4.2 %collective-permute-start.11 = (bf16[32,4096]{1,0:T(8,128)(2,1)S(1)}, bf16[32,4096]{1,0:T(8,128)(2,1)S(1)}, u32[]{:S(2)}, u32[]{:S(2)}) collective-permute-start(bf16[32,4096]{1,0:T(8,128)(2,1)S(1)} %expert.10), channel_id=1, source_target_pairs={{0,4},{1,5},{2,6},{3,7},{12,8},{13,9},{14,10},{15,11},{16,20},{17,... | collective-permute-start | bytes 786440 | tf_op jit(solution)/shard_map/ppermute | solution.py:225
  56.2 0.1 add_convert_fusion.3
  56.3 0.7 collective-permute-start.14
  57.0 1.7 %expert.13 = bf16[32,4096]{1,0:T(8,128)(2,1)S(1)} custom-call(bf16[32,4096]{1,0:T(8,128)(2,1)S(1)} %broadcast_select_fusion.rows_ref, bf16[1,4096,384]{2,1,0:T(8,128)(2,1)S(1)} %copy-done.1, bf16[1,4096,384]{2,1,0:T(8,128)(2,1)S(1)} %copy-done.2, bf16[1,384,4096]{2,1,0:T(8,128)(2,1)S(1)} %copy-done.3), custom_call_target="tpu_custom_call" | custom-call | flops 301989888 | bytes 9437184 | tf_op jit(solution)/shard_map/expert/pallas_call | solution.py:184
  58.7 4.1 %collective-permute-start.23 = (bf16[32,4096]{1,0:T(8,128)(2,1)S(1)}, bf16[32,4096]{1,0:T(8,128)(2,1)S(1)}, u32[]{:S(2)}, u32[]{:S(2)}) collective-permute-start(bf16[32,4096]{1,0:T(8,128)(2,1)S(1)} %expert.13), channel_id=1, source_target_pairs={{0,4},{1,5},{2,6},{3,7},{12,8},{13,9},{14,10},{15,11},{16,20},{17,... | collective-permute-start | bytes 786440 | tf_op jit(solution)/shard_map/ppermute | solution.py:225
  62.8 0.1 add_convert_fusion
  62.9 0.7 collective-permute-start.26
  63.5 0.1 add_convert_fusion.5
  63.6 0.7 collective-permute-start.12
  64.3 2.3 %collective-permute-done.23 = bf16[32,4096]{1,0:T(8,128)(2,1)S(1)} collective-permute-done((bf16[32,4096]{1,0:T(8,128)(2,1)S(1)}, bf16[32,4096]{1,0:T(8,128)(2,1)S(1)}, u32[]{:S(2)}, u32[]{:S(2)}) %collective-permute-start.23) | collective-permute-done | bytes 262176 | tf_op jit(solution)/shard_map/ppermute | solution.py:225
  66.6 0.1 add_convert_fusion.2
  66.7 0.7 collective-permute-start.24
  67.4 0.1 add_convert_fusion.4
  67.5 1.3 %collective-permute-start.13 = (bf16[32,4096]{1,0:T(8,128)(2,1)S(1)}, bf16[32,4096]{1,0:T(8,128)(2,1)S(1)}, u32[]{:S(2)}, u32[]{:S(2)}) collective-permute-start(bf16[32,4096]{1,0:T(8,128)(2,1)S(1)} %add_convert_fusion.4), channel_id=1, source_target_pairs={{4,0},{5,1},{6,2},{7,3},{8,12},{9,13},{10,14},{11,15},{20,16},{21,... | collective-permute-start | bytes 786440 | tf_op jit(solution)/shard_map/ppermute | solution.py:225
  68.8 0.1 add_convert_fusion.1
  68.9 1.5 %collective-permute-start.25 = (bf16[32,4096]{1,0:T(8,128)(2,1)S(1)}, bf16[32,4096]{1,0:T(8,128)(2,1)S(1)}, u32[]{:S(2)}, u32[]{:S(2)}) collective-permute-start(bf16[32,4096]{1,0:T(8,128)(2,1)S(1)} %add_convert_fusion.1), channel_id=1, source_target_pairs={{4,0},{5,1},{6,2},{7,3},{8,12},{9,13},{10,14},{11,15},{20,16},{21,... | collective-permute-start | bytes 786440 | tf_op jit(solution)/shard_map/ppermute | solution.py:225
  70.3 1.8 %expert.7 = bf16[64,4096]{1,0:T(8,128)(2,1)S(1)} custom-call(bf16[64,4096]{1,0:T(8,128)(2,1)S(1)} %get-tuple-element.32.rows_ref, bf16[1,4096,384]{2,1,0:T(8,128)(2,1)S(1)} %copy-done.1, bf16[1,4096,384]{2,1,0:T(8,128)(2,1)S(1)} %copy-done.2, bf16[1,384,4096]{2,1,0:T(8,128)(2,1)S(1)} %copy-done.3), custom_call_target="tpu_custom_call" | custom-call | flops 603979776 | bytes 9437184 | tf_op jit(solution)/shard_map/expert/pallas_call | solution.py:184
  72.2 12.1 %collective-permute-done.13 = bf16[32,4096]{1,0:T(8,128)(2,1)S(1)} collective-permute-done((bf16[32,4096]{1,0:T(8,128)(2,1)S(1)}, bf16[32,4096]{1,0:T(8,128)(2,1)S(1)}, u32[]{:S(2)}, u32[]{:S(2)}) %collective-permute-start.13) | collective-permute-done | bytes 262176 | tf_op jit(solution)/shard_map/ppermute | solution.py:225
  84.3 2.8 %collective-permute-done.25 = bf16[32,4096]{1,0:T(8,128)(2,1)S(1)} collective-permute-done((bf16[32,4096]{1,0:T(8,128)(2,1)S(1)}, bf16[32,4096]{1,0:T(8,128)(2,1)S(1)}, u32[]{:S(2)}, u32[]{:S(2)}) %collective-permute-start.25) | collective-permute-done | bytes 262176 | tf_op jit(solution)/shard_map/ppermute | solution.py:225
  87.1 0.3 fusion.6
  87.4 0.1 collective-permute-start.15
  87.5 1.6 %collective-permute-start.16 = (bf16[8,4096]{1,0:T(8,128)(2,1)S(1)}, bf16[8,4096]{1,0:T(8,128)(2,1)S(1)}, u32[]{:S(2)}, u32[]{:S(2)}) collective-permute-start(bf16[8,4096]{1,0:T(8,128)(2,1)S(1)} %get-tuple-element.28), channel_id=1, source_target_pairs={{0,2},{1,3},{2,0},{3,1},{4,6},{5,7},{6,4},{7,5},{8,10},{9,11},{10,... | collective-permute-start | bytes 196616 | tf_op jit(solution)/shard_map/ppermute | solution.py:219
  89.1 0.3 collective-permute-start.17
  89.4 0.4 collective-permute-start.27
  89.8 1.6 %collective-permute-start.28 = (bf16[8,4096]{1,0:T(8,128)(2,1)S(1)}, bf16[8,4096]{1,0:T(8,128)(2,1)S(1)}, u32[]{:S(2)}, u32[]{:S(2)}) collective-permute-start(bf16[8,4096]{1,0:T(8,128)(2,1)S(1)} %get-tuple-element.24), channel_id=1, source_target_pairs={{0,2},{1,3},{2,0},{3,1},{4,6},{5,7},{6,4},{7,5},{8,10},{9,11},{10,... | collective-permute-start | bytes 196616 | tf_op jit(solution)/shard_map/ppermute | solution.py:219
  91.4 1.1 %shares.1.weight_ref = bf16[128,128]{1,0:T(8,128)(2,1)S(1)} custom-call(s32[1]{0:T(128)} %bitcast.me_ref, bf16[128,4096]{1,0:T(8,128)(2,1)S(1)} %copy-done.5, bf16[1,4096]{1,0:T(2,128)(2,1)S(1)} %broadcast_in_dim.7.gain_ref, s32[8,128]{1,0:T(8,128)S(1)} %bitcast.3, bf16[4096,128]{1,0:T(8,128)(2,1)S(1)} %copy-done.6), custom_call_target="tpu_custom_call" | custom-call | flops 134217728 | bytes 2097152 | tf_op jit(solution)/shard_map/shares/pallas_call | solution.py:167
  92.5 0.6 collective-permute-done.17.refs_3_
  93.1 2.1 %collective-permute-done.28.refs_6_ = bf16[8,4096]{1,0:T(8,128)(2,1)S(1)} collective-permute-done((bf16[8,4096]{1,0:T(8,128)(2,1)S(1)}, bf16[8,4096]{1,0:T(8,128)(2,1)S(1)}, u32[]{:S(2)}, u32[]{:S(2)}) %collective-permute-start.28) | collective-permute-done | bytes 65568 | tf_op jit(solution)/shard_map/ppermute | solution.py:219
  95.2 0.7 collective-permute-done.29.refs_7_
  95.9 2.1 %combine.1 = bf16[128,4096]{1,0:T(8,128)(2,1)} custom-call(bf16[128,128]{1,0:T(8,128)(2,1)S(1)} %shares.1.weight_ref, bf16[8,4096]{1,0:T(8,128)(2,1)S(1)} %get-tuple-element.30.refs_0_, bf16[8,4096]{1,0:T(8,128)(2,1)S(1)} %collective-permute-done.15.refs_1_, bf16[8,4096]{1,0:T(8,128)(2,1)S(1)} %collective-permute-done.16.refs_2_, ...), custom_call_target="tpu_custom_call" | custom-call | tf_op jit(solution)/shard_map/combine/pallas_call | solution.py:201
  (50 shorter events, 0.5 us)
Async XLA Ops:
  0.7 1.2 %copy-start.4 = (bf16[128,4096]{1,0:T(8,128)(2,1)S(1)}, bf16[128,4096]{1,0:T(8,128)(2,1)}, u32[]{:S(2)}) copy-start(bf16[128,4096]{1,0:T(8,128)(2,1)} %hidden_ref.3) | copy-start | bytes 3145732
  1.9 0.7 copy-start.7
  3.3 5.3 %collective-permute-start = (bf16[8,4096]{1,0:T(8,128)(2,1)S(1)}, bf16[8,4096]{1,0:T(8,128)(2,1)S(1)}, u32[]{:S(2)}, u32[]{:S(2)}) collective-permute-start(bf16[8,4096]{1,0:T(8,128)(2,1)S(1)} %get-tuple-element.14), channel_id=1, source_target_pairs={{0,1},{1,0},{2,3},{3,2},{4,5},{5,4},{6,7},{7,6},{8,9},{9,8},{10,11... | collective-permute-start | bytes 196616 | tf_op jit(solution)/shard_map/ppermute | solution.py:219
  3.8 5.3 %collective-permute-start.1 = (bf16[8,4096]{1,0:T(8,128)(2,1)S(1)}, bf16[8,4096]{1,0:T(8,128)(2,1)S(1)}, u32[]{:S(2)}, u32[]{:S(2)}) collective-permute-start(bf16[8,4096]{1,0:T(8,128)(2,1)S(1)} %get-tuple-element.15), channel_id=1, source_target_pairs={{0,2},{1,3},{2,0},{3,1},{4,6},{5,7},{6,4},{7,5},{8,10},{9,11},{10,... | collective-permute-start | bytes 196616 | tf_op jit(solution)/shard_map/ppermute | solution.py:219
  6.4 4.0 %collective-permute-start.2 = (bf16[8,4096]{1,0:T(8,128)(2,1)S(1)}, bf16[8,4096]{1,0:T(8,128)(2,1)S(1)}, u32[]{:S(2)}, u32[]{:S(2)}) collective-permute-start(bf16[8,4096]{1,0:T(8,128)(2,1)S(1)} %get-tuple-element.16), channel_id=1, source_target_pairs={{0,3},{1,2},{2,1},{3,0},{4,7},{5,6},{6,5},{7,4},{8,11},{9,10},{10,... | collective-permute-start | bytes 196616 | tf_op jit(solution)/shard_map/ppermute | solution.py:219
  6.5 6.3 %collective-permute-start.3 = (bf16[8,4096]{1,0:T(8,128)(2,1)S(1)}, bf16[8,4096]{1,0:T(8,128)(2,1)S(1)}, u32[]{:S(2)}, u32[]{:S(2)}) collective-permute-start(bf16[8,4096]{1,0:T(8,128)(2,1)S(1)} %get-tuple-element.18), channel_id=1, source_target_pairs={{0,1},{1,0},{2,3},{3,2},{4,5},{5,4},{6,7},{7,6},{8,9},{9,8},{10,11... | collective-permute-start | bytes 196616 | tf_op jit(solution)/shard_map/ppermute | solution.py:219
  6.6 6.2 %collective-permute-start.4 = (bf16[8,4096]{1,0:T(8,128)(2,1)S(1)}, bf16[8,4096]{1,0:T(8,128)(2,1)S(1)}, u32[]{:S(2)}, u32[]{:S(2)}) collective-permute-start(bf16[8,4096]{1,0:T(8,128)(2,1)S(1)} %get-tuple-element.19), channel_id=1, source_target_pairs={{0,2},{1,3},{2,0},{3,1},{4,6},{5,7},{6,4},{7,5},{8,10},{9,11},{10,... | collective-permute-start | bytes 196616 | tf_op jit(solution)/shard_map/ppermute | solution.py:219
  8.6 4.7 %collective-permute-start.5 = (bf16[8,4096]{1,0:T(8,128)(2,1)S(1)}, bf16[8,4096]{1,0:T(8,128)(2,1)S(1)}, u32[]{:S(2)}, u32[]{:S(2)}) collective-permute-start(bf16[8,4096]{1,0:T(8,128)(2,1)S(1)} %get-tuple-element.20), channel_id=1, source_target_pairs={{0,3},{1,2},{2,1},{3,0},{4,7},{5,6},{6,5},{7,4},{8,11},{9,10},{10,... | collective-permute-start | bytes 196616 | tf_op jit(solution)/shard_map/ppermute | solution.py:219
  10.5 9.2 %collective-permute-start.6 = (bf16[32,4096]{1,0:T(8,128)(2,1)S(1)}, bf16[32,4096]{1,0:T(8,128)(2,1)S(1)}, u32[]{:S(2)}, u32[]{:S(2)}) collective-permute-start(bf16[32,4096]{1,0:T(8,128)(2,1)S(1)} %get-tuple-element.40), channel_id=1, source_target_pairs={{0,4},{1,5},{2,6},{3,7},{4,0},{5,1},{6,2},{7,3},{8,12},{9,13},{10,... | collective-permute-start | bytes 786440 | tf_op jit(solution)/shard_map/ppermute | solution.py:225
  12.1 14.9 %collective-permute-start.7 = (bf16[32,4096]{1,0:T(8,128)(2,1)S(1)}, bf16[32,4096]{1,0:T(8,128)(2,1)S(1)}, u32[]{:S(2)}, u32[]{:S(2)}) collective-permute-start(bf16[32,4096]{1,0:T(8,128)(2,1)S(1)} %get-tuple-element.40), channel_id=1, source_target_pairs={{4,8},{5,9},{6,10},{7,11},{8,4},{9,5},{10,6},{11,7},{20,24},{21,25... | collective-permute-start | bytes 786440 | tf_op jit(solution)/shard_map/ppermute | solution.py:230
  13.3 15.4 %collective-permute-start.18 = (bf16[32,4096]{1,0:T(8,128)(2,1)S(1)}, bf16[32,4096]{1,0:T(8,128)(2,1)S(1)}, u32[]{:S(2)}, u32[]{:S(2)}) collective-permute-start(bf16[32,4096]{1,0:T(8,128)(2,1)S(1)} %get-tuple-element.31), channel_id=1, source_target_pairs={{0,4},{1,5},{2,6},{3,7},{4,0},{5,1},{6,2},{7,3},{8,12},{9,13},{10,... | collective-permute-start | bytes 786440 | tf_op jit(solution)/shard_map/ppermute | solution.py:225
  17.4 13.0 %collective-permute-start.19 = (bf16[32,4096]{1,0:T(8,128)(2,1)S(1)}, bf16[32,4096]{1,0:T(8,128)(2,1)S(1)}, u32[]{:S(2)}, u32[]{:S(2)}) collective-permute-start(bf16[32,4096]{1,0:T(8,128)(2,1)S(1)} %get-tuple-element.31), channel_id=1, source_target_pairs={{4,8},{5,9},{6,10},{7,11},{8,4},{9,5},{10,6},{11,7},{20,24},{21,25... | collective-permute-start | bytes 786440 | tf_op jit(solution)/shard_map/ppermute | solution.py:230
  19.7 1.9 %copy-start = (bf16[1,4096,384]{2,1,0:T(8,128)(2,1)S(1)}, bf16[1,4096,384]{2,1,0:T(8,128)(2,1)}, u32[]{:S(2)}) copy-start(bf16[1,4096,384]{2,1,0:T(8,128)(2,1)} %gate_ref.13) | copy-start | bytes 9437188
  21.5 1.9 %copy-start.2 = (bf16[1,4096,384]{2,1,0:T(8,128)(2,1)S(1)}, bf16[1,4096,384]{2,1,0:T(8,128)(2,1)}, u32[]{:S(2)}) copy-start(bf16[1,4096,384]{2,1,0:T(8,128)(2,1)} %up_ref.13) | copy-start | bytes 9437188
  23.4 1.9 %copy-start.3 = (bf16[1,384,4096]{2,1,0:T(8,128)(2,1)S(1)}, bf16[1,384,4096]{2,1,0:T(8,128)(2,1)}, u32[]{:S(2)}) copy-start(bf16[1,384,4096]{2,1,0:T(8,128)(2,1)} %down_ref.13) | copy-start | bytes 9437188
  25.3 3.3 %copy-start.1 = (bf16[1,4096,384]{2,1,0:T(8,128)(2,1)S(1)}, bf16[1,4096,384]{2,1,0:T(8,128)(2,1)}, u32[]{:S(2)}) copy-start(bf16[1,4096,384]{2,1,0:T(8,128)(2,1)} %gate_ref.13) | copy-start | bytes 9437188
  27.0 9.3 %collective-permute-start.8 = (bf16[32,4096]{1,0:T(8,128)(2,1)S(1)}, bf16[32,4096]{1,0:T(8,128)(2,1)S(1)}, u32[]{:S(2)}, u32[]{:S(2)}) collective-permute-start(bf16[32,4096]{1,0:T(8,128)(2,1)S(1)} %broadcast_select_fusion.7), channel_id=1, source_target_pairs={{0,4},{1,5},{2,6},{3,7},{4,0},{5,1},{6,2},{7,3},{8,12},{9,13},{10,... | collective-permute-start | bytes 786440 | tf_op jit(solution)/shard_map/ppermute | solution.py:225
  30.4 13.3 %collective-permute-start.20 = (bf16[32,4096]{1,0:T(8,128)(2,1)S(1)}, bf16[32,4096]{1,0:T(8,128)(2,1)S(1)}, u32[]{:S(2)}, u32[]{:S(2)}) collective-permute-start(bf16[32,4096]{1,0:T(8,128)(2,1)S(1)} %broadcast_select_fusion.3), channel_id=1, source_target_pairs={{0,4},{1,5},{2,6},{3,7},{4,0},{5,1},{6,2},{7,3},{8,12},{9,13},{10,... | collective-permute-start | bytes 786440 | tf_op jit(solution)/shard_map/ppermute | solution.py:225
  30.9 7.1 %collective-permute-start.9 = (bf16[32,4096]{1,0:T(8,128)(2,1)S(1)}, bf16[32,4096]{1,0:T(8,128)(2,1)S(1)}, u32[]{:S(2)}, u32[]{:S(2)}) collective-permute-start(bf16[32,4096]{1,0:T(8,128)(2,1)S(1)} %collective-permute-done.6.rows_ref), channel_id=1, source_target_pairs={{4,8},{5,9},{6,10},{7,11},{8,4},{9,5},{10,6},{11,7},{20,24},{21,25... | collective-permute-start | bytes 786440 | tf_op jit(solution)/shard_map/ppermute | solution.py:230
  31.6 13.8 %collective-permute-start.21 = (bf16[32,4096]{1,0:T(8,128)(2,1)S(1)}, bf16[32,4096]{1,0:T(8,128)(2,1)S(1)}, u32[]{:S(2)}, u32[]{:S(2)}) collective-permute-start(bf16[32,4096]{1,0:T(8,128)(2,1)S(1)} %collective-permute-done.18.rows_ref), channel_id=1, source_target_pairs={{4,8},{5,9},{6,10},{7,11},{8,4},{9,5},{10,6},{11,7},{20,24},{21,25... | collective-permute-start | bytes 786440 | tf_op jit(solution)/shard_map/ppermute | solution.py:230
  38.1 12.3 %collective-permute-start.10 = (bf16[32,4096]{1,0:T(8,128)(2,1)S(1)}, bf16[32,4096]{1,0:T(8,128)(2,1)S(1)}, u32[]{:S(2)}, u32[]{:S(2)}) collective-permute-start(bf16[32,4096]{1,0:T(8,128)(2,1)S(1)} %broadcast_select_fusion.5), channel_id=1, source_target_pairs={{0,4},{1,5},{2,6},{3,7},{4,0},{5,1},{6,2},{7,3},{8,12},{9,13},{10,... | collective-permute-start | bytes 786440 | tf_op jit(solution)/shard_map/ppermute | solution.py:225
  45.4 11.5 %collective-permute-start.22 = (bf16[32,4096]{1,0:T(8,128)(2,1)S(1)}, bf16[32,4096]{1,0:T(8,128)(2,1)S(1)}, u32[]{:S(2)}, u32[]{:S(2)}) collective-permute-start(bf16[32,4096]{1,0:T(8,128)(2,1)S(1)} %broadcast_select_fusion.1), channel_id=1, source_target_pairs={{0,4},{1,5},{2,6},{3,7},{4,0},{5,1},{6,2},{7,3},{8,12},{9,13},{10,... | collective-permute-start | bytes 786440 | tf_op jit(solution)/shard_map/ppermute | solution.py:225
  52.1 11.5 %collective-permute-start.11 = (bf16[32,4096]{1,0:T(8,128)(2,1)S(1)}, bf16[32,4096]{1,0:T(8,128)(2,1)S(1)}, u32[]{:S(2)}, u32[]{:S(2)}) collective-permute-start(bf16[32,4096]{1,0:T(8,128)(2,1)S(1)} %expert.10), channel_id=1, source_target_pairs={{0,4},{1,5},{2,6},{3,7},{12,8},{13,9},{14,10},{15,11},{16,20},{17,... | collective-permute-start | bytes 786440 | tf_op jit(solution)/shard_map/ppermute | solution.py:225
  56.3 15.8 %collective-permute-start.14 = (bf16[32,4096]{1,0:T(8,128)(2,1)S(1)}, bf16[32,4096]{1,0:T(8,128)(2,1)S(1)}, u32[]{:S(2)}, u32[]{:S(2)}) collective-permute-start(bf16[32,4096]{1,0:T(8,128)(2,1)S(1)} %add_convert_fusion.3), channel_id=1, source_target_pairs={{4,8},{5,9},{6,10},{7,11},{8,4},{9,5},{10,6},{11,7},{20,24},{21,25... | collective-permute-start | bytes 786440 | tf_op jit(solution)/shard_map/ppermute | solution.py:230
  58.7 8.0 %collective-permute-start.23 = (bf16[32,4096]{1,0:T(8,128)(2,1)S(1)}, bf16[32,4096]{1,0:T(8,128)(2,1)S(1)}, u32[]{:S(2)}, u32[]{:S(2)}) collective-permute-start(bf16[32,4096]{1,0:T(8,128)(2,1)S(1)} %expert.13), channel_id=1, source_target_pairs={{0,4},{1,5},{2,6},{3,7},{12,8},{13,9},{14,10},{15,11},{16,20},{17,... | collective-permute-start | bytes 786440 | tf_op jit(solution)/shard_map/ppermute | solution.py:225
  62.9 9.3 %collective-permute-start.26 = (bf16[32,4096]{1,0:T(8,128)(2,1)S(1)}, bf16[32,4096]{1,0:T(8,128)(2,1)S(1)}, u32[]{:S(2)}, u32[]{:S(2)}) collective-permute-start(bf16[32,4096]{1,0:T(8,128)(2,1)S(1)} %add_convert_fusion), channel_id=1, source_target_pairs={{4,8},{5,9},{6,10},{7,11},{8,4},{9,5},{10,6},{11,7},{20,24},{21,25... | collective-permute-start | bytes 786440 | tf_op jit(solution)/shard_map/ppermute | solution.py:230
  63.6 3.8 %collective-permute-start.12 = (bf16[32,4096]{1,0:T(8,128)(2,1)S(1)}, bf16[32,4096]{1,0:T(8,128)(2,1)S(1)}, u32[]{:S(2)}, u32[]{:S(2)}) collective-permute-start(bf16[32,4096]{1,0:T(8,128)(2,1)S(1)} %add_convert_fusion.5), channel_id=1, source_target_pairs={{4,8},{5,9},{6,10},{7,11},{8,4},{9,5},{10,6},{11,7},{20,24},{21,25... | collective-permute-start | bytes 786440 | tf_op jit(solution)/shard_map/ppermute | solution.py:230
  66.7 2.1 %collective-permute-start.24 = (bf16[32,4096]{1,0:T(8,128)(2,1)S(1)}, bf16[32,4096]{1,0:T(8,128)(2,1)S(1)}, u32[]{:S(2)}, u32[]{:S(2)}) collective-permute-start(bf16[32,4096]{1,0:T(8,128)(2,1)S(1)} %add_convert_fusion.2), channel_id=1, source_target_pairs={{4,8},{5,9},{6,10},{7,11},{8,4},{9,5},{10,6},{11,7},{20,24},{21,25... | collective-permute-start | bytes 786440 | tf_op jit(solution)/shard_map/ppermute | solution.py:230
  67.5 16.8 %collective-permute-start.13 = (bf16[32,4096]{1,0:T(8,128)(2,1)S(1)}, bf16[32,4096]{1,0:T(8,128)(2,1)S(1)}, u32[]{:S(2)}, u32[]{:S(2)}) collective-permute-start(bf16[32,4096]{1,0:T(8,128)(2,1)S(1)} %add_convert_fusion.4), channel_id=1, source_target_pairs={{4,0},{5,1},{6,2},{7,3},{8,12},{9,13},{10,14},{11,15},{20,16},{21,... | collective-permute-start | bytes 786440 | tf_op jit(solution)/shard_map/ppermute | solution.py:225
  68.9 18.2 %collective-permute-start.25 = (bf16[32,4096]{1,0:T(8,128)(2,1)S(1)}, bf16[32,4096]{1,0:T(8,128)(2,1)S(1)}, u32[]{:S(2)}, u32[]{:S(2)}) collective-permute-start(bf16[32,4096]{1,0:T(8,128)(2,1)S(1)} %add_convert_fusion.1), channel_id=1, source_target_pairs={{4,0},{5,1},{6,2},{7,3},{8,12},{9,13},{10,14},{11,15},{20,16},{21,... | collective-permute-start | bytes 786440 | tf_op jit(solution)/shard_map/ppermute | solution.py:225
  72.1 19.2 %copy-start.5 = (bf16[128,4096]{1,0:T(8,128)(2,1)S(1)}, bf16[128,4096]{1,0:T(8,128)(2,1)}, u32[]{:S(2)}) copy-start(bf16[128,4096]{1,0:T(8,128)(2,1)} %hidden_ref.3) | copy-start | bytes 3145732
  72.1 19.2 %copy-start.6 = (bf16[4096,128]{1,0:T(8,128)(2,1)S(1)}, bf16[4096,128]{1,0:T(8,128)(2,1)}, u32[]{:S(2)}) copy-start(bf16[4096,128]{1,0:T(8,128)(2,1)} %router_ref.1) | copy-start | bytes 3145732
  72.1 19.2 %copy-start.8 = (s32[128,8]{0,1:T(8,128)S(1)}, s32[128,8]{0,1:T(8,128)}, u32[]{:S(2)}) copy-start(s32[128,8]{0,1:T(8,128)} %param.10) | copy-start | bytes 12292
  87.4 3.9 %collective-permute-start.15 = (bf16[8,4096]{1,0:T(8,128)(2,1)S(1)}, bf16[8,4096]{1,0:T(8,128)(2,1)S(1)}, u32[]{:S(2)}, u32[]{:S(2)}) collective-permute-start(bf16[8,4096]{1,0:T(8,128)(2,1)S(1)} %get-tuple-element.29), channel_id=1, source_target_pairs={{0,1},{1,0},{2,3},{3,2},{4,5},{5,4},{6,7},{7,6},{8,9},{9,8},{10,11... | collective-permute-start | bytes 196616 | tf_op jit(solution)/shard_map/ppermute | solution.py:219
  87.5 5.0 %collective-permute-start.16 = (bf16[8,4096]{1,0:T(8,128)(2,1)S(1)}, bf16[8,4096]{1,0:T(8,128)(2,1)S(1)}, u32[]{:S(2)}, u32[]{:S(2)}) collective-permute-start(bf16[8,4096]{1,0:T(8,128)(2,1)S(1)} %get-tuple-element.28), channel_id=1, source_target_pairs={{0,2},{1,3},{2,0},{3,1},{4,6},{5,7},{6,4},{7,5},{8,10},{9,11},{10,... | collective-permute-start | bytes 196616 | tf_op jit(solution)/shard_map/ppermute | solution.py:219
  89.1 4.0 %collective-permute-start.17 = (bf16[8,4096]{1,0:T(8,128)(2,1)S(1)}, bf16[8,4096]{1,0:T(8,128)(2,1)S(1)}, u32[]{:S(2)}, u32[]{:S(2)}) collective-permute-start(bf16[8,4096]{1,0:T(8,128)(2,1)S(1)} %get-tuple-element.27), channel_id=1, source_target_pairs={{0,3},{1,2},{2,1},{3,0},{4,7},{5,6},{6,5},{7,4},{8,11},{9,10},{10,... | collective-permute-start | bytes 196616 | tf_op jit(solution)/shard_map/ppermute | solution.py:219
  89.4 3.8 %collective-permute-start.27 = (bf16[8,4096]{1,0:T(8,128)(2,1)S(1)}, bf16[8,4096]{1,0:T(8,128)(2,1)S(1)}, u32[]{:S(2)}, u32[]{:S(2)}) collective-permute-start(bf16[8,4096]{1,0:T(8,128)(2,1)S(1)} %get-tuple-element.25), channel_id=1, source_target_pairs={{0,1},{1,0},{2,3},{3,2},{4,5},{5,4},{6,7},{7,6},{8,9},{9,8},{10,11... | collective-permute-start | bytes 196616 | tf_op jit(solution)/shard_map/ppermute | solution.py:219
  89.8 5.4 %collective-permute-start.28 = (bf16[8,4096]{1,0:T(8,128)(2,1)S(1)}, bf16[8,4096]{1,0:T(8,128)(2,1)S(1)}, u32[]{:S(2)}, u32[]{:S(2)}) collective-permute-start(bf16[8,4096]{1,0:T(8,128)(2,1)S(1)} %get-tuple-element.24), channel_id=1, source_target_pairs={{0,2},{1,3},{2,0},{3,1},{4,6},{5,7},{6,4},{7,5},{8,10},{9,11},{10,... | collective-permute-start | bytes 196616 | tf_op jit(solution)/shard_map/ppermute | solution.py:219
  91.3 4.6 %collective-permute-start.29 = (bf16[8,4096]{1,0:T(8,128)(2,1)S(1)}, bf16[8,4096]{1,0:T(8,128)(2,1)S(1)}, u32[]{:S(2)}, u32[]{:S(2)}) collective-permute-start(bf16[8,4096]{1,0:T(8,128)(2,1)S(1)} %get-tuple-element.23), channel_id=1, source_target_pairs={{0,3},{1,2},{2,1},{3,0},{4,7},{5,6},{6,5},{7,4},{8,11},{9,10},{10,... | collective-permute-start | bytes 196616 | tf_op jit(solution)/shard_map/ppermute | solution.py:219

commit v3 on v2

v3 whole, which is shorter than its diff:
```python
import functools

import jax
import jax.numpy as jnp
from jax import lax
from jax.experimental import pallas as pl
from jax.experimental.pallas import tpu as pltpu
from jax.sharding import PartitionSpec as P

SPLIT = 4
CAP = 16
EPS = 1e-06
PIECE = 512
COLUMNS = 512
VMEM_LIMIT = 16 * 1024 * 1024


def slots_of(ids, me, flight):
    tokens = ids.shape[1]
    named = jnp.concatenate(
        [
            jnp.max((ids == (me ^ k)).astype(jnp.float32), axis=0, keepdims=True)
            for k in range(flight)
        ],
        axis=0,
    )
    earlier = lax.broadcasted_iota(jnp.int32, (tokens, tokens), 0) < lax.broadcasted_iota(
        jnp.int32, (tokens, tokens), 1
    )
    place = jnp.dot(
        named.astype(jnp.bfloat16),
        earlier.astype(jnp.float32).astype(jnp.bfloat16),
        preferred_element_type=jnp.float32,
    )
    return named, place


def spread(named, place, value, flight):
    slot = lax.broadcasted_iota(jnp.int32, (CAP, named.shape[1]), 0).astype(jnp.float32)
    return jnp.concatenate(
        [
            jnp.where(
                (place[k : k + 1] == slot) & (named[k : k + 1] > 0.0), value[k : k + 1], 0.0
            )
            for k in range(flight)
        ],
        axis=0,
    )


def inv_rms_of(hidden_ref):
    rows, width = hidden_ref.shape
    piece = min(width, PIECE)
    total = jnp.zeros((rows, 1), jnp.float32)
    for i in range(width // piece):
        x = hidden_ref[:, i * piece : (i + 1) * piece].astype(jnp.float32)
        total = total + jnp.sum(x * x, axis=1, keepdims=True)
    return lax.rsqrt(total / width + EPS)


def normed_piece(hidden_ref, gain_ref, inv_rms, cols):
    x = hidden_ref[:, cols].astype(jnp.float32)
    lanes = gain_ref.shape[1]
    gain = jnp.concatenate(
        [
            gain_ref[row : row + 1].astype(jnp.float32)
            for row in range(cols.start // lanes, (cols.start + cols.size) // lanes)
        ],
        axis=1,
    )
    return (x * inv_rms * gain).astype(jnp.bfloat16)


def fetch(sources, targets, sems):
    copies = [
        pltpu.make_async_copy(source, target, sems.at[at])
        for at, (source, target) in enumerate(zip(sources, targets))
    ]
    for copy in copies:
        copy.start()
    for copy in copies:
        copy.wait()


def dispatch_kernel(flight, me_ref, outer_ref, inner_ref, *refs):
    out_refs = refs[3 : 3 + flight]
    hidden_ref, gain_ref, ids_ref, sems = refs[3 + flight :]
    fetch(refs[:3], (hidden_ref, gain_ref, ids_ref), sems)
    width = hidden_ref.shape[1]
    piece = min(width, PIECE)
    inv_rms = inv_rms_of(hidden_ref)
    named, place = slots_of(ids_ref[...], me_ref[0], flight)
    select = spread(named, place, named, flight).astype(jnp.bfloat16)
    for i in range(width // piece):
        cols = pl.ds(i * piece, piece)
        normed = normed_piece(hidden_ref, gain_ref, inv_rms, cols)
        rows = jnp.dot(select, normed, preferred_element_type=jnp.float32)
        for at, out_ref in enumerate(out_refs):
            out_ref[:, cols] = rows[at * CAP : (at + 1) * CAP].astype(jnp.bfloat16)


def shares_kernel(flight, me_ref, *refs):
    out_ref = refs[-6]
    hidden_ref, gain_ref, ids_ref, router_ref, sems = refs[-5:]
    fetch(refs[:4], (hidden_ref, gain_ref, ids_ref, router_ref), sems)
    width = hidden_ref.shape[1]
    experts = router_ref.shape[1]
    piece = min(width, PIECE)
    inv_rms = inv_rms_of(hidden_ref)
    logits = jnp.zeros((hidden_ref.shape[0], experts), jnp.float32)
    for i in range(width // piece):
        cols = pl.ds(i * piece, piece)
        normed = normed_piece(hidden_ref, gain_ref, inv_rms, cols)
        logits += jnp.dot(normed, router_ref[cols, :], preferred_element_type=jnp.float32)
    logits = logits.T
    raised = jnp.exp(logits - jnp.max(logits, axis=0, keepdims=True))
    probs = raised / jnp.sum(raised, axis=0, keepdims=True)
    ids = ids_ref[...]
    expert = lax.broadcasted_iota(jnp.int32, probs.shape, 0)
    picked = jnp.zeros(probs.shape, jnp.float32)
    for k in range(ids.shape[0]):
        picked = jnp.where(ids[k : k + 1] == expert, probs, picked)
    me = me_ref[0]
    named, place = slots_of(ids, me, flight)
    flying = jnp.concatenate(
        [
            jnp.sum(jnp.where(expert == (me ^ k), probs, 0.0), axis=0, keepdims=True)
            for k in range(flight)
        ],
        axis=0,
    )
    share = flying / jnp.sum(picked, axis=0, keepdims=True)
    weight = spread(named, place, share, flight).T
    high = weight.astype(jnp.bfloat16)
    low = (weight - high.astype(jnp.float32)).astype(jnp.bfloat16)
    out_ref[...] = jnp.concatenate([high, low], axis=1)


def expert_kernel(rows_ref, gate_ref, up_ref, down_ref, *refs):
    out_ref = refs[-1]
    rows = rows_ref[...]
    gate_act = jnp.dot(rows, gate_ref[0], preferred_element_type=jnp.float32)
    up_act = jnp.dot(rows, up_ref[0], preferred_element_type=jnp.float32)
    hidden_act = (jax.nn.silu(gate_act) * up_act).astype(jnp.bfloat16)
    width = out_ref.shape[1]
    piece = min(width, PIECE)
    for i in range(width // piece):
        cols = pl.ds(i * piece, piece)
        out_ref[:, cols] = jnp.dot(
            hidden_act, down_ref[0, :, cols], preferred_element_type=jnp.float32
        ).astype(jnp.bfloat16)


def expert_if_kernel(flag_ref, *refs):
    @pl.when(flag_ref[0] != 0)
    def _():
        expert_kernel(*refs)

    @pl.when(flag_ref[0] == 0)
    def _():
        refs[-1][...] = jnp.zeros_like(refs[-1])


def combine_kernel(weight_ref, *refs):
    *parts, out_ref, block_ref, sems = refs
    width = block_ref.shape[1]
    piece = min(width, COLUMNS)
    weight = weight_ref[...]
    copies = []
    for i in range(width // piece):
        cols = pl.ds(i * piece, piece)
        rows = jnp.concatenate([part[:, cols] for part in parts], axis=0)
        block_ref[:, cols] = jnp.dot(
            weight, jnp.concatenate([rows, rows], axis=0), preferred_element_type=jnp.float32
        ).astype(jnp.bfloat16)
        copy = pltpu.make_async_copy(block_ref.at[:, cols], out_ref.at[:, cols], sems.at[i])
        copy.start()
        copies.append(copy)
    for copy in copies:
        copy.wait()


def touch_kernel(*refs):
    refs[-1][...] = jnp.zeros_like(refs[-1])


def choose_kernel(flag_ref, ours_ref, theirs_ref, *refs):
    out_ref = refs[-1]

    @pl.when(flag_ref[0] != 0)
    def _():
        out_ref[...] = ours_ref[...]

    @pl.when(flag_ref[0] == 0)
    def _():
        out_ref[...] = theirs_ref[...]


def choose(flag, ours, theirs, after=()):
    return pl.pallas_call(
        choose_kernel,
        out_shape=jax.ShapeDtypeStruct(ours.shape, ours.dtype),
        in_specs=smem(1) + vmem(2) + anywhere(len(after)),
        out_specs=vmem(1)[0],
        compiler_params=params(),
        name="choose",
    )(flag, ours, theirs, *after)


def join_kernel(count, *refs):
    out_ref = refs[-1]
    depth = refs[0].shape[0]
    for at in range(count):
        out_ref[at * depth : (at + 1) * depth] = refs[at][...]


def join(parts, after=()):
    rows, width = parts[0].shape
    return pl.pallas_call(
        functools.partial(join_kernel, len(parts)),
        out_shape=jax.ShapeDtypeStruct((rows * len(parts), width), jnp.bfloat16),
        in_specs=vmem(len(parts)) + anywhere(len(after)),
        out_specs=vmem(1)[0],
        compiler_params=params(),
        name="join",
    )(*parts, *after)


def touch_any(*arrays):
    return pl.pallas_call(
        touch_kernel,
        out_shape=jax.ShapeDtypeStruct((8, 128), jnp.float32),
        in_specs=anywhere(len(arrays)),
        out_specs=vmem(1)[0],
        compiler_params=params(),
        name="seen",
    )(*arrays)


def mix_kernel(terms, *refs):
    out_refs = refs[terms[1] :]
    total = refs[0][...].astype(jnp.float32)
    for ref in refs[1 : terms[0]]:
        total = total + ref[...].astype(jnp.float32)
    depth = out_refs[0].shape[0]
    for at, out_ref in enumerate(out_refs):
        out_ref[...] = total[at * depth : (at + 1) * depth].astype(jnp.bfloat16)


def vmem(count):
    return [pl.BlockSpec(memory_space=pltpu.VMEM)] * count


def anywhere(count):
    return [pl.BlockSpec(memory_space=pl.ANY)] * count


def smem(count):
    return [pl.BlockSpec(memory_space=pltpu.SMEM)] * count


def params(limit=VMEM_LIMIT):
    return pltpu.CompilerParams(vmem_limit_bytes=limit)


def dispatch(scalars, hidden, gain, ids, flight):
    shape = jax.ShapeDtypeStruct((CAP, hidden.shape[1]), jnp.bfloat16)
    return pl.pallas_call(
        functools.partial(dispatch_kernel, flight),
        out_shape=[shape] * flight,
        in_specs=smem(len(scalars)) + anywhere(3),
        out_specs=vmem(flight),
        scratch_shapes=[pltpu.VMEM(x.shape, x.dtype) for x in (hidden, gain, ids)]
        + [pltpu.SemaphoreType.DMA((3,))],
        compiler_params=params(),
        cost_estimate=pl.CostEstimate(flops=1 << 17, bytes_accessed=128, transcendentals=0),
        name="dispatch",
    )(*scalars, hidden, gain, ids)


def shares(me, hidden, gain, ids, router, flight, *after):
    rows, width = hidden.shape
    return pl.pallas_call(
        functools.partial(shares_kernel, flight),
        out_shape=jax.ShapeDtypeStruct((rows, 2 * flight * CAP), jnp.bfloat16),
        in_specs=smem(1) + anywhere(4 + len(after)),
        out_specs=vmem(1)[0],
        scratch_shapes=[pltpu.VMEM(x.shape, x.dtype) for x in (hidden, gain, ids, router)]
        + [pltpu.SemaphoreType.DMA((4,))],
        compiler_params=params(),
        name="shares",
    )(me, hidden, gain, ids, router, *after)


def touch(array, *after):
    return pl.pallas_call(
        touch_kernel,
        out_shape=jax.ShapeDtypeStruct((8, 128), jnp.float32),
        in_specs=vmem(1) + anywhere(len(after)),
        out_specs=vmem(1)[0],
        compiler_params=params(),
        name="touch",
    )(array, *after)


def mix(terms, pieces=1, after=()):
    rows, width = terms[0].shape
    shape = jax.ShapeDtypeStruct((rows // pieces, width), jnp.bfloat16)
    return pl.pallas_call(
        functools.partial(mix_kernel, (len(terms), len(terms) + len(after))),
        out_shape=[shape] * pieces,
        in_specs=vmem(len(terms)) + anywhere(len(after)),
        out_specs=vmem(pieces),
        compiler_params=params(),
        name="mix",
    )(*terms, *after)


def finish_kernel(count, flag_ref, own_ref, *refs):
    ours, theirs = refs[: count[0]], refs[count[0] : count[1]]
    out_refs = refs[count[1] + count[2] :]
    depth = out_refs[0].shape[0]

    def add(others):
        total = own_ref[...].astype(jnp.float32)
        for ref in others:
            total = total + ref[...].astype(jnp.float32)
        for at, out_ref in enumerate(out_refs):
            out_ref[...] = total[at * depth : (at + 1) * depth].astype(jnp.bfloat16)

    @pl.when(flag_ref[0] != 0)
    def _():
        add(ours)

    @pl.when(flag_ref[0] == 0)
    def _():
        add(theirs)


def finish(flag, own, ours, theirs, pieces, after=()):
    rows, width = own.shape
    shape = jax.ShapeDtypeStruct((rows // pieces, width), jnp.bfloat16)
    return pl.pallas_call(
        functools.partial(
            finish_kernel, (len(ours), len(ours) + len(theirs), len(after))
        ),
        out_shape=[shape] * pieces,
        in_specs=smem(1) + vmem(1 + len(ours) + len(theirs)) + anywhere(len(after)),
        out_specs=vmem(pieces),
        compiler_params=params(),
        name="finish",
    )(flag, own, *ours, *theirs, *after)


def expert(name, flag, rows, gate_weight, up_weight, down_weight, after=()):
    count = gate_weight.size + up_weight.size + down_weight.size
    flags = [] if flag is None else [flag]
    return pl.pallas_call(
        expert_kernel if flag is None else expert_if_kernel,
        out_shape=jax.ShapeDtypeStruct(rows.shape, jnp.bfloat16),
        in_specs=smem(len(flags)) + vmem(4) + anywhere(len(after)),
        out_specs=vmem(1)[0],
        compiler_params=params(),
        cost_estimate=pl.CostEstimate(
            flops=2 * rows.shape[0] * count, bytes_accessed=2 * count, transcendentals=0
        ),
        name=name,
    )(*flags, rows, gate_weight, up_weight, down_weight, *after)


def combine(weight, parts):
    rows = weight.shape[0]
    width = parts[0].shape[1]
    return pl.pallas_call(
        combine_kernel,
        out_shape=jax.ShapeDtypeStruct((rows, width), jnp.bfloat16),
        in_specs=vmem(1 + len(parts)),
        out_specs=anywhere(1)[0],
        scratch_shapes=[
            pltpu.VMEM((rows, width), jnp.bfloat16),
            pltpu.SemaphoreType.DMA((width // min(width, COLUMNS),)),
        ],
        compiler_params=params(),
        name="combine",
    )(weight, *parts)


def in_plane(rows, k, flight):
    if k == 0:
        return rows
    pairs = [(m * flight + e, m * flight + (e ^ k)) for m in range(SPLIT) for e in range(flight)]
    with jax.named_scope("plane%d" % k):
        return lax.ppermute(rows, "expert", pairs)


def end_pair(rows, flight):
    pairs = [(m * flight + e, (m ^ 1) * flight + e) for m in range(SPLIT) for e in range(flight)]
    return lax.ppermute(rows, "expert", pairs)


def mirror_pair(rows, flight, members):
    pairs = [
        (m * flight + e, (SPLIT - 1 - m) * flight + e if m in members else m * flight + (e ^ 1))
        for m in range(SPLIT)
        for e in range(flight)
    ]
    return lax.ppermute(rows, "expert", pairs)


def shards(hidden, norm_gain, router_weight, expert_ids, gate_weight, up_weight, down_weight):
    devices = lax.axis_size("expert")
    flight = devices // SPLIT
    gain = norm_gain.reshape(-1, 128)
    ids = expert_ids.T
    index = lax.axis_index("expert")
    member = lax.div(index, flight)
    me = lax.rem(index, flight).reshape(1)
    inner_number = lax.rem(lax.div(member + 1, 2), 2)
    at_inner, at_outer = inner_number.reshape(1), (1 - inner_number).reshape(1)
    half = flight // 2
    tick = []

    def then(value):
        tick[:] = [value[0] if isinstance(value, (list, tuple)) else value]
        return value

    def partial(rows, flag=None):
        return then(
            expert("expert", flag, rows, gate_weight, up_weight, down_weight, tuple(tick))
        )

    def pick(ours, theirs):
        return then(choose(at_outer, ours, theirs, tuple(tick)))

    def total(*terms):
        return then(mix(terms, 1, tuple(tick)))[0]

    def seen(*arrays):
        return then(touch_any(*arrays, *tick))

    def end(name, rows):
        with jax.named_scope(name):
            return end_pair(rows, flight)

    def middle(name, rows, members=(1, 2)):
        with jax.named_scope(name):
            return mirror_pair(rows, flight, members)

    hidden, gain, ids = (
        pltpu.with_memory_space_constraint(x, pltpu.HBM) for x in (hidden, gain, ids)
    )
    sent = then(dispatch((me, at_outer, at_inner), hidden, gain, ids, flight))
    came = [in_plane(rows, k, flight) for k, rows in enumerate(sent)]
    own_a = then(join(came[:half], tuple(tick)))
    near_a, far_in_a = end("near_a", own_a), middle("far_in_a", own_a)
    for array in (gate_weight, up_weight, down_weight):
        then(touch(array, *tick))
    own_b = then(join(came[half:], tuple(tick)))
    near_b, far_in_b = end("near_b", own_b), middle("far_in_b", own_b)
    near_part_a = partial(near_a)
    last_in_a = middle("last_in_a", near_a)
    two_a = end("two_a", pick(near_part_a, far_in_a))
    near_part_b = partial(near_b)
    two_b = end("two_b", pick(near_part_b, far_in_b))
    last_in_b = middle("last_in_b", near_b)
    seen(last_in_a)
    far_part_a = partial(pick(two_a, far_in_a))
    three_a = end("three_a", pick(far_part_a, last_in_a))
    across_b = middle("across_b", partial(last_in_b, at_inner))
    far_part_b = partial(pick(two_b, far_in_b))
    three_b = end("three_b", pick(far_part_b, last_in_b))
    mid_a = middle("mid_a", total(far_part_a, three_a))
    last_part_a = partial(pick(three_a, last_in_a))
    four = end("four", pick(last_part_a, total(near_part_b, across_b)))
    mid_b = middle("mid_b", total(far_part_b, three_b))
    direct_b = middle("direct_b", partial(three_b, at_outer), (0, 3))
    seen(mid_a)
    mid2_a = middle("mid2_a", total(last_part_a, four))
    weight = then(shares(me, hidden, gain, ids, router_weight, flight, *tick))
    own_part_b, own_part_a = partial(own_b), partial(own_a)
    seen(mid_b)
    five_a = end("five_a", total(near_part_a, mid2_a))
    done_b = then(
        finish(at_outer, own_part_b, [four, direct_b], [two_b, mid_b], flight - half, tuple(tick))
    )
    done_a = then(finish(at_outer, own_part_a, [five_a], [two_a, mid_a], half, tuple(tick)))
    back = [in_plane(rows, k, flight) for k, rows in enumerate(list(done_a) + list(done_b))]
    return combine(weight, back)


def solution(mesh):
    tokens = P(("group", "expert"), None)
    sliced = P("expert", None, None)
    return jax.shard_map(
        shards,
        mesh=mesh,
        in_specs=(tokens, P(), P(), tokens, sliced, sliced, sliced),
        out_specs=tokens,
        check_vma=False,
    )
```

time: 98.6 us -> 76 us (0.77)
  waiting for transfers between devices: 31.9 us -> 15.1 us
  local copies, waits for them, and re-layouts: 8.42 us -> 1.91 us
  Pallas kernels: 15.5 us -> 19.8 us
  starting transfers between devices: 40.7 us -> 38.6 us
    ppermute x10 -> x8, waiting for transfers between devices: 26.3 us -> 9.74 us  [end_pair(): return lax.ppermute(rows, 'expert', pairs)]
    ppermute x20 -> x15, starting transfers between devices: 14.6 us -> 7.27 us  [the longest x6 4.84 us: in_plane(): return lax.ppermute(rows, 'expert', pairs)]
    unnamed x25 -> x10, local copies, waits for them, and re-layouts: 7.67 us -> 1.91 us
    ppermute x10 -> x8, starting transfers between devices: 26.1 us -> 31.3 us  [end_pair(): return lax.ppermute(rows, 'expert', pairs)]
    pallas_call x7 -> x32, Pallas kernels: 11.6 us -> 14.2 us  [the longest x9 13.4 us: expert(): pl.pallas_call(expert_kernel if flag is None else expert_if_kernel, out_s...]
    pallas_call x1, Pallas kernels: 0.68 us -> 2.08 us  [dispatch(): pl.pallas_call(functools.partial(dispatch_kernel, flight), out_shape=[sha...]
    pallas_call x1, Pallas kernels: 1.12 us -> 2.38 us  [shares(): pl.pallas_call(functools.partial(shares_kernel, flight), out_shape=jax.Sh...]
    ppermute x20 -> x15, waiting for transfers between devices: 5.66 us -> 5.31 us  [the longest x6 5.28 us: in_plane(): return lax.ppermute(rows, 'expert', pairs)]
  transfers between devices with their start and end apart: 30 -> 23, of which waited for: 12 -> 11; matrix products, arithmetic and copies ran while one was open for 1% -> 0% of each run, Pallas kernels for 13% -> 22%
where the time goes in v3:
time: 76 us; the launch traced here: 75.9 us
  starting transfers between devices  38.6 us (51%)
  Pallas kernels  19.8 us (26%)
  waiting for transfers between devices  15.1 us (20%)
  local copies, waits for them, and re-layouts  1.91 us (3%)
    ppermute x8, starting transfers between devices, end_pair(): return lax.ppermute(rows, 'expert', pairs)  31.3 us
    pallas_call x9, Pallas kernels, expert(): pl.pallas_call(expert_kernel if flag is None else expert_if_kernel, out_s...  13.4 us
    ppermute x8, waiting for transfers between devices, end_pair(): return lax.ppermute(rows, 'expert', pairs)  9.74 us
    ppermute x6, waiting for transfers between devices, in_plane(): return lax.ppermute(rows, 'expert', pairs)  5.28 us
    ppermute x6, starting transfers between devices, in_plane(): return lax.ppermute(rows, 'expert', pairs)  4.84 us
    ppermute x9, starting transfers between devices, mirror_pair(): return lax.ppermute(rows, 'expert', pairs)  2.43 us
    pallas_call x1, Pallas kernels, shares(): pl.pallas_call(functools.partial(shares_kernel, flight), out_shape=jax.Sh...  2.38 us
    pallas_call x1, Pallas kernels, dispatch(): pl.pallas_call(functools.partial(dispatch_kernel, flight), out_shape=[sha...  2.08 us
  transfers between devices with their start and end apart: 23, of which 11 were waited for; matrix products, arithmetic and copies ran while one was open for 0% of the time, Pallas kernels for 22%

profile of v3, /device:TPU:0, one launch (start us, length us, event | category | flops | bytes accessed | tf_op | source)
XLA Modules:
  0.0 75.9 jit_solution(1683253624986381661)
XLA Ops:
  0.0 2.1 %dispatch.1 = (bf16[16,4096]{1,0:T(8,128)(2,1)S(1)}, bf16[16,4096]{1,0:T(8,128)(2,1)S(1)}, bf16[16,4096]{1,0:T(8,128)(2,1)S(1)}, bf16[16,4096]{1,0:T(8,128)(2,1)S(1)}) custom-call(s32[1]{0:T(128)} %bitcast.me_ref, s32[1]{0:T(128)} %bitcast.3.outer_ref.flag_ref, s32[1]{0:T(128)} %bitcast.4.inner_ref.flag_ref, bf16[128,4096]{1,0:T(8,128)(2,1)} %refs_0_.9, ...), custom_call_target="tpu_custom_call" | custom-call | flops 131072 | bytes 128 | tf_op jit(solution)/shard_map/dispatch/pallas_call | solution.py:268
  2.1 0.5 collective-permute-start
  2.6 2.6 %collective-permute-start.2 = (bf16[16,4096]{1,0:T(8,128)(2,1)S(1)}, bf16[16,4096]{1,0:T(8,128)(2,1)S(1)}, u32[]{:S(2)}, u32[]{:S(2)}) collective-permute-start(bf16[16,4096]{1,0:T(8,128)(2,1)S(1)} %get-tuple-element.15), channel_id=1, source_target_pairs={{0,2},{1,3},{2,0},{3,1},{4,6},{5,7},{6,4},{7,5},{8,10},{9,11},{10,... | collective-permute-start | bytes 393224 | tf_op jit(solution)/shard_map/plane2/ppermute | solution.py:393
  5.2 0.1 collective-permute-start.3
  5.3 0.0 collective-permute-done.refs_1_
  5.3 0.0 copy-start.1
  5.3 1.8 %collective-permute-start.1 = (bf16[32,4096]{1,0:T(8,128)(2,1)S(1)}, bf16[32,4096]{1,0:T(8,128)(2,1)S(1)}, u32[]{:S(2)}, u32[]{:S(2)}) collective-permute-start(bf16[32,4096]{1,0:T(8,128)(2,1)S(1)} %join.2.refs_1_.rows_ref), channel_id=1, source_target_pairs={{0,4},{1,5},{2,6},{3,7},{4,0},{5,1},{6,2},{7,3},{8,12},{9,13},{10,... | collective-permute-start | bytes 786440 | tf_op jit(solution)/shard_map/near_a/ppermute | solution.py:398
  7.2 0.1 collective-permute-start.4
  7.2 1.9 %copy-done.2 = bf16[1,4096,384]{2,1,0:T(8,128)(2,1)S(1)} copy-done((bf16[1,4096,384]{2,1,0:T(8,128)(2,1)S(1)}, bf16[1,4096,384]{2,1,0:T(8,128)(2,1)}, u32[]{:S(2)}) %copy-start.2) | copy-done | bytes 3145752
  9.1 0.4 collective-permute-done.2.refs_0_
  9.6 2.3 %collective-permute-done.3.refs_1_ = bf16[16,4096]{1,0:T(8,128)(2,1)S(1)} collective-permute-done((bf16[16,4096]{1,0:T(8,128)(2,1)S(1)}, bf16[16,4096]{1,0:T(8,128)(2,1)S(1)}, u32[]{:S(2)}, u32[]{:S(2)}) %collective-permute-start.3) | collective-permute-done | bytes 131104 | tf_op jit(solution)/shard_map/plane3/ppermute | solution.py:393
  11.9 1.7 %collective-permute-start.7 = (bf16[32,4096]{1,0:T(8,128)(2,1)S(1)}, bf16[32,4096]{1,0:T(8,128)(2,1)S(1)}, u32[]{:S(2)}, u32[]{:S(2)}) collective-permute-start(bf16[32,4096]{1,0:T(8,128)(2,1)S(1)} %join.3.refs_0_.rows_ref), channel_id=1, source_target_pairs={{0,4},{1,5},{2,6},{3,7},{4,0},{5,1},{6,2},{7,3},{8,12},{9,13},{10,... | collective-permute-start | bytes 786440 | tf_op jit(solution)/shard_map/near_b/ppermute | solution.py:398
  13.5 0.3 collective-permute-start.8
  13.8 0.1 collective-permute-done.1.rows_ref
  14.0 1.7 %expert.9.ours_ref.refs_0_ = bf16[32,4096]{1,0:T(8,128)(2,1)S(1)} custom-call(bf16[32,4096]{1,0:T(8,128)(2,1)S(1)} %collective-permute-done.1.rows_ref, bf16[1,4096,384]{2,1,0:T(8,128)(2,1)S(1)} %copy-done.3, bf16[1,4096,384]{2,1,0:T(8,128)(2,1)S(1)} %copy-done, bf16[1,384,4096]{2,1,0:T(8,128)(2,1)S(1)} %copy-done.1, bf16[32,4096]{1,0:T(8,128)(2,1)S(1)} %join.3.refs_0_.rows_ref), custom_call_target="tpu_custom_call" | custom-call | flops 301989888 | bytes 9437184 | tf_op jit(solution)/shard_map/expert/pallas_call | solution.py:358
  15.6 0.1 collective-permute-start.6
  15.8 0.0 collective-permute-done.4.theirs_ref
  15.8 3.3 %collective-permute-start.5 = (bf16[32,4096]{1,0:T(8,128)(2,1)S(1)}, bf16[32,4096]{1,0:T(8,128)(2,1)S(1)}, u32[]{:S(2)}, u32[]{:S(2)}) collective-permute-start(bf16[32,4096]{1,0:T(8,128)(2,1)S(1)} %choose.8.refs_0_), channel_id=1, source_target_pairs={{0,4},{1,5},{2,6},{3,7},{4,0},{5,1},{6,2},{7,3},{8,12},{9,13},{10,... | collective-permute-start | bytes 786440 | tf_op jit(solution)/shard_map/two_a/ppermute | solution.py:398
  19.1 2.0 %collective-permute-done.7.rows_ref = bf16[32,4096]{1,0:T(8,128)(2,1)S(1)} collective-permute-done((bf16[32,4096]{1,0:T(8,128)(2,1)S(1)}, bf16[32,4096]{1,0:T(8,128)(2,1)S(1)}, u32[]{:S(2)}, u32[]{:S(2)}) %collective-permute-start.7) | collective-permute-done | bytes 262176 | tf_op jit(solution)/shard_map/near_b/ppermute | solution.py:398
  21.1 0.0 collective-permute-start.11
  21.1 1.7 %expert.10.ours_ref.refs_0_ = bf16[32,4096]{1,0:T(8,128)(2,1)S(1)} custom-call(bf16[32,4096]{1,0:T(8,128)(2,1)S(1)} %collective-permute-done.7.rows_ref, bf16[1,4096,384]{2,1,0:T(8,128)(2,1)S(1)} %copy-done.3, bf16[1,4096,384]{2,1,0:T(8,128)(2,1)S(1)} %copy-done, bf16[1,384,4096]{2,1,0:T(8,128)(2,1)S(1)} %copy-done.1, bf16[32,4096]{1,0:T(8,128)(2,1)S(1)} %choose.8.refs_0_), custom_call_target="tpu_custom_call" | custom-call | flops 301989888 | bytes 9437184 | tf_op jit(solution)/shard_map/expert/pallas_call | solution.py:358
  22.7 0.0 collective-permute-done.8.theirs_ref
  22.8 3.2 %collective-permute-start.10 = (bf16[32,4096]{1,0:T(8,128)(2,1)S(1)}, bf16[32,4096]{1,0:T(8,128)(2,1)S(1)}, u32[]{:S(2)}, u32[]{:S(2)}) collective-permute-start(bf16[32,4096]{1,0:T(8,128)(2,1)S(1)} %choose.9.refs_1_), channel_id=1, source_target_pairs={{0,4},{1,5},{2,6},{3,7},{4,0},{5,1},{6,2},{7,3},{8,12},{9,13},{10,... | collective-permute-start | bytes 786440 | tf_op jit(solution)/shard_map/two_b/ppermute | solution.py:398
  26.0 0.0 collective-permute-done.6.refs_0_.theirs_ref
  26.0 0.3 collective-permute-done.5.ours_ref.refs_1_
  26.3 1.7 %expert.11.ours_ref.refs_0_ = bf16[32,4096]{1,0:T(8,128)(2,1)S(1)} custom-call(bf16[32,4096]{1,0:T(8,128)(2,1)S(1)} %choose.10.rows_ref.refs_0_, bf16[1,4096,384]{2,1,0:T(8,128)(2,1)S(1)} %copy-done.3, bf16[1,4096,384]{2,1,0:T(8,128)(2,1)S(1)} %copy-done, bf16[1,384,4096]{2,1,0:T(8,128)(2,1)S(1)} %copy-done.1, bf16[32,4096]{1,0:T(8,128)(2,1)S(1)} %choose.10.rows_ref.refs_0_), custom_call_target="tpu_custom_call" | custom-call | flops 301989888 | bytes 9437184 | tf_op jit(solution)/shard_map/expert/pallas_call | solution.py:358
  28.0 3.1 %collective-permute-start.9 = (bf16[32,4096]{1,0:T(8,128)(2,1)S(1)}, bf16[32,4096]{1,0:T(8,128)(2,1)S(1)}, u32[]{:S(2)}, u32[]{:S(2)}) collective-permute-start(bf16[32,4096]{1,0:T(8,128)(2,1)S(1)} %choose.11.refs_4_), channel_id=1, source_target_pairs={{0,4},{1,5},{2,6},{3,7},{4,0},{5,1},{6,2},{7,3},{8,12},{9,13},{10,... | collective-permute-start | bytes 786440 | tf_op jit(solution)/shard_map/three_a/ppermute | solution.py:398
  31.2 0.1 collective-permute-start.12
  31.3 0.8 %collective-permute-done.10.ours_ref.refs_2_ = bf16[32,4096]{1,0:T(8,128)(2,1)S(1)} collective-permute-done((bf16[32,4096]{1,0:T(8,128)(2,1)S(1)}, bf16[32,4096]{1,0:T(8,128)(2,1)S(1)}, u32[]{:S(2)}, u32[]{:S(2)}) %collective-permute-start.10) | collective-permute-done | bytes 262176 | tf_op jit(solution)/shard_map/two_b/ppermute | solution.py:398
  32.1 1.7 %expert.13.ours_ref.refs_0_ = bf16[32,4096]{1,0:T(8,128)(2,1)S(1)} custom-call(bf16[32,4096]{1,0:T(8,128)(2,1)S(1)} %choose.12.rows_ref.refs_0_, bf16[1,4096,384]{2,1,0:T(8,128)(2,1)S(1)} %copy-done.3, bf16[1,4096,384]{2,1,0:T(8,128)(2,1)S(1)} %copy-done, bf16[1,384,4096]{2,1,0:T(8,128)(2,1)S(1)} %copy-done.1, bf16[32,4096]{1,0:T(8,128)(2,1)S(1)} %choose.12.rows_ref.refs_0_), custom_call_target="tpu_custom_call" | custom-call | flops 301989888 | bytes 9437184 | tf_op jit(solution)/shard_map/expert/pallas_call | solution.py:358
  33.8 6.1 %collective-permute-start.15 = (bf16[32,4096]{1,0:T(8,128)(2,1)S(1)}, bf16[32,4096]{1,0:T(8,128)(2,1)S(1)}, u32[]{:S(2)}, u32[]{:S(2)}) collective-permute-start(bf16[32,4096]{1,0:T(8,128)(2,1)S(1)} %choose.13.refs_2_), channel_id=1, source_target_pairs={{0,4},{1,5},{2,6},{3,7},{4,0},{5,1},{6,2},{7,3},{8,12},{9,13},{10,... | collective-permute-start | bytes 786440 | tf_op jit(solution)/shard_map/three_b/ppermute | solution.py:398
  39.9 0.0 collective-permute-done.9.refs_1_.ours_ref
  39.9 0.1 mix.5.refs_0_
  40.0 0.1 collective-permute-start.14
  40.1 1.6 %expert.14.refs_2_.ours_ref.refs_0_ = bf16[32,4096]{1,0:T(8,128)(2,1)S(1)} custom-call(bf16[32,4096]{1,0:T(8,128)(2,1)S(1)} %choose.14.rows_ref.refs_0_, bf16[1,4096,384]{2,1,0:T(8,128)(2,1)S(1)} %copy-done.3, bf16[1,4096,384]{2,1,0:T(8,128)(2,1)S(1)} %copy-done, bf16[1,384,4096]{2,1,0:T(8,128)(2,1)S(1)} %copy-done.1, ...), custom_call_target="tpu_custom_call" | custom-call | flops 301989888 | bytes 9437184 | tf_op jit(solution)/shard_map/expert/pallas_call | solution.py:358
  41.8 0.0 collective-permute-done.12.refs_1_
  41.8 0.1 mix.6.theirs_ref.refs_0_
  41.9 3.9 %collective-permute-start.13 = (bf16[32,4096]{1,0:T(8,128)(2,1)S(1)}, bf16[32,4096]{1,0:T(8,128)(2,1)S(1)}, u32[]{:S(2)}, u32[]{:S(2)}) collective-permute-start(bf16[32,4096]{1,0:T(8,128)(2,1)S(1)} %choose.15.refs_2_), channel_id=1, source_target_pairs={{0,4},{1,5},{2,6},{3,7},{4,0},{5,1},{6,2},{7,3},{8,12},{9,13},{10,... | collective-permute-start | bytes 786440 | tf_op jit(solution)/shard_map/four/ppermute | solution.py:398
  45.8 0.3 collective-permute-done.15.refs_1_.refs_0_
  46.1 0.1 mix.7.refs_4_
  46.2 0.0 copy-start.4
  46.2 0.1 collective-permute-start.17
  46.3 1.8 %expert.15.refs_1_ = bf16[32,4096]{1,0:T(8,128)(2,1)S(1)} custom-call(s32[1]{0:T(128)} %bitcast.3.outer_ref.flag_ref, bf16[32,4096]{1,0:T(8,128)(2,1)S(1)} %collective-permute-done.15.refs_1_.refs_0_, bf16[1,4096,384]{2,1,0:T(8,128)(2,1)S(1)} %copy-done.3, bf16[1,4096,384]{2,1,0:T(8,128)(2,1)S(1)} %copy-done, bf16[1,384,4096]{2,1,0:T(8,128)(2,1)S(1)} %copy-done.1, ...), custom_call_target="tpu_custom_call" | custom-call | flops 301989888 | bytes 9437184 | tf_op jit(solution)/shard_map/expert/pallas_call | solution.py:358
  48.1 0.0 collective-permute-done.14.refs_0_.refs_2_
  48.1 3.1 %collective-permute-done.13.refs_1_.refs_0_ = bf16[32,4096]{1,0:T(8,128)(2,1)S(1)} collective-permute-done((bf16[32,4096]{1,0:T(8,128)(2,1)S(1)}, bf16[32,4096]{1,0:T(8,128)(2,1)S(1)}, u32[]{:S(2)}, u32[]{:S(2)}) %collective-permute-start.13) | collective-permute-done | bytes 262176 | tf_op jit(solution)/shard_map/four/ppermute | solution.py:398
  51.2 0.1 mix.8.refs_4_
  51.3 0.1 collective-permute-start.16
  51.4 1.7 %collective-permute-start.19 = (bf16[32,4096]{1,0:T(8,128)(2,1)S(1)}, bf16[32,4096]{1,0:T(8,128)(2,1)S(1)}, u32[]{:S(2)}, u32[]{:S(2)}) collective-permute-start(bf16[32,4096]{1,0:T(8,128)(2,1)S(1)} %expert.15.refs_1_), channel_id=1, source_target_pairs={{0,12},{1,13},{2,14},{3,15},{4,5},{5,4},{6,7},{7,6},{8,9},{9,8},{1... | collective-permute-start | bytes 786440 | tf_op jit(solution)/shard_map/direct_b/ppermute | solution.py:407
  53.0 2.4 %shares.1.refs_0_.weight_ref = bf16[128,128]{1,0:T(8,128)(2,1)S(1)} custom-call(s32[1]{0:T(128)} %bitcast.me_ref, bf16[128,4096]{1,0:T(8,128)(2,1)} %refs_0_.9, bf16[32,128]{1,0:T(8,128)(2,1)} %bitcast.6, s32[8,128]{1,0:T(8,128)} %bitcast.8, bf16[4096,128]{1,0:T(8,128)(2,1)S(1)} %copy-done.4, bf16[32,4096]{1,0:T(8,128)(2,1)S(1)} %mix.8.refs_4_), custom_call_target="tpu_custom_call" | custom-call | tf_op jit(solution)/shard_map/shares/pallas_call | solution.py:283
  55.4 1.7 %expert.16.refs_0_.own_ref = bf16[32,4096]{1,0:T(8,128)(2,1)S(1)} custom-call(bf16[32,4096]{1,0:T(8,128)(2,1)S(1)} %join.3.refs_0_.rows_ref, bf16[1,4096,384]{2,1,0:T(8,128)(2,1)S(1)} %copy-done.3, bf16[1,4096,384]{2,1,0:T(8,128)(2,1)S(1)} %copy-done, bf16[1,384,4096]{2,1,0:T(8,128)(2,1)S(1)} %copy-done.1, bf16[128,128]{1,0:T(8,128)(2,1)S(1)} %shares.1.refs_0_.weight_ref), custom_call_target="tpu_custom_call" | custom-call | flops 301989888 | bytes 9437184 | tf_op jit(solution)/shard_map/expert/pallas_call | solution.py:358
  57.1 1.7 %expert.17.refs_1_.own_ref = bf16[32,4096]{1,0:T(8,128)(2,1)S(1)} custom-call(bf16[32,4096]{1,0:T(8,128)(2,1)S(1)} %join.2.refs_1_.rows_ref, bf16[1,4096,384]{2,1,0:T(8,128)(2,1)S(1)} %copy-done.3, bf16[1,4096,384]{2,1,0:T(8,128)(2,1)S(1)} %copy-done, bf16[1,384,4096]{2,1,0:T(8,128)(2,1)S(1)} %copy-done.1, bf16[32,4096]{1,0:T(8,128)(2,1)S(1)} %expert.16.refs_0_.own_ref), custom_call_target="tpu_custom_call" | custom-call | flops 301989888 | bytes 9437184 | tf_op jit(solution)/shard_map/expert/pallas_call | solution.py:358
  58.7 0.0 collective-permute-done.17.refs_0_.refs_3_
  58.8 0.0 collective-permute-done.16.refs_1_
  58.8 0.1 mix.9.refs_4_
  58.8 8.2 %collective-permute-start.18 = (bf16[32,4096]{1,0:T(8,128)(2,1)S(1)}, bf16[32,4096]{1,0:T(8,128)(2,1)S(1)}, u32[]{:S(2)}, u32[]{:S(2)}) collective-permute-start(bf16[32,4096]{1,0:T(8,128)(2,1)S(1)} %mix.9.refs_4_), channel_id=1, source_target_pairs={{0,4},{1,5},{2,6},{3,7},{4,0},{5,1},{6,2},{7,3},{8,12},{9,13},{10,... | collective-permute-start | bytes 786440 | tf_op jit(solution)/shard_map/five_a/ppermute | solution.py:398
  67.0 0.0 collective-permute-done.19.refs_1_
  67.0 0.1 finish.2
  67.1 1.6 %collective-permute-start.21 = (bf16[16,4096]{1,0:T(8,128)(2,1)S(1)}, bf16[16,4096]{1,0:T(8,128)(2,1)S(1)}, u32[]{:S(2)}, u32[]{:S(2)}) collective-permute-start(bf16[16,4096]{1,0:T(8,128)(2,1)S(1)} %get-tuple-element.17.refs_3_), channel_id=1, source_target_pairs={{0,2},{1,3},{2,0},{3,1},{4,6},{5,7},{6,4},{7,5},{8,10},{9,11},{10,... | collective-permute-start | bytes 393224 | tf_op jit(solution)/shard_map/plane2/ppermute | solution.py:393
  68.7 3.0 %collective-permute-done.18.refs_0_ = bf16[32,4096]{1,0:T(8,128)(2,1)S(1)} collective-permute-done((bf16[32,4096]{1,0:T(8,128)(2,1)S(1)}, bf16[32,4096]{1,0:T(8,128)(2,1)S(1)}, u32[]{:S(2)}, u32[]{:S(2)}) %collective-permute-start.18) | collective-permute-done | bytes 262176 | tf_op jit(solution)/shard_map/five_a/ppermute | solution.py:398
  71.8 0.1 finish.3
  71.8 0.1 collective-permute-start.20
  71.9 0.7 collective-permute-done.21.refs_2_
  72.6 1.9 %collective-permute-done.22.refs_3_ = bf16[16,4096]{1,0:T(8,128)(2,1)S(1)} collective-permute-done((bf16[16,4096]{1,0:T(8,128)(2,1)S(1)}, bf16[16,4096]{1,0:T(8,128)(2,1)S(1)}, u32[]{:S(2)}, u32[]{:S(2)}) %collective-permute-start.22) | collective-permute-done | bytes 131104 | tf_op jit(solution)/shard_map/plane3/ppermute | solution.py:393
  74.5 1.2 %combine.1 = bf16[128,4096]{1,0:T(8,128)(2,1)} custom-call(bf16[128,128]{1,0:T(8,128)(2,1)S(1)} %shares.1.refs_0_.weight_ref, bf16[16,4096]{1,0:T(8,128)(2,1)S(1)} %get-tuple-element.18.refs_0_, bf16[16,4096]{1,0:T(8,128)(2,1)S(1)} %collective-permute-done.20.refs_1_, bf16[16,4096]{1,0:T(8,128)(2,1)S(1)} %collective-permute-done.21.refs_2_, ...), custom_call_target="tpu_custom_call" | custom-call | tf_op jit(solution)/shard_map/combine/pallas_call | solution.py:374
  (27 shorter events, 0.3 us)
Async XLA Ops:
  0.0 9.1 %copy-start = (bf16[1,4096,384]{2,1,0:T(8,128)(2,1)S(1)}, bf16[1,4096,384]{2,1,0:T(8,128)(2,1)}, u32[]{:S(2)}) copy-start(bf16[1,4096,384]{2,1,0:T(8,128)(2,1)} %up_ref.13) | copy-start | bytes 9437188
  2.1 3.2 %collective-permute-start = (bf16[16,4096]{1,0:T(8,128)(2,1)S(1)}, bf16[16,4096]{1,0:T(8,128)(2,1)S(1)}, u32[]{:S(2)}, u32[]{:S(2)}) collective-permute-start(bf16[16,4096]{1,0:T(8,128)(2,1)S(1)} %get-tuple-element.14), channel_id=1, source_target_pairs={{0,1},{1,0},{2,3},{3,2},{4,5},{5,4},{6,7},{7,6},{8,9},{9,8},{10,11... | collective-permute-start | bytes 393224 | tf_op jit(solution)/shard_map/plane1/ppermute | solution.py:393
  2.6 6.9 %collective-permute-start.2 = (bf16[16,4096]{1,0:T(8,128)(2,1)S(1)}, bf16[16,4096]{1,0:T(8,128)(2,1)S(1)}, u32[]{:S(2)}, u32[]{:S(2)}) collective-permute-start(bf16[16,4096]{1,0:T(8,128)(2,1)S(1)} %get-tuple-element.15), channel_id=1, source_target_pairs={{0,2},{1,3},{2,0},{3,1},{4,6},{5,7},{6,4},{7,5},{8,10},{9,11},{10,... | collective-permute-start | bytes 393224 | tf_op jit(solution)/shard_map/plane2/ppermute | solution.py:393
  5.2 6.6 %collective-permute-start.3 = (bf16[16,4096]{1,0:T(8,128)(2,1)S(1)}, bf16[16,4096]{1,0:T(8,128)(2,1)S(1)}, u32[]{:S(2)}, u32[]{:S(2)}) collective-permute-start(bf16[16,4096]{1,0:T(8,128)(2,1)S(1)} %get-tuple-element.16), channel_id=1, source_target_pairs={{0,3},{1,2},{2,1},{3,0},{4,7},{5,6},{6,5},{7,4},{8,11},{9,10},{10,... | collective-permute-start | bytes 393224 | tf_op jit(solution)/shard_map/plane3/ppermute | solution.py:393
  5.3 3.8 %copy-start.1 = (bf16[1,384,4096]{2,1,0:T(8,128)(2,1)S(1)}, bf16[1,384,4096]{2,1,0:T(8,128)(2,1)}, u32[]{:S(2)}) copy-start(bf16[1,384,4096]{2,1,0:T(8,128)(2,1)} %down_ref.13) | copy-start | bytes 9437188
  5.3 8.7 %collective-permute-start.1 = (bf16[32,4096]{1,0:T(8,128)(2,1)S(1)}, bf16[32,4096]{1,0:T(8,128)(2,1)S(1)}, u32[]{:S(2)}, u32[]{:S(2)}) collective-permute-start(bf16[32,4096]{1,0:T(8,128)(2,1)S(1)} %join.2.refs_1_.rows_ref), channel_id=1, source_target_pairs={{0,4},{1,5},{2,6},{3,7},{4,0},{5,1},{6,2},{7,3},{8,12},{9,13},{10,... | collective-permute-start | bytes 786440 | tf_op jit(solution)/shard_map/near_a/ppermute | solution.py:398
  7.2 8.6 %collective-permute-start.4 = (bf16[32,4096]{1,0:T(8,128)(2,1)S(1)}, bf16[32,4096]{1,0:T(8,128)(2,1)S(1)}, u32[]{:S(2)}, u32[]{:S(2)}) collective-permute-start(bf16[32,4096]{1,0:T(8,128)(2,1)S(1)} %join.2.refs_1_.rows_ref), channel_id=1, source_target_pairs={{0,1},{1,0},{2,3},{3,2},{4,8},{5,9},{6,10},{7,11},{8,4},{9,5},{10,... | collective-permute-start | bytes 786440 | tf_op jit(solution)/shard_map/far_in_a/ppermute | solution.py:407
  7.2 1.9 %copy-start.2 = (bf16[1,4096,384]{2,1,0:T(8,128)(2,1)S(1)}, bf16[1,4096,384]{2,1,0:T(8,128)(2,1)}, u32[]{:S(2)}) copy-start(bf16[1,4096,384]{2,1,0:T(8,128)(2,1)} %gate_ref.13) | copy-start | bytes 9437188
  9.1 4.9 %copy-start.3 = (bf16[1,4096,384]{2,1,0:T(8,128)(2,1)S(1)}, bf16[1,4096,384]{2,1,0:T(8,128)(2,1)}, u32[]{:S(2)}) copy-start(bf16[1,4096,384]{2,1,0:T(8,128)(2,1)} %gate_ref.13) | copy-start | bytes 9437188
  11.9 9.2 %collective-permute-start.7 = (bf16[32,4096]{1,0:T(8,128)(2,1)S(1)}, bf16[32,4096]{1,0:T(8,128)(2,1)S(1)}, u32[]{:S(2)}, u32[]{:S(2)}) collective-permute-start(bf16[32,4096]{1,0:T(8,128)(2,1)S(1)} %join.3.refs_0_.rows_ref), channel_id=1, source_target_pairs={{0,4},{1,5},{2,6},{3,7},{4,0},{5,1},{6,2},{7,3},{8,12},{9,13},{10,... | collective-permute-start | bytes 786440 | tf_op jit(solution)/shard_map/near_b/ppermute | solution.py:398
  13.5 9.2 %collective-permute-start.8 = (bf16[32,4096]{1,0:T(8,128)(2,1)S(1)}, bf16[32,4096]{1,0:T(8,128)(2,1)S(1)}, u32[]{:S(2)}, u32[]{:S(2)}) collective-permute-start(bf16[32,4096]{1,0:T(8,128)(2,1)S(1)} %join.3.refs_0_.rows_ref), channel_id=1, source_target_pairs={{0,1},{1,0},{2,3},{3,2},{4,8},{5,9},{6,10},{7,11},{8,4},{9,5},{10,... | collective-permute-start | bytes 786440 | tf_op jit(solution)/shard_map/far_in_b/ppermute | solution.py:407
  15.6 10.4 %collective-permute-start.6 = (bf16[32,4096]{1,0:T(8,128)(2,1)S(1)}, bf16[32,4096]{1,0:T(8,128)(2,1)S(1)}, u32[]{:S(2)}, u32[]{:S(2)}) collective-permute-start(bf16[32,4096]{1,0:T(8,128)(2,1)S(1)} %collective-permute-done.1.rows_ref), channel_id=1, source_target_pairs={{0,1},{1,0},{2,3},{3,2},{4,8},{5,9},{6,10},{7,11},{8,4},{9,5},{10,... | collective-permute-start | bytes 786440 | tf_op jit(solution)/shard_map/last_in_a/ppermute | solution.py:407
  15.8 10.5 %collective-permute-start.5 = (bf16[32,4096]{1,0:T(8,128)(2,1)S(1)}, bf16[32,4096]{1,0:T(8,128)(2,1)S(1)}, u32[]{:S(2)}, u32[]{:S(2)}) collective-permute-start(bf16[32,4096]{1,0:T(8,128)(2,1)S(1)} %choose.8.refs_0_), channel_id=1, source_target_pairs={{0,4},{1,5},{2,6},{3,7},{4,0},{5,1},{6,2},{7,3},{8,12},{9,13},{10,... | collective-permute-start | bytes 786440 | tf_op jit(solution)/shard_map/two_a/ppermute | solution.py:398
  21.1 10.1 %collective-permute-start.11 = (bf16[32,4096]{1,0:T(8,128)(2,1)S(1)}, bf16[32,4096]{1,0:T(8,128)(2,1)S(1)}, u32[]{:S(2)}, u32[]{:S(2)}) collective-permute-start(bf16[32,4096]{1,0:T(8,128)(2,1)S(1)} %collective-permute-done.7.rows_ref), channel_id=1, source_target_pairs={{0,1},{1,0},{2,3},{3,2},{4,8},{5,9},{6,10},{7,11},{8,4},{9,5},{10,... | collective-permute-start | bytes 786440 | tf_op jit(solution)/shard_map/last_in_b/ppermute | solution.py:407
  22.8 9.3 %collective-permute-start.10 = (bf16[32,4096]{1,0:T(8,128)(2,1)S(1)}, bf16[32,4096]{1,0:T(8,128)(2,1)S(1)}, u32[]{:S(2)}, u32[]{:S(2)}) collective-permute-start(bf16[32,4096]{1,0:T(8,128)(2,1)S(1)} %choose.9.refs_1_), channel_id=1, source_target_pairs={{0,4},{1,5},{2,6},{3,7},{4,0},{5,1},{6,2},{7,3},{8,12},{9,13},{10,... | collective-permute-start | bytes 786440 | tf_op jit(solution)/shard_map/two_b/ppermute | solution.py:398
  28.0 11.9 %collective-permute-start.9 = (bf16[32,4096]{1,0:T(8,128)(2,1)S(1)}, bf16[32,4096]{1,0:T(8,128)(2,1)S(1)}, u32[]{:S(2)}, u32[]{:S(2)}) collective-permute-start(bf16[32,4096]{1,0:T(8,128)(2,1)S(1)} %choose.11.refs_4_), channel_id=1, source_target_pairs={{0,4},{1,5},{2,6},{3,7},{4,0},{5,1},{6,2},{7,3},{8,12},{9,13},{10,... | collective-permute-start | bytes 786440 | tf_op jit(solution)/shard_map/three_a/ppermute | solution.py:398
  31.2 10.6 %collective-permute-start.12 = (bf16[32,4096]{1,0:T(8,128)(2,1)S(1)}, bf16[32,4096]{1,0:T(8,128)(2,1)S(1)}, u32[]{:S(2)}, u32[]{:S(2)}) collective-permute-start(bf16[32,4096]{1,0:T(8,128)(2,1)S(1)} %expert.12.refs_0_), channel_id=1, source_target_pairs={{0,1},{1,0},{2,3},{3,2},{4,8},{5,9},{6,10},{7,11},{8,4},{9,5},{10,... | collective-permute-start | bytes 786440 | tf_op jit(solution)/shard_map/across_b/ppermute | solution.py:407
  33.8 12.3 %collective-permute-start.15 = (bf16[32,4096]{1,0:T(8,128)(2,1)S(1)}, bf16[32,4096]{1,0:T(8,128)(2,1)S(1)}, u32[]{:S(2)}, u32[]{:S(2)}) collective-permute-start(bf16[32,4096]{1,0:T(8,128)(2,1)S(1)} %choose.13.refs_2_), channel_id=1, source_target_pairs={{0,4},{1,5},{2,6},{3,7},{4,0},{5,1},{6,2},{7,3},{8,12},{9,13},{10,... | collective-permute-start | bytes 786440 | tf_op jit(solution)/shard_map/three_b/ppermute | solution.py:398
  40.0 8.1 %collective-permute-start.14 = (bf16[32,4096]{1,0:T(8,128)(2,1)S(1)}, bf16[32,4096]{1,0:T(8,128)(2,1)S(1)}, u32[]{:S(2)}, u32[]{:S(2)}) collective-permute-start(bf16[32,4096]{1,0:T(8,128)(2,1)S(1)} %mix.5.refs_0_), channel_id=1, source_target_pairs={{0,1},{1,0},{2,3},{3,2},{4,8},{5,9},{6,10},{7,11},{8,4},{9,5},{10,... | collective-permute-start | bytes 786440 | tf_op jit(solution)/shard_map/mid_a/ppermute | solution.py:407
  41.9 9.3 %collective-permute-start.13 = (bf16[32,4096]{1,0:T(8,128)(2,1)S(1)}, bf16[32,4096]{1,0:T(8,128)(2,1)S(1)}, u32[]{:S(2)}, u32[]{:S(2)}) collective-permute-start(bf16[32,4096]{1,0:T(8,128)(2,1)S(1)} %choose.15.refs_2_), channel_id=1, source_target_pairs={{0,4},{1,5},{2,6},{3,7},{4,0},{5,1},{6,2},{7,3},{8,12},{9,13},{10,... | collective-permute-start | bytes 786440 | tf_op jit(solution)/shard_map/four/ppermute | solution.py:398
  46.2 6.9 %copy-start.4 = (bf16[4096,128]{1,0:T(8,128)(2,1)S(1)}, bf16[4096,128]{1,0:T(8,128)(2,1)}, u32[]{:S(2)}) copy-start(bf16[4096,128]{1,0:T(8,128)(2,1)} %refs_3_.5) | copy-start | bytes 3145732
  46.2 12.6 %collective-permute-start.17 = (bf16[32,4096]{1,0:T(8,128)(2,1)S(1)}, bf16[32,4096]{1,0:T(8,128)(2,1)S(1)}, u32[]{:S(2)}, u32[]{:S(2)}) collective-permute-start(bf16[32,4096]{1,0:T(8,128)(2,1)S(1)} %mix.7.refs_4_), channel_id=1, source_target_pairs={{0,1},{1,0},{2,3},{3,2},{4,8},{5,9},{6,10},{7,11},{8,4},{9,5},{10,... | collective-permute-start | bytes 786440 | tf_op jit(solution)/shard_map/mid_b/ppermute | solution.py:407
  51.3 7.5 %collective-permute-start.16 = (bf16[32,4096]{1,0:T(8,128)(2,1)S(1)}, bf16[32,4096]{1,0:T(8,128)(2,1)S(1)}, u32[]{:S(2)}, u32[]{:S(2)}) collective-permute-start(bf16[32,4096]{1,0:T(8,128)(2,1)S(1)} %mix.8.refs_4_), channel_id=1, source_target_pairs={{0,1},{1,0},{2,3},{3,2},{4,8},{5,9},{6,10},{7,11},{8,4},{9,5},{10,... | collective-permute-start | bytes 786440 | tf_op jit(solution)/shard_map/mid2_a/ppermute | solution.py:407
  51.4 15.6 %collective-permute-start.19 = (bf16[32,4096]{1,0:T(8,128)(2,1)S(1)}, bf16[32,4096]{1,0:T(8,128)(2,1)S(1)}, u32[]{:S(2)}, u32[]{:S(2)}) collective-permute-start(bf16[32,4096]{1,0:T(8,128)(2,1)S(1)} %expert.15.refs_1_), channel_id=1, source_target_pairs={{0,12},{1,13},{2,14},{3,15},{4,5},{5,4},{6,7},{7,6},{8,9},{9,8},{1... | collective-permute-start | bytes 786440 | tf_op jit(solution)/shard_map/direct_b/ppermute | solution.py:407
  58.8 12.9 %collective-permute-start.18 = (bf16[32,4096]{1,0:T(8,128)(2,1)S(1)}, bf16[32,4096]{1,0:T(8,128)(2,1)S(1)}, u32[]{:S(2)}, u32[]{:S(2)}) collective-permute-start(bf16[32,4096]{1,0:T(8,128)(2,1)S(1)} %mix.9.refs_4_), channel_id=1, source_target_pairs={{0,4},{1,5},{2,6},{3,7},{4,0},{5,1},{6,2},{7,3},{8,12},{9,13},{10,... | collective-permute-start | bytes 786440 | tf_op jit(solution)/shard_map/five_a/ppermute | solution.py:398
  67.1 5.5 %collective-permute-start.21 = (bf16[16,4096]{1,0:T(8,128)(2,1)S(1)}, bf16[16,4096]{1,0:T(8,128)(2,1)S(1)}, u32[]{:S(2)}, u32[]{:S(2)}) collective-permute-start(bf16[16,4096]{1,0:T(8,128)(2,1)S(1)} %get-tuple-element.17.refs_3_), channel_id=1, source_target_pairs={{0,2},{1,3},{2,0},{3,1},{4,6},{5,7},{6,4},{7,5},{8,10},{9,11},{10,... | collective-permute-start | bytes 393224 | tf_op jit(solution)/shard_map/plane2/ppermute | solution.py:393
  68.7 5.8 %collective-permute-start.22 = (bf16[16,4096]{1,0:T(8,128)(2,1)S(1)}, bf16[16,4096]{1,0:T(8,128)(2,1)S(1)}, u32[]{:S(2)}, u32[]{:S(2)}) collective-permute-start(bf16[16,4096]{1,0:T(8,128)(2,1)S(1)} %get-tuple-element.20), channel_id=1, source_target_pairs={{0,3},{1,2},{2,1},{3,0},{4,7},{5,6},{6,5},{7,4},{8,11},{9,10},{10,... | collective-permute-start | bytes 393224 | tf_op jit(solution)/shard_map/plane3/ppermute | solution.py:393
  71.8 2.7 %collective-permute-start.20 = (bf16[16,4096]{1,0:T(8,128)(2,1)S(1)}, bf16[16,4096]{1,0:T(8,128)(2,1)S(1)}, u32[]{:S(2)}, u32[]{:S(2)}) collective-permute-start(bf16[16,4096]{1,0:T(8,128)(2,1)S(1)} %get-tuple-element.19), channel_id=1, source_target_pairs={{0,1},{1,0},{2,3},{3,2},{4,5},{5,4},{6,7},{7,6},{8,9},{9,8},{10,11... | collective-permute-start | bytes 393224 | tf_op jit(solution)/shard_map/plane1/ppermute | solution.py:393

commit v4 on v3

--- a/solution.py
+++ b/solution.py
@@ -83,8 +83,8 @@
 
 
 def dispatch_kernel(flight, me_ref, outer_ref, inner_ref, *refs):
-    out_refs = refs[3 : 3 + flight]
-    hidden_ref, gain_ref, ids_ref, sems = refs[3 + flight :]
+    out_refs = refs[3:-4]
+    hidden_ref, gain_ref, ids_ref, sems = refs[-4:]
     fetch(refs[:3], (hidden_ref, gain_ref, ids_ref), sems)
     width = hidden_ref.shape[1]
     piece = min(width, PIECE)
@@ -263,17 +263,20 @@
     return pltpu.CompilerParams(vmem_limit_bytes=limit)
 
 
+def cost(flops, moved):
+    return pl.CostEstimate(flops=flops, bytes_accessed=moved, transcendentals=0)
+
+
 def dispatch(scalars, hidden, gain, ids, flight):
-    shape = jax.ShapeDtypeStruct((CAP, hidden.shape[1]), jnp.bfloat16)
     return pl.pallas_call(
         functools.partial(dispatch_kernel, flight),
-        out_shape=[shape] * flight,
+        out_shape=[jax.ShapeDtypeStruct((CAP, hidden.shape[1]), jnp.bfloat16)] * flight,
         in_specs=smem(len(scalars)) + anywhere(3),
         out_specs=vmem(flight),
         scratch_shapes=[pltpu.VMEM(x.shape, x.dtype) for x in (hidden, gain, ids)]
         + [pltpu.SemaphoreType.DMA((3,))],
         compiler_params=params(),
-        cost_estimate=pl.CostEstimate(flops=1 << 17, bytes_accessed=128, transcendentals=0),
+        cost_estimate=cost(hidden.size // 4, 128),
         name="dispatch",
     )(*scalars, hidden, gain, ids)
 
@@ -288,6 +291,9 @@
         scratch_shapes=[pltpu.VMEM(x.shape, x.dtype) for x in (hidden, gain, ids, router)]
         + [pltpu.SemaphoreType.DMA((4,))],
         compiler_params=params(),
+        cost_estimate=cost(
+            2 * hidden.size * router.shape[1], 2 * (hidden.size + router.size)
+        ),
         name="shares",
     )(me, hidden, gain, ids, router, *after)
 
@@ -318,7 +324,7 @@
 
 def finish_kernel(count, flag_ref, own_ref, *refs):
     ours, theirs = refs[: count[0]], refs[count[0] : count[1]]
-    out_refs = refs[count[1] + count[2] :]
+    out_refs = refs[count[2] :]
     depth = out_refs[0].shape[0]
 
     def add(others):
@@ -339,20 +345,18 @@
 
 def finish(flag, own, ours, theirs, pieces, after=()):
     rows, width = own.shape
-    shape = jax.ShapeDtypeStruct((rows // pieces, width), jnp.bfloat16)
-    return pl.pallas_call(
-        functools.partial(
-            finish_kernel, (len(ours), len(ours) + len(theirs), len(after))
-        ),
-        out_shape=[shape] * pieces,
-        in_specs=smem(1) + vmem(1 + len(ours) + len(theirs)) + anywhere(len(after)),
+    count = [len(ours), len(ours) + len(theirs), len(ours) + len(theirs) + len(after)]
+    return pl.pallas_call(
+        functools.partial(finish_kernel, count),
+        out_shape=[jax.ShapeDtypeStruct((rows // pieces, width), jnp.bfloat16)] * pieces,
+        in_specs=smem(1) + vmem(1 + count[1]) + anywhere(len(after)),
         out_specs=vmem(pieces),
         compiler_params=params(),
         name="finish",
     )(flag, own, *ours, *theirs, *after)
 
 
-def expert(name, flag, rows, gate_weight, up_weight, down_weight, after=()):
+def expert(flag, rows, gate_weight, up_weight, down_weight, after=()):
     count = gate_weight.size + up_weight.size + down_weight.size
     flags = [] if flag is None else [flag]
     return pl.pallas_call(
@@ -361,10 +365,8 @@
         in_specs=smem(len(flags)) + vmem(4) + anywhere(len(after)),
         out_specs=vmem(1)[0],
         compiler_params=params(),
-        cost_estimate=pl.CostEstimate(
-            flops=2 * rows.shape[0] * count, bytes_accessed=2 * count, transcendentals=0
-        ),
-        name=name,
+        cost_estimate=cost(2 * rows.shape[0] * count, 2 * count),
+        name="expert",
     )(*flags, rows, gate_weight, up_weight, down_weight, *after)
 
 
@@ -404,6 +406,12 @@
         for m in range(SPLIT)
         for e in range(flight)
     ]
+    return lax.ppermute(rows, "expert", pairs)
+
+
+def inward_shift(rows, flight, near):
+    to = {1: 0, 2: 3, 0: 1, 3: 2} if near else {1: 3, 2: 0}
+    pairs = [(m * flight + e, to[m] * flight + e) for m in to for e in range(flight)]
     return lax.ppermute(rows, "expert", pairs)
 
 
@@ -425,9 +433,7 @@
         return value
 
     def partial(rows, flag=None):
-        return then(
-            expert("expert", flag, rows, gate_weight, up_weight, down_weight, tuple(tick))
-        )
+        return then(expert(flag, rows, gate_weight, up_weight, down_weight, tuple(tick)))
 
     def pick(ours, theirs):
         return then(choose(at_outer, ours, theirs, tuple(tick)))
@@ -445,6 +451,10 @@
     def middle(name, rows, members=(1, 2)):
         with jax.named_scope(name):
             return mirror_pair(rows, flight, members)
+
+    def inward(name, rows, near):
+        with jax.named_scope(name):
+            return inward_shift(rows, flight, near)
 
     hidden, gain, ids = (
         pltpu.with_memory_space_constraint(x, pltpu.HBM) for x in (hidden, gain, ids)
@@ -471,20 +481,19 @@
     three_b = end("three_b", pick(far_part_b, last_in_b))
     mid_a = middle("mid_a", total(far_part_a, three_a))
     last_part_a = partial(pick(three_a, last_in_a))
-    four = end("four", pick(last_part_a, total(near_part_b, across_b)))
+    seen(across_b)
+    four = end("four", pick(last_part_a, near_part_a))
     mid_b = middle("mid_b", total(far_part_b, three_b))
     direct_b = middle("direct_b", partial(three_b, at_outer), (0, 3))
+    sum_b = inward("sum_b", total(near_part_b, across_b), True)
     seen(mid_a)
-    mid2_a = middle("mid2_a", total(last_part_a, four))
+    across_a = inward("across_a", total(last_part_a, four), False)
     weight = then(shares(me, hidden, gain, ids, router_weight, flight, *tick))
     own_part_b, own_part_a = partial(own_b), partial(own_a)
-    seen(mid_b)
-    five_a = end("five_a", total(near_part_a, mid2_a))
-    done_b = then(
-        finish(at_outer, own_part_b, [four, direct_b], [two_b, mid_b], flight - half, tuple(tick))
-    )
-    done_a = then(finish(at_outer, own_part_a, [five_a], [two_a, mid_a], half, tuple(tick)))
-    back = [in_plane(rows, k, flight) for k, rows in enumerate(list(done_a) + list(done_b))]
+    done_b = then(finish(at_outer, own_part_b, [sum_b, direct_b], [two_b, mid_b], half, tuple(tick)))
+    done_a = then(finish(at_outer, own_part_a, [four, across_a], [two_a, mid_a], half, tuple(tick)))
+    done = list(done_a) + list(done_b)
+    back = [in_plane(rows, k, flight) for k, rows in enumerate(done)]
     return combine(weight, back)
 
 

time: 76 us -> 72.8 us (0.958)
  starting transfers between devices: 38.6 us -> 32.5 us
  waiting for transfers between devices: 15.1 us -> 18.1 us
    ppermute x8 -> x7, starting transfers between devices: 31.3 us -> 23.1 us  [end_pair(): return lax.ppermute(rows, 'expert', pairs)]
    ppermute x0 -> x2, waiting for transfers between devices: none -> 3.99 us  [inward_shift(): return lax.ppermute(rows, 'expert', pairs)]
    ppermute x9 -> x8, waiting for transfers between devices: 0.04 us -> 3.59 us  [mirror_pair(): return lax.ppermute(rows, 'expert', pairs)]
    ppermute x8 -> x7, waiting for transfers between devices: 9.74 us -> 6.26 us  [end_pair(): return lax.ppermute(rows, 'expert', pairs)]
    ppermute x0 -> x2, starting transfers between devices: none -> 2.34 us  [inward_shift(): return lax.ppermute(rows, 'expert', pairs)]
    ppermute x6, waiting for transfers between devices: 5.28 us -> 4.3 us  [in_plane(): return lax.ppermute(rows, 'expert', pairs)]
    ppermute x9 -> x8, starting transfers between devices: 2.43 us -> 2.14 us  [mirror_pair(): return lax.ppermute(rows, 'expert', pairs)]
  transfers between devices with their start and end apart: 23 -> 23, of which waited for: 11 -> 11; matrix products, arithmetic and copies ran while one was open for 0% -> 0% of each run, Pallas kernels for 22% -> 23%
where the time goes in v4:
time: 72.8 us; the launch traced here: 72.6 us
  starting transfers between devices  32.5 us (45%)
  Pallas kernels  19.7 us (27%)
  waiting for transfers between devices  18.1 us (25%)
  local copies, waits for them, and re-layouts  1.91 us (3%)
    ppermute x7, starting transfers between devices, end_pair(): return lax.ppermute(rows, 'expert', pairs)  23.1 us
    pallas_call x9, Pallas kernels, expert(): pl.pallas_call(expert_kernel if flag is None else expert_if_kernel, out_s...  13.3 us
    ppermute x7, waiting for transfers between devices, end_pair(): return lax.ppermute(rows, 'expert', pairs)  6.26 us
    ppermute x6, starting transfers between devices, in_plane(): return lax.ppermute(rows, 'expert', pairs)  4.84 us
    ppermute x6, waiting for transfers between devices, in_plane(): return lax.ppermute(rows, 'expert', pairs)  4.3 us
    ppermute x2, waiting for transfers between devices, inward_shift(): return lax.ppermute(rows, 'expert', pairs)  3.99 us
    ppermute x8, waiting for transfers between devices, mirror_pair(): return lax.ppermute(rows, 'expert', pairs)  3.59 us
    pallas_call x1, Pallas kernels, shares(): pl.pallas_call(functools.partial(shares_kernel, flight), out_shape=jax.Sh...  2.4 us
  transfers between devices with their start and end apart: 23, of which 11 were waited for; matrix products, arithmetic and copies ran while one was open for 0% of the time, Pallas kernels for 23%

profile of v4, /device:TPU:0, one launch (start us, length us, event | category | flops | bytes accessed | tf_op | source)
XLA Modules:
  0.0 72.6 jit_solution(7684449533248791193)
XLA Ops:
  0.0 2.1 %dispatch.1 = (bf16[16,4096]{1,0:T(8,128)(2,1)S(1)}, bf16[16,4096]{1,0:T(8,128)(2,1)S(1)}, bf16[16,4096]{1,0:T(8,128)(2,1)S(1)}, bf16[16,4096]{1,0:T(8,128)(2,1)S(1)}) custom-call(s32[1]{0:T(128)} %bitcast.me_ref, s32[1]{0:T(128)} %bitcast.3.outer_ref.flag_ref, s32[1]{0:T(128)} %bitcast.4.inner_ref.flag_ref, bf16[128,4096]{1,0:T(8,128)(2,1)} %refs_0_.9, ...), custom_call_target="tpu_custom_call" | custom-call | flops 131072 | bytes 128 | tf_op jit(solution)/shard_map/dispatch/pallas_call | solution.py:271
  2.1 0.5 collective-permute-start
  2.6 2.6 %collective-permute-start.2 = (bf16[16,4096]{1,0:T(8,128)(2,1)S(1)}, bf16[16,4096]{1,0:T(8,128)(2,1)S(1)}, u32[]{:S(2)}, u32[]{:S(2)}) collective-permute-start(bf16[16,4096]{1,0:T(8,128)(2,1)S(1)} %get-tuple-element.15), channel_id=1, source_target_pairs={{0,2},{1,3},{2,0},{3,1},{4,6},{5,7},{6,4},{7,5},{8,10},{9,11},{10,... | collective-permute-start | bytes 393224 | tf_op jit(solution)/shard_map/plane2/ppermute | solution.py:395
  5.2 0.1 collective-permute-start.3
  5.3 0.0 collective-permute-done.refs_1_
  5.3 0.0 copy-start.1
  5.3 1.8 %collective-permute-start.1 = (bf16[32,4096]{1,0:T(8,128)(2,1)S(1)}, bf16[32,4096]{1,0:T(8,128)(2,1)S(1)}, u32[]{:S(2)}, u32[]{:S(2)}) collective-permute-start(bf16[32,4096]{1,0:T(8,128)(2,1)S(1)} %join.2.refs_1_.rows_ref), channel_id=1, source_target_pairs={{0,4},{1,5},{2,6},{3,7},{4,0},{5,1},{6,2},{7,3},{8,12},{9,13},{10,... | collective-permute-start | bytes 786440 | tf_op jit(solution)/shard_map/near_a/ppermute | solution.py:400
  7.2 0.1 collective-permute-start.4
  7.2 1.9 %copy-done.2 = bf16[1,4096,384]{2,1,0:T(8,128)(2,1)S(1)} copy-done((bf16[1,4096,384]{2,1,0:T(8,128)(2,1)S(1)}, bf16[1,4096,384]{2,1,0:T(8,128)(2,1)}, u32[]{:S(2)}) %copy-start.2) | copy-done | bytes 3145752
  9.1 0.4 collective-permute-done.2.refs_0_
  9.6 2.3 %collective-permute-done.3.refs_1_ = bf16[16,4096]{1,0:T(8,128)(2,1)S(1)} collective-permute-done((bf16[16,4096]{1,0:T(8,128)(2,1)S(1)}, bf16[16,4096]{1,0:T(8,128)(2,1)S(1)}, u32[]{:S(2)}, u32[]{:S(2)}) %collective-permute-start.3) | collective-permute-done | bytes 131104 | tf_op jit(solution)/shard_map/plane3/ppermute | solution.py:395
  11.9 1.7 %collective-permute-start.7 = (bf16[32,4096]{1,0:T(8,128)(2,1)S(1)}, bf16[32,4096]{1,0:T(8,128)(2,1)S(1)}, u32[]{:S(2)}, u32[]{:S(2)}) collective-permute-start(bf16[32,4096]{1,0:T(8,128)(2,1)S(1)} %join.3.refs_0_.rows_ref), channel_id=1, source_target_pairs={{0,4},{1,5},{2,6},{3,7},{4,0},{5,1},{6,2},{7,3},{8,12},{9,13},{10,... | collective-permute-start | bytes 786440 | tf_op jit(solution)/shard_map/near_b/ppermute | solution.py:400
  13.5 0.3 collective-permute-start.8
  13.8 0.1 collective-permute-done.1.rows_ref
  14.0 1.7 %expert.9.ours_ref.refs_0_.theirs_ref = bf16[32,4096]{1,0:T(8,128)(2,1)S(1)} custom-call(bf16[32,4096]{1,0:T(8,128)(2,1)S(1)} %collective-permute-done.1.rows_ref, bf16[1,4096,384]{2,1,0:T(8,128)(2,1)S(1)} %copy-done.3, bf16[1,4096,384]{2,1,0:T(8,128)(2,1)S(1)} %copy-done, bf16[1,384,4096]{2,1,0:T(8,128)(2,1)S(1)} %copy-done.1, ...), custom_call_target="tpu_custom_call" | custom-call | flops 301989888 | bytes 9437184 | tf_op jit(solution)/shard_map/expert/pallas_call | solution.py:362
  15.6 0.1 collective-permute-start.6
  15.8 0.0 collective-permute-done.4.theirs_ref
  15.8 3.3 %collective-permute-start.5 = (bf16[32,4096]{1,0:T(8,128)(2,1)S(1)}, bf16[32,4096]{1,0:T(8,128)(2,1)S(1)}, u32[]{:S(2)}, u32[]{:S(2)}) collective-permute-start(bf16[32,4096]{1,0:T(8,128)(2,1)S(1)} %choose.8.refs_0_), channel_id=1, source_target_pairs={{0,4},{1,5},{2,6},{3,7},{4,0},{5,1},{6,2},{7,3},{8,12},{9,13},{10,... | collective-permute-start | bytes 786440 | tf_op jit(solution)/shard_map/two_a/ppermute | solution.py:400
  19.1 2.0 %collective-permute-done.7.rows_ref = bf16[32,4096]{1,0:T(8,128)(2,1)S(1)} collective-permute-done((bf16[32,4096]{1,0:T(8,128)(2,1)S(1)}, bf16[32,4096]{1,0:T(8,128)(2,1)S(1)}, u32[]{:S(2)}, u32[]{:S(2)}) %collective-permute-start.7) | collective-permute-done | bytes 262176 | tf_op jit(solution)/shard_map/near_b/ppermute | solution.py:400
  21.1 0.0 collective-permute-start.11
  21.1 1.7 %expert.10.ours_ref.refs_0_ = bf16[32,4096]{1,0:T(8,128)(2,1)S(1)} custom-call(bf16[32,4096]{1,0:T(8,128)(2,1)S(1)} %collective-permute-done.7.rows_ref, bf16[1,4096,384]{2,1,0:T(8,128)(2,1)S(1)} %copy-done.3, bf16[1,4096,384]{2,1,0:T(8,128)(2,1)S(1)} %copy-done, bf16[1,384,4096]{2,1,0:T(8,128)(2,1)S(1)} %copy-done.1, bf16[32,4096]{1,0:T(8,128)(2,1)S(1)} %choose.8.refs_0_), custom_call_target="tpu_custom_call" | custom-call | flops 301989888 | bytes 9437184 | tf_op jit(solution)/shard_map/expert/pallas_call | solution.py:362
  22.7 0.0 collective-permute-done.8.theirs_ref
  22.8 3.2 %collective-permute-start.10 = (bf16[32,4096]{1,0:T(8,128)(2,1)S(1)}, bf16[32,4096]{1,0:T(8,128)(2,1)S(1)}, u32[]{:S(2)}, u32[]{:S(2)}) collective-permute-start(bf16[32,4096]{1,0:T(8,128)(2,1)S(1)} %choose.9.refs_1_), channel_id=1, source_target_pairs={{0,4},{1,5},{2,6},{3,7},{4,0},{5,1},{6,2},{7,3},{8,12},{9,13},{10,... | collective-permute-start | bytes 786440 | tf_op jit(solution)/shard_map/two_b/ppermute | solution.py:400
  26.0 0.0 collective-permute-done.6.refs_0_.theirs_ref
  26.0 0.3 collective-permute-done.5.ours_ref.refs_2_
  26.3 1.7 %expert.11.ours_ref.refs_0_ = bf16[32,4096]{1,0:T(8,128)(2,1)S(1)} custom-call(bf16[32,4096]{1,0:T(8,128)(2,1)S(1)} %choose.10.rows_ref.refs_0_, bf16[1,4096,384]{2,1,0:T(8,128)(2,1)S(1)} %copy-done.3, bf16[1,4096,384]{2,1,0:T(8,128)(2,1)S(1)} %copy-done, bf16[1,384,4096]{2,1,0:T(8,128)(2,1)S(1)} %copy-done.1, bf16[32,4096]{1,0:T(8,128)(2,1)S(1)} %choose.10.rows_ref.refs_0_), custom_call_target="tpu_custom_call" | custom-call | flops 301989888 | bytes 9437184 | tf_op jit(solution)/shard_map/expert/pallas_call | solution.py:362
  28.0 3.1 %collective-permute-start.9 = (bf16[32,4096]{1,0:T(8,128)(2,1)S(1)}, bf16[32,4096]{1,0:T(8,128)(2,1)S(1)}, u32[]{:S(2)}, u32[]{:S(2)}) collective-permute-start(bf16[32,4096]{1,0:T(8,128)(2,1)S(1)} %choose.11.refs_4_), channel_id=1, source_target_pairs={{0,4},{1,5},{2,6},{3,7},{4,0},{5,1},{6,2},{7,3},{8,12},{9,13},{10,... | collective-permute-start | bytes 786440 | tf_op jit(solution)/shard_map/three_a/ppermute | solution.py:400
  31.2 0.0 collective-permute-done.11.refs_0_.theirs_ref
  31.2 0.1 collective-permute-start.12
  31.3 0.8 %collective-permute-done.10.ours_ref.refs_2_ = bf16[32,4096]{1,0:T(8,128)(2,1)S(1)} collective-permute-done((bf16[32,4096]{1,0:T(8,128)(2,1)S(1)}, bf16[32,4096]{1,0:T(8,128)(2,1)S(1)}, u32[]{:S(2)}, u32[]{:S(2)}) %collective-permute-start.10) | collective-permute-done | bytes 262176 | tf_op jit(solution)/shard_map/two_b/ppermute | solution.py:400
  32.1 1.7 %expert.13.ours_ref.refs_0_ = bf16[32,4096]{1,0:T(8,128)(2,1)S(1)} custom-call(bf16[32,4096]{1,0:T(8,128)(2,1)S(1)} %choose.12.rows_ref.refs_0_, bf16[1,4096,384]{2,1,0:T(8,128)(2,1)S(1)} %copy-done.3, bf16[1,4096,384]{2,1,0:T(8,128)(2,1)S(1)} %copy-done, bf16[1,384,4096]{2,1,0:T(8,128)(2,1)S(1)} %copy-done.1, bf16[32,4096]{1,0:T(8,128)(2,1)S(1)} %choose.12.rows_ref.refs_0_), custom_call_target="tpu_custom_call" | custom-call | flops 301989888 | bytes 9437184 | tf_op jit(solution)/shard_map/expert/pallas_call | solution.py:362
  33.8 6.1 %collective-permute-start.15 = (bf16[32,4096]{1,0:T(8,128)(2,1)S(1)}, bf16[32,4096]{1,0:T(8,128)(2,1)S(1)}, u32[]{:S(2)}, u32[]{:S(2)}) collective-permute-start(bf16[32,4096]{1,0:T(8,128)(2,1)S(1)} %choose.13.refs_2_), channel_id=1, source_target_pairs={{0,4},{1,5},{2,6},{3,7},{4,0},{5,1},{6,2},{7,3},{8,12},{9,13},{10,... | collective-permute-start | bytes 786440 | tf_op jit(solution)/shard_map/three_b/ppermute | solution.py:400
  39.9 0.1 mix.4.refs_0_
  40.0 0.1 collective-permute-start.14
  40.1 1.6 %expert.14.refs_1_.ours_ref.refs_0_ = bf16[32,4096]{1,0:T(8,128)(2,1)S(1)} custom-call(bf16[32,4096]{1,0:T(8,128)(2,1)S(1)} %choose.14.rows_ref.refs_0_, bf16[1,4096,384]{2,1,0:T(8,128)(2,1)S(1)} %copy-done.3, bf16[1,4096,384]{2,1,0:T(8,128)(2,1)S(1)} %copy-done, bf16[1,384,4096]{2,1,0:T(8,128)(2,1)S(1)} %copy-done.1, ...), custom_call_target="tpu_custom_call" | custom-call | flops 301989888 | bytes 9437184 | tf_op jit(solution)/shard_map/expert/pallas_call | solution.py:362
  41.7 0.0 collective-permute-done.12.refs_0_.refs_1_
  41.8 3.9 %collective-permute-start.13 = (bf16[32,4096]{1,0:T(8,128)(2,1)S(1)}, bf16[32,4096]{1,0:T(8,128)(2,1)S(1)}, u32[]{:S(2)}, u32[]{:S(2)}) collective-permute-start(bf16[32,4096]{1,0:T(8,128)(2,1)S(1)} %choose.15.refs_2_), channel_id=1, source_target_pairs={{0,4},{1,5},{2,6},{3,7},{4,0},{5,1},{6,2},{7,3},{8,12},{9,13},{10,... | collective-permute-start | bytes 786440 | tf_op jit(solution)/shard_map/four/ppermute | solution.py:400
  45.7 0.5 collective-permute-done.15.refs_1_.refs_0_
  46.1 0.1 mix.5.refs_4_
  46.2 0.0 copy-start.4
  46.2 1.7 %expert.15.refs_2_ = bf16[32,4096]{1,0:T(8,128)(2,1)S(1)} custom-call(s32[1]{0:T(128)} %bitcast.3.outer_ref.flag_ref, bf16[32,4096]{1,0:T(8,128)(2,1)S(1)} %collective-permute-done.15.refs_1_.refs_0_, bf16[1,4096,384]{2,1,0:T(8,128)(2,1)S(1)} %copy-done.3, bf16[1,4096,384]{2,1,0:T(8,128)(2,1)S(1)} %copy-done, bf16[1,384,4096]{2,1,0:T(8,128)(2,1)S(1)} %copy-done.1, ...), custom_call_target="tpu_custom_call" | custom-call | flops 301989888 | bytes 9437184 | tf_op jit(solution)/shard_map/expert/pallas_call | solution.py:362
  47.9 0.1 mix.6.refs_1_
  47.9 0.9 %collective-permute-start.17 = (bf16[32,4096]{1,0:T(8,128)(2,1)S(1)}, bf16[32,4096]{1,0:T(8,128)(2,1)S(1)}, u32[]{:S(2)}, u32[]{:S(2)}) collective-permute-start(bf16[32,4096]{1,0:T(8,128)(2,1)S(1)} %mix.6.refs_1_), channel_id=1, source_target_pairs={{4,0},{5,1},{6,2},{7,3},{8,12},{9,13},{10,14},{11,15},{0,4},{1,5},... | collective-permute-start | bytes 786440 | tf_op jit(solution)/shard_map/sum_b/ppermute | solution.py:415
  48.8 1.5 %collective-permute-start.18 = (bf16[32,4096]{1,0:T(8,128)(2,1)S(1)}, bf16[32,4096]{1,0:T(8,128)(2,1)S(1)}, u32[]{:S(2)}, u32[]{:S(2)}) collective-permute-start(bf16[32,4096]{1,0:T(8,128)(2,1)S(1)} %expert.15.refs_2_), channel_id=1, source_target_pairs={{0,12},{1,13},{2,14},{3,15},{4,5},{5,4},{6,7},{7,6},{8,9},{9,8},{1... | collective-permute-start | bytes 786440 | tf_op jit(solution)/shard_map/direct_b/ppermute | solution.py:409
  50.3 0.0 collective-permute-start.19
  50.3 0.0 collective-permute-done.14.refs_0_.refs_3_
  50.3 2.6 %collective-permute-done.13.refs_1_.refs_0_ = bf16[32,4096]{1,0:T(8,128)(2,1)S(1)} collective-permute-done((bf16[32,4096]{1,0:T(8,128)(2,1)S(1)}, bf16[32,4096]{1,0:T(8,128)(2,1)S(1)}, u32[]{:S(2)}, u32[]{:S(2)}) %collective-permute-start.13) | collective-permute-done | bytes 262176 | tf_op jit(solution)/shard_map/four/ppermute | solution.py:400
  52.9 0.1 mix.7.refs_4_
  53.0 1.5 %collective-permute-start.16 = (bf16[32,4096]{1,0:T(8,128)(2,1)S(1)}, bf16[32,4096]{1,0:T(8,128)(2,1)S(1)}, u32[]{:S(2)}, u32[]{:S(2)}) collective-permute-start(bf16[32,4096]{1,0:T(8,128)(2,1)S(1)} %mix.7.refs_4_), channel_id=1, source_target_pairs={{4,12},{5,13},{6,14},{7,15},{8,0},{9,1},{10,2},{11,3},{20,28},{21,... | collective-permute-start | bytes 786440 | tf_op jit(solution)/shard_map/across_a/ppermute | solution.py:415
  54.5 2.4 %shares.1.refs_0_.weight_ref = bf16[128,128]{1,0:T(8,128)(2,1)S(1)} custom-call(s32[1]{0:T(128)} %bitcast.me_ref, bf16[128,4096]{1,0:T(8,128)(2,1)} %refs_0_.9, bf16[32,128]{1,0:T(8,128)(2,1)} %bitcast.6, s32[8,128]{1,0:T(8,128)} %bitcast.8, bf16[4096,128]{1,0:T(8,128)(2,1)S(1)} %copy-done.4, bf16[32,4096]{1,0:T(8,128)(2,1)S(1)} %mix.7.refs_4_), custom_call_target="tpu_custom_call" | custom-call | flops 134217728 | bytes 2097152 | tf_op jit(solution)/shard_map/shares/pallas_call | solution.py:286
  56.9 1.6 %expert.16.refs_0_.own_ref = bf16[32,4096]{1,0:T(8,128)(2,1)S(1)} custom-call(bf16[32,4096]{1,0:T(8,128)(2,1)S(1)} %join.3.refs_0_.rows_ref, bf16[1,4096,384]{2,1,0:T(8,128)(2,1)S(1)} %copy-done.3, bf16[1,4096,384]{2,1,0:T(8,128)(2,1)S(1)} %copy-done, bf16[1,384,4096]{2,1,0:T(8,128)(2,1)S(1)} %copy-done.1, bf16[128,128]{1,0:T(8,128)(2,1)S(1)} %shares.1.refs_0_.weight_ref), custom_call_target="tpu_custom_call" | custom-call | flops 301989888 | bytes 9437184 | tf_op jit(solution)/shard_map/expert/pallas_call | solution.py:362
  58.5 1.7 %expert.17.refs_4_.own_ref = bf16[32,4096]{1,0:T(8,128)(2,1)S(1)} custom-call(bf16[32,4096]{1,0:T(8,128)(2,1)S(1)} %join.2.refs_1_.rows_ref, bf16[1,4096,384]{2,1,0:T(8,128)(2,1)S(1)} %copy-done.3, bf16[1,4096,384]{2,1,0:T(8,128)(2,1)S(1)} %copy-done, bf16[1,384,4096]{2,1,0:T(8,128)(2,1)S(1)} %copy-done.1, bf16[32,4096]{1,0:T(8,128)(2,1)S(1)} %expert.16.refs_0_.own_ref), custom_call_target="tpu_custom_call" | custom-call | flops 301989888 | bytes 9437184 | tf_op jit(solution)/shard_map/expert/pallas_call | solution.py:362
  60.2 0.0 collective-permute-done.17.refs_0_
  60.2 3.6 %collective-permute-done.18.refs_1_ = bf16[32,4096]{1,0:T(8,128)(2,1)S(1)} collective-permute-done((bf16[32,4096]{1,0:T(8,128)(2,1)S(1)}, bf16[32,4096]{1,0:T(8,128)(2,1)S(1)}, u32[]{:S(2)}, u32[]{:S(2)}) %collective-permute-start.18) | collective-permute-done | bytes 262176 | tf_op jit(solution)/shard_map/direct_b/ppermute | solution.py:409
  63.7 0.0 collective-permute-done.19.refs_3_
  63.8 0.1 finish.2
  63.9 1.6 %collective-permute-start.21 = (bf16[16,4096]{1,0:T(8,128)(2,1)S(1)}, bf16[16,4096]{1,0:T(8,128)(2,1)S(1)}, u32[]{:S(2)}, u32[]{:S(2)}) collective-permute-start(bf16[16,4096]{1,0:T(8,128)(2,1)S(1)} %get-tuple-element.17.refs_4_), channel_id=1, source_target_pairs={{0,2},{1,3},{2,0},{3,1},{4,6},{5,7},{6,4},{7,5},{8,10},{9,11},{10,... | collective-permute-start | bytes 393224 | tf_op jit(solution)/shard_map/plane2/ppermute | solution.py:395
  65.4 0.0 collective-permute-start.22
  65.4 4.0 %collective-permute-done.16.refs_1_ = bf16[32,4096]{1,0:T(8,128)(2,1)S(1)} collective-permute-done((bf16[32,4096]{1,0:T(8,128)(2,1)S(1)}, bf16[32,4096]{1,0:T(8,128)(2,1)S(1)}, u32[]{:S(2)}, u32[]{:S(2)}) %collective-permute-start.16) | collective-permute-done | bytes 262176 | tf_op jit(solution)/shard_map/across_a/ppermute | solution.py:415
  69.4 0.1 finish.3
  69.5 0.1 collective-permute-start.20
  69.6 1.6 %collective-permute-done.22.refs_3_ = bf16[16,4096]{1,0:T(8,128)(2,1)S(1)} collective-permute-done((bf16[16,4096]{1,0:T(8,128)(2,1)S(1)}, bf16[16,4096]{1,0:T(8,128)(2,1)S(1)}, u32[]{:S(2)}, u32[]{:S(2)}) %collective-permute-start.22) | collective-permute-done | bytes 131104 | tf_op jit(solution)/shard_map/plane3/ppermute | solution.py:395
  71.2 0.0 collective-permute-done.20.refs_1_
  71.2 1.2 %combine.1 = bf16[128,4096]{1,0:T(8,128)(2,1)} custom-call(bf16[128,128]{1,0:T(8,128)(2,1)S(1)} %shares.1.refs_0_.weight_ref, bf16[16,4096]{1,0:T(8,128)(2,1)S(1)} %get-tuple-element.18.refs_0_, bf16[16,4096]{1,0:T(8,128)(2,1)S(1)} %collective-permute-done.20.refs_1_, bf16[16,4096]{1,0:T(8,128)(2,1)S(1)} %collective-permute-done.21.refs_2_, ...), custom_call_target="tpu_custom_call" | custom-call | tf_op jit(solution)/shard_map/combine/pallas_call | solution.py:376
  (26 shorter events, 0.3 us)
Async XLA Ops:
  0.0 9.1 %copy-start = (bf16[1,4096,384]{2,1,0:T(8,128)(2,1)S(1)}, bf16[1,4096,384]{2,1,0:T(8,128)(2,1)}, u32[]{:S(2)}) copy-start(bf16[1,4096,384]{2,1,0:T(8,128)(2,1)} %up_ref.13) | copy-start | bytes 9437188
  2.1 3.2 %collective-permute-start = (bf16[16,4096]{1,0:T(8,128)(2,1)S(1)}, bf16[16,4096]{1,0:T(8,128)(2,1)S(1)}, u32[]{:S(2)}, u32[]{:S(2)}) collective-permute-start(bf16[16,4096]{1,0:T(8,128)(2,1)S(1)} %get-tuple-element.14), channel_id=1, source_target_pairs={{0,1},{1,0},{2,3},{3,2},{4,5},{5,4},{6,7},{7,6},{8,9},{9,8},{10,11... | collective-permute-start | bytes 393224 | tf_op jit(solution)/shard_map/plane1/ppermute | solution.py:395
  2.6 6.9 %collective-permute-start.2 = (bf16[16,4096]{1,0:T(8,128)(2,1)S(1)}, bf16[16,4096]{1,0:T(8,128)(2,1)S(1)}, u32[]{:S(2)}, u32[]{:S(2)}) collective-permute-start(bf16[16,4096]{1,0:T(8,128)(2,1)S(1)} %get-tuple-element.15), channel_id=1, source_target_pairs={{0,2},{1,3},{2,0},{3,1},{4,6},{5,7},{6,4},{7,5},{8,10},{9,11},{10,... | collective-permute-start | bytes 393224 | tf_op jit(solution)/shard_map/plane2/ppermute | solution.py:395
  5.2 6.6 %collective-permute-start.3 = (bf16[16,4096]{1,0:T(8,128)(2,1)S(1)}, bf16[16,4096]{1,0:T(8,128)(2,1)S(1)}, u32[]{:S(2)}, u32[]{:S(2)}) collective-permute-start(bf16[16,4096]{1,0:T(8,128)(2,1)S(1)} %get-tuple-element.16), channel_id=1, source_target_pairs={{0,3},{1,2},{2,1},{3,0},{4,7},{5,6},{6,5},{7,4},{8,11},{9,10},{10,... | collective-permute-start | bytes 393224 | tf_op jit(solution)/shard_map/plane3/ppermute | solution.py:395
  5.3 3.8 %copy-start.1 = (bf16[1,384,4096]{2,1,0:T(8,128)(2,1)S(1)}, bf16[1,384,4096]{2,1,0:T(8,128)(2,1)}, u32[]{:S(2)}) copy-start(bf16[1,384,4096]{2,1,0:T(8,128)(2,1)} %down_ref.13) | copy-start | bytes 9437188
  5.3 8.7 %collective-permute-start.1 = (bf16[32,4096]{1,0:T(8,128)(2,1)S(1)}, bf16[32,4096]{1,0:T(8,128)(2,1)S(1)}, u32[]{:S(2)}, u32[]{:S(2)}) collective-permute-start(bf16[32,4096]{1,0:T(8,128)(2,1)S(1)} %join.2.refs_1_.rows_ref), channel_id=1, source_target_pairs={{0,4},{1,5},{2,6},{3,7},{4,0},{5,1},{6,2},{7,3},{8,12},{9,13},{10,... | collective-permute-start | bytes 786440 | tf_op jit(solution)/shard_map/near_a/ppermute | solution.py:400
  7.2 8.6 %collective-permute-start.4 = (bf16[32,4096]{1,0:T(8,128)(2,1)S(1)}, bf16[32,4096]{1,0:T(8,128)(2,1)S(1)}, u32[]{:S(2)}, u32[]{:S(2)}) collective-permute-start(bf16[32,4096]{1,0:T(8,128)(2,1)S(1)} %join.2.refs_1_.rows_ref), channel_id=1, source_target_pairs={{0,1},{1,0},{2,3},{3,2},{4,8},{5,9},{6,10},{7,11},{8,4},{9,5},{10,... | collective-permute-start | bytes 786440 | tf_op jit(solution)/shard_map/far_in_a/ppermute | solution.py:409
  7.2 1.9 %copy-start.2 = (bf16[1,4096,384]{2,1,0:T(8,128)(2,1)S(1)}, bf16[1,4096,384]{2,1,0:T(8,128)(2,1)}, u32[]{:S(2)}) copy-start(bf16[1,4096,384]{2,1,0:T(8,128)(2,1)} %gate_ref.13) | copy-start | bytes 9437188
  9.1 4.9 %copy-start.3 = (bf16[1,4096,384]{2,1,0:T(8,128)(2,1)S(1)}, bf16[1,4096,384]{2,1,0:T(8,128)(2,1)}, u32[]{:S(2)}) copy-start(bf16[1,4096,384]{2,1,0:T(8,128)(2,1)} %gate_ref.13) | copy-start | bytes 9437188
  11.9 9.2 %collective-permute-start.7 = (bf16[32,4096]{1,0:T(8,128)(2,1)S(1)}, bf16[32,4096]{1,0:T(8,128)(2,1)S(1)}, u32[]{:S(2)}, u32[]{:S(2)}) collective-permute-start(bf16[32,4096]{1,0:T(8,128)(2,1)S(1)} %join.3.refs_0_.rows_ref), channel_id=1, source_target_pairs={{0,4},{1,5},{2,6},{3,7},{4,0},{5,1},{6,2},{7,3},{8,12},{9,13},{10,... | collective-permute-start | bytes 786440 | tf_op jit(solution)/shard_map/near_b/ppermute | solution.py:400
  13.5 9.2 %collective-permute-start.8 = (bf16[32,4096]{1,0:T(8,128)(2,1)S(1)}, bf16[32,4096]{1,0:T(8,128)(2,1)S(1)}, u32[]{:S(2)}, u32[]{:S(2)}) collective-permute-start(bf16[32,4096]{1,0:T(8,128)(2,1)S(1)} %join.3.refs_0_.rows_ref), channel_id=1, source_target_pairs={{0,1},{1,0},{2,3},{3,2},{4,8},{5,9},{6,10},{7,11},{8,4},{9,5},{10,... | collective-permute-start | bytes 786440 | tf_op jit(solution)/shard_map/far_in_b/ppermute | solution.py:409
  15.6 10.4 %collective-permute-start.6 = (bf16[32,4096]{1,0:T(8,128)(2,1)S(1)}, bf16[32,4096]{1,0:T(8,128)(2,1)S(1)}, u32[]{:S(2)}, u32[]{:S(2)}) collective-permute-start(bf16[32,4096]{1,0:T(8,128)(2,1)S(1)} %collective-permute-done.1.rows_ref), channel_id=1, source_target_pairs={{0,1},{1,0},{2,3},{3,2},{4,8},{5,9},{6,10},{7,11},{8,4},{9,5},{10,... | collective-permute-start | bytes 786440 | tf_op jit(solution)/shard_map/last_in_a/ppermute | solution.py:409
  15.8 10.5 %collective-permute-start.5 = (bf16[32,4096]{1,0:T(8,128)(2,1)S(1)}, bf16[32,4096]{1,0:T(8,128)(2,1)S(1)}, u32[]{:S(2)}, u32[]{:S(2)}) collective-permute-start(bf16[32,4096]{1,0:T(8,128)(2,1)S(1)} %choose.8.refs_0_), channel_id=1, source_target_pairs={{0,4},{1,5},{2,6},{3,7},{4,0},{5,1},{6,2},{7,3},{8,12},{9,13},{10,... | collective-permute-start | bytes 786440 | tf_op jit(solution)/shard_map/two_a/ppermute | solution.py:400
  21.1 10.1 %collective-permute-start.11 = (bf16[32,4096]{1,0:T(8,128)(2,1)S(1)}, bf16[32,4096]{1,0:T(8,128)(2,1)S(1)}, u32[]{:S(2)}, u32[]{:S(2)}) collective-permute-start(bf16[32,4096]{1,0:T(8,128)(2,1)S(1)} %collective-permute-done.7.rows_ref), channel_id=1, source_target_pairs={{0,1},{1,0},{2,3},{3,2},{4,8},{5,9},{6,10},{7,11},{8,4},{9,5},{10,... | collective-permute-start | bytes 786440 | tf_op jit(solution)/shard_map/last_in_b/ppermute | solution.py:409
  22.8 9.3 %collective-permute-start.10 = (bf16[32,4096]{1,0:T(8,128)(2,1)S(1)}, bf16[32,4096]{1,0:T(8,128)(2,1)S(1)}, u32[]{:S(2)}, u32[]{:S(2)}) collective-permute-start(bf16[32,4096]{1,0:T(8,128)(2,1)S(1)} %choose.9.refs_1_), channel_id=1, source_target_pairs={{0,4},{1,5},{2,6},{3,7},{4,0},{5,1},{6,2},{7,3},{8,12},{9,13},{10,... | collective-permute-start | bytes 786440 | tf_op jit(solution)/shard_map/two_b/ppermute | solution.py:400
  28.0 11.9 %collective-permute-start.9 = (bf16[32,4096]{1,0:T(8,128)(2,1)S(1)}, bf16[32,4096]{1,0:T(8,128)(2,1)S(1)}, u32[]{:S(2)}, u32[]{:S(2)}) collective-permute-start(bf16[32,4096]{1,0:T(8,128)(2,1)S(1)} %choose.11.refs_4_), channel_id=1, source_target_pairs={{0,4},{1,5},{2,6},{3,7},{4,0},{5,1},{6,2},{7,3},{8,12},{9,13},{10,... | collective-permute-start | bytes 786440 | tf_op jit(solution)/shard_map/three_a/ppermute | solution.py:400
  31.2 10.6 %collective-permute-start.12 = (bf16[32,4096]{1,0:T(8,128)(2,1)S(1)}, bf16[32,4096]{1,0:T(8,128)(2,1)S(1)}, u32[]{:S(2)}, u32[]{:S(2)}) collective-permute-start(bf16[32,4096]{1,0:T(8,128)(2,1)S(1)} %expert.12.refs_0_), channel_id=1, source_target_pairs={{0,1},{1,0},{2,3},{3,2},{4,8},{5,9},{6,10},{7,11},{8,4},{9,5},{10,... | collective-permute-start | bytes 786440 | tf_op jit(solution)/shard_map/across_b/ppermute | solution.py:409
  33.8 12.3 %collective-permute-start.15 = (bf16[32,4096]{1,0:T(8,128)(2,1)S(1)}, bf16[32,4096]{1,0:T(8,128)(2,1)S(1)}, u32[]{:S(2)}, u32[]{:S(2)}) collective-permute-start(bf16[32,4096]{1,0:T(8,128)(2,1)S(1)} %choose.13.refs_2_), channel_id=1, source_target_pairs={{0,4},{1,5},{2,6},{3,7},{4,0},{5,1},{6,2},{7,3},{8,12},{9,13},{10,... | collective-permute-start | bytes 786440 | tf_op jit(solution)/shard_map/three_b/ppermute | solution.py:400
  40.0 10.4 %collective-permute-start.14 = (bf16[32,4096]{1,0:T(8,128)(2,1)S(1)}, bf16[32,4096]{1,0:T(8,128)(2,1)S(1)}, u32[]{:S(2)}, u32[]{:S(2)}) collective-permute-start(bf16[32,4096]{1,0:T(8,128)(2,1)S(1)} %mix.4.refs_0_), channel_id=1, source_target_pairs={{0,1},{1,0},{2,3},{3,2},{4,8},{5,9},{6,10},{7,11},{8,4},{9,5},{10,... | collective-permute-start | bytes 786440 | tf_op jit(solution)/shard_map/mid_a/ppermute | solution.py:409
  41.8 11.1 %collective-permute-start.13 = (bf16[32,4096]{1,0:T(8,128)(2,1)S(1)}, bf16[32,4096]{1,0:T(8,128)(2,1)S(1)}, u32[]{:S(2)}, u32[]{:S(2)}) collective-permute-start(bf16[32,4096]{1,0:T(8,128)(2,1)S(1)} %choose.15.refs_2_), channel_id=1, source_target_pairs={{0,4},{1,5},{2,6},{3,7},{4,0},{5,1},{6,2},{7,3},{8,12},{9,13},{10,... | collective-permute-start | bytes 786440 | tf_op jit(solution)/shard_map/four/ppermute | solution.py:400
  46.2 8.2 %copy-start.4 = (bf16[4096,128]{1,0:T(8,128)(2,1)S(1)}, bf16[4096,128]{1,0:T(8,128)(2,1)}, u32[]{:S(2)}) copy-start(bf16[4096,128]{1,0:T(8,128)(2,1)} %refs_3_.5) | copy-start | bytes 3145732
  47.9 12.2 %collective-permute-start.17 = (bf16[32,4096]{1,0:T(8,128)(2,1)S(1)}, bf16[32,4096]{1,0:T(8,128)(2,1)S(1)}, u32[]{:S(2)}, u32[]{:S(2)}) collective-permute-start(bf16[32,4096]{1,0:T(8,128)(2,1)S(1)} %mix.6.refs_1_), channel_id=1, source_target_pairs={{4,0},{5,1},{6,2},{7,3},{8,12},{9,13},{10,14},{11,15},{0,4},{1,5},... | collective-permute-start | bytes 786440 | tf_op jit(solution)/shard_map/sum_b/ppermute | solution.py:415
  48.8 14.9 %collective-permute-start.18 = (bf16[32,4096]{1,0:T(8,128)(2,1)S(1)}, bf16[32,4096]{1,0:T(8,128)(2,1)S(1)}, u32[]{:S(2)}, u32[]{:S(2)}) collective-permute-start(bf16[32,4096]{1,0:T(8,128)(2,1)S(1)} %expert.15.refs_2_), channel_id=1, source_target_pairs={{0,12},{1,13},{2,14},{3,15},{4,5},{5,4},{6,7},{7,6},{8,9},{9,8},{1... | collective-permute-start | bytes 786440 | tf_op jit(solution)/shard_map/direct_b/ppermute | solution.py:409
  50.3 13.4 %collective-permute-start.19 = (bf16[32,4096]{1,0:T(8,128)(2,1)S(1)}, bf16[32,4096]{1,0:T(8,128)(2,1)S(1)}, u32[]{:S(2)}, u32[]{:S(2)}) collective-permute-start(bf16[32,4096]{1,0:T(8,128)(2,1)S(1)} %mix.5.refs_4_), channel_id=1, source_target_pairs={{0,1},{1,0},{2,3},{3,2},{4,8},{5,9},{6,10},{7,11},{8,4},{9,5},{10,... | collective-permute-start | bytes 786440 | tf_op jit(solution)/shard_map/mid_b/ppermute | solution.py:409
  53.0 16.5 %collective-permute-start.16 = (bf16[32,4096]{1,0:T(8,128)(2,1)S(1)}, bf16[32,4096]{1,0:T(8,128)(2,1)S(1)}, u32[]{:S(2)}, u32[]{:S(2)}) collective-permute-start(bf16[32,4096]{1,0:T(8,128)(2,1)S(1)} %mix.7.refs_4_), channel_id=1, source_target_pairs={{4,12},{5,13},{6,14},{7,15},{8,0},{9,1},{10,2},{11,3},{20,28},{21,... | collective-permute-start | bytes 786440 | tf_op jit(solution)/shard_map/across_a/ppermute | solution.py:415
  63.9 5.8 %collective-permute-start.21 = (bf16[16,4096]{1,0:T(8,128)(2,1)S(1)}, bf16[16,4096]{1,0:T(8,128)(2,1)S(1)}, u32[]{:S(2)}, u32[]{:S(2)}) collective-permute-start(bf16[16,4096]{1,0:T(8,128)(2,1)S(1)} %get-tuple-element.17.refs_4_), channel_id=1, source_target_pairs={{0,2},{1,3},{2,0},{3,1},{4,6},{5,7},{6,4},{7,5},{8,10},{9,11},{10,... | collective-permute-start | bytes 393224 | tf_op jit(solution)/shard_map/plane2/ppermute | solution.py:395
  65.4 5.8 %collective-permute-start.22 = (bf16[16,4096]{1,0:T(8,128)(2,1)S(1)}, bf16[16,4096]{1,0:T(8,128)(2,1)S(1)}, u32[]{:S(2)}, u32[]{:S(2)}) collective-permute-start(bf16[16,4096]{1,0:T(8,128)(2,1)S(1)} %get-tuple-element.20), channel_id=1, source_target_pairs={{0,3},{1,2},{2,1},{3,0},{4,7},{5,6},{6,5},{7,4},{8,11},{9,10},{10,... | collective-permute-start | bytes 393224 | tf_op jit(solution)/shard_map/plane3/ppermute | solution.py:395
  69.5 1.7 %collective-permute-start.20 = (bf16[16,4096]{1,0:T(8,128)(2,1)S(1)}, bf16[16,4096]{1,0:T(8,128)(2,1)S(1)}, u32[]{:S(2)}, u32[]{:S(2)}) collective-permute-start(bf16[16,4096]{1,0:T(8,128)(2,1)S(1)} %get-tuple-element.19), channel_id=1, source_target_pairs={{0,1},{1,0},{2,3},{3,2},{4,5},{5,4},{6,7},{7,6},{8,9},{9,8},{10,11... | collective-permute-start | bytes 393224 | tf_op jit(solution)/shard_map/plane1/ppermute | solution.py:395

commit v5 on v4

--- a/solution.py
+++ b/solution.py
@@ -410,7 +410,7 @@
 
 
 def inward_shift(rows, flight, near):
-    to = {1: 0, 2: 3, 0: 1, 3: 2} if near else {1: 3, 2: 0}
+    to = {1: 0, 2: 3} if near else {1: 3, 2: 0}
     pairs = [(m * flight + e, to[m] * flight + e) for m in to for e in range(flight)]
     return lax.ppermute(rows, "expert", pairs)
 
@@ -484,8 +484,8 @@
     seen(across_b)
     four = end("four", pick(last_part_a, near_part_a))
     mid_b = middle("mid_b", total(far_part_b, three_b))
+    sum_b = inward("sum_b", total(near_part_b, across_b), True)
     direct_b = middle("direct_b", partial(three_b, at_outer), (0, 3))
-    sum_b = inward("sum_b", total(near_part_b, across_b), True)
     seen(mid_a)
     across_a = inward("across_a", total(last_part_a, four), False)
     weight = then(shares(me, hidden, gain, ids, router_weight, flight, *tick))

time: 72.8 us -> 71.9 us (0.988)
  waiting for transfers between devices: 18.1 us -> 16 us
  starting transfers between devices: 32.5 us -> 33.7 us
    ppermute x8, waiting for transfers between devices: 3.59 us -> 0.04 us  [mirror_pair(): return lax.ppermute(rows, 'expert', pairs)]
    ppermute x2, waiting for transfers between devices: 3.99 us -> 7.26 us  [inward_shift(): return lax.ppermute(rows, 'expert', pairs)]
    ppermute x7, waiting for transfers between devices: 6.26 us -> 4.52 us  [end_pair(): return lax.ppermute(rows, 'expert', pairs)]
    ppermute x8, starting transfers between devices: 2.14 us -> 2.98 us  [mirror_pair(): return lax.ppermute(rows, 'expert', pairs)]
where the time goes in v5:
time: 71.9 us; the launch traced here: 71.7 us
  starting transfers between devices  33.7 us (47%)
  Pallas kernels  19.7 us (27%)
  waiting for transfers between devices  16 us (22%)
  local copies, waits for them, and re-layouts  1.91 us (3%)
    ppermute x7, starting transfers between devices, end_pair(): return lax.ppermute(rows, 'expert', pairs)  23.1 us
    pallas_call x9, Pallas kernels, expert(): pl.pallas_call(expert_kernel if flag is None else expert_if_kernel, out_s...  13.3 us
    ppermute x2, waiting for transfers between devices, inward_shift(): return lax.ppermute(rows, 'expert', pairs)  7.26 us
    ppermute x6, starting transfers between devices, in_plane(): return lax.ppermute(rows, 'expert', pairs)  4.84 us
    ppermute x7, waiting for transfers between devices, end_pair(): return lax.ppermute(rows, 'expert', pairs)  4.52 us
    ppermute x6, waiting for transfers between devices, in_plane(): return lax.ppermute(rows, 'expert', pairs)  4.16 us
    ppermute x8, starting transfers between devices, mirror_pair(): return lax.ppermute(rows, 'expert', pairs)  2.98 us
    ppermute x2, starting transfers between devices, inward_shift(): return lax.ppermute(rows, 'expert', pairs)  2.75 us
  transfers between devices with their start and end apart: 23, of which 11 were waited for; matrix products, arithmetic and copies ran while one was open for 0% of the time, Pallas kernels for 23%

profile of v5, /device:TPU:0, one launch (start us, length us, event | category | flops | bytes accessed | tf_op | source)
XLA Modules:
  0.0 71.7 jit_solution(3767158678939608728)
XLA Ops:
  0.0 2.1 %dispatch.1 = (bf16[16,4096]{1,0:T(8,128)(2,1)S(1)}, bf16[16,4096]{1,0:T(8,128)(2,1)S(1)}, bf16[16,4096]{1,0:T(8,128)(2,1)S(1)}, bf16[16,4096]{1,0:T(8,128)(2,1)S(1)}) custom-call(s32[1]{0:T(128)} %bitcast.me_ref, s32[1]{0:T(128)} %bitcast.3.outer_ref.flag_ref, s32[1]{0:T(128)} %bitcast.4.inner_ref.flag_ref, bf16[128,4096]{1,0:T(8,128)(2,1)} %refs_0_.9, ...), custom_call_target="tpu_custom_call" | custom-call | flops 131072 | bytes 128 | tf_op jit(solution)/shard_map/dispatch/pallas_call | solution.py:271
  2.1 0.5 collective-permute-start
  2.6 2.6 %collective-permute-start.2 = (bf16[16,4096]{1,0:T(8,128)(2,1)S(1)}, bf16[16,4096]{1,0:T(8,128)(2,1)S(1)}, u32[]{:S(2)}, u32[]{:S(2)}) collective-permute-start(bf16[16,4096]{1,0:T(8,128)(2,1)S(1)} %get-tuple-element.15), channel_id=1, source_target_pairs={{0,2},{1,3},{2,0},{3,1},{4,6},{5,7},{6,4},{7,5},{8,10},{9,11},{10,... | collective-permute-start | bytes 393224 | tf_op jit(solution)/shard_map/plane2/ppermute | solution.py:395
  5.2 0.1 collective-permute-start.3
  5.3 0.0 collective-permute-done.refs_1_
  5.3 0.0 copy-start.1
  5.3 1.8 %collective-permute-start.1 = (bf16[32,4096]{1,0:T(8,128)(2,1)S(1)}, bf16[32,4096]{1,0:T(8,128)(2,1)S(1)}, u32[]{:S(2)}, u32[]{:S(2)}) collective-permute-start(bf16[32,4096]{1,0:T(8,128)(2,1)S(1)} %join.2.refs_1_.rows_ref), channel_id=1, source_target_pairs={{0,4},{1,5},{2,6},{3,7},{4,0},{5,1},{6,2},{7,3},{8,12},{9,13},{10,... | collective-permute-start | bytes 786440 | tf_op jit(solution)/shard_map/near_a/ppermute | solution.py:400
  7.2 0.1 collective-permute-start.4
  7.2 1.9 %copy-done.2 = bf16[1,4096,384]{2,1,0:T(8,128)(2,1)S(1)} copy-done((bf16[1,4096,384]{2,1,0:T(8,128)(2,1)S(1)}, bf16[1,4096,384]{2,1,0:T(8,128)(2,1)}, u32[]{:S(2)}) %copy-start.2) | copy-done | bytes 3145752
  9.1 0.4 collective-permute-done.2.refs_0_
  9.6 2.3 %collective-permute-done.3.refs_1_ = bf16[16,4096]{1,0:T(8,128)(2,1)S(1)} collective-permute-done((bf16[16,4096]{1,0:T(8,128)(2,1)S(1)}, bf16[16,4096]{1,0:T(8,128)(2,1)S(1)}, u32[]{:S(2)}, u32[]{:S(2)}) %collective-permute-start.3) | collective-permute-done | bytes 131104 | tf_op jit(solution)/shard_map/plane3/ppermute | solution.py:395
  11.9 1.7 %collective-permute-start.7 = (bf16[32,4096]{1,0:T(8,128)(2,1)S(1)}, bf16[32,4096]{1,0:T(8,128)(2,1)S(1)}, u32[]{:S(2)}, u32[]{:S(2)}) collective-permute-start(bf16[32,4096]{1,0:T(8,128)(2,1)S(1)} %join.3.refs_0_.rows_ref), channel_id=1, source_target_pairs={{0,4},{1,5},{2,6},{3,7},{4,0},{5,1},{6,2},{7,3},{8,12},{9,13},{10,... | collective-permute-start | bytes 786440 | tf_op jit(solution)/shard_map/near_b/ppermute | solution.py:400
  13.5 0.3 collective-permute-start.8
  13.8 0.1 collective-permute-done.1.rows_ref
  14.0 1.7 %expert.9.ours_ref.refs_0_.theirs_ref = bf16[32,4096]{1,0:T(8,128)(2,1)S(1)} custom-call(bf16[32,4096]{1,0:T(8,128)(2,1)S(1)} %collective-permute-done.1.rows_ref, bf16[1,4096,384]{2,1,0:T(8,128)(2,1)S(1)} %copy-done.3, bf16[1,4096,384]{2,1,0:T(8,128)(2,1)S(1)} %copy-done, bf16[1,384,4096]{2,1,0:T(8,128)(2,1)S(1)} %copy-done.1, ...), custom_call_target="tpu_custom_call" | custom-call | flops 301989888 | bytes 9437184 | tf_op jit(solution)/shard_map/expert/pallas_call | solution.py:362
  15.6 0.1 collective-permute-start.6
  15.8 0.0 collective-permute-done.4.theirs_ref
  15.8 3.3 %collective-permute-start.5 = (bf16[32,4096]{1,0:T(8,128)(2,1)S(1)}, bf16[32,4096]{1,0:T(8,128)(2,1)S(1)}, u32[]{:S(2)}, u32[]{:S(2)}) collective-permute-start(bf16[32,4096]{1,0:T(8,128)(2,1)S(1)} %choose.8.refs_0_), channel_id=1, source_target_pairs={{0,4},{1,5},{2,6},{3,7},{4,0},{5,1},{6,2},{7,3},{8,12},{9,13},{10,... | collective-permute-start | bytes 786440 | tf_op jit(solution)/shard_map/two_a/ppermute | solution.py:400
  19.1 2.0 %collective-permute-done.7.rows_ref = bf16[32,4096]{1,0:T(8,128)(2,1)S(1)} collective-permute-done((bf16[32,4096]{1,0:T(8,128)(2,1)S(1)}, bf16[32,4096]{1,0:T(8,128)(2,1)S(1)}, u32[]{:S(2)}, u32[]{:S(2)}) %collective-permute-start.7) | collective-permute-done | bytes 262176 | tf_op jit(solution)/shard_map/near_b/ppermute | solution.py:400
  21.1 0.0 collective-permute-start.11
  21.1 1.7 %expert.10.ours_ref.refs_0_ = bf16[32,4096]{1,0:T(8,128)(2,1)S(1)} custom-call(bf16[32,4096]{1,0:T(8,128)(2,1)S(1)} %collective-permute-done.7.rows_ref, bf16[1,4096,384]{2,1,0:T(8,128)(2,1)S(1)} %copy-done.3, bf16[1,4096,384]{2,1,0:T(8,128)(2,1)S(1)} %copy-done, bf16[1,384,4096]{2,1,0:T(8,128)(2,1)S(1)} %copy-done.1, bf16[32,4096]{1,0:T(8,128)(2,1)S(1)} %choose.8.refs_0_), custom_call_target="tpu_custom_call" | custom-call | flops 301989888 | bytes 9437184 | tf_op jit(solution)/shard_map/expert/pallas_call | solution.py:362
  22.7 0.0 collective-permute-done.8.theirs_ref
  22.8 3.2 %collective-permute-start.10 = (bf16[32,4096]{1,0:T(8,128)(2,1)S(1)}, bf16[32,4096]{1,0:T(8,128)(2,1)S(1)}, u32[]{:S(2)}, u32[]{:S(2)}) collective-permute-start(bf16[32,4096]{1,0:T(8,128)(2,1)S(1)} %choose.9.refs_1_), channel_id=1, source_target_pairs={{0,4},{1,5},{2,6},{3,7},{4,0},{5,1},{6,2},{7,3},{8,12},{9,13},{10,... | collective-permute-start | bytes 786440 | tf_op jit(solution)/shard_map/two_b/ppermute | solution.py:400
  26.0 0.0 collective-permute-done.6.refs_0_.theirs_ref
  26.0 0.3 collective-permute-done.5.ours_ref.refs_2_
  26.3 1.7 %expert.11.ours_ref.refs_0_ = bf16[32,4096]{1,0:T(8,128)(2,1)S(1)} custom-call(bf16[32,4096]{1,0:T(8,128)(2,1)S(1)} %choose.10.rows_ref.refs_0_, bf16[1,4096,384]{2,1,0:T(8,128)(2,1)S(1)} %copy-done.3, bf16[1,4096,384]{2,1,0:T(8,128)(2,1)S(1)} %copy-done, bf16[1,384,4096]{2,1,0:T(8,128)(2,1)S(1)} %copy-done.1, bf16[32,4096]{1,0:T(8,128)(2,1)S(1)} %choose.10.rows_ref.refs_0_), custom_call_target="tpu_custom_call" | custom-call | flops 301989888 | bytes 9437184 | tf_op jit(solution)/shard_map/expert/pallas_call | solution.py:362
  28.0 3.1 %collective-permute-start.9 = (bf16[32,4096]{1,0:T(8,128)(2,1)S(1)}, bf16[32,4096]{1,0:T(8,128)(2,1)S(1)}, u32[]{:S(2)}, u32[]{:S(2)}) collective-permute-start(bf16[32,4096]{1,0:T(8,128)(2,1)S(1)} %choose.11.refs_4_), channel_id=1, source_target_pairs={{0,4},{1,5},{2,6},{3,7},{4,0},{5,1},{6,2},{7,3},{8,12},{9,13},{10,... | collective-permute-start | bytes 786440 | tf_op jit(solution)/shard_map/three_a/ppermute | solution.py:400
  31.2 0.0 collective-permute-done.11.refs_0_.theirs_ref
  31.2 0.1 collective-permute-start.12
  31.3 0.8 %collective-permute-done.10.ours_ref.refs_2_ = bf16[32,4096]{1,0:T(8,128)(2,1)S(1)} collective-permute-done((bf16[32,4096]{1,0:T(8,128)(2,1)S(1)}, bf16[32,4096]{1,0:T(8,128)(2,1)S(1)}, u32[]{:S(2)}, u32[]{:S(2)}) %collective-permute-start.10) | collective-permute-done | bytes 262176 | tf_op jit(solution)/shard_map/two_b/ppermute | solution.py:400
  32.1 1.7 %expert.13.ours_ref.refs_0_ = bf16[32,4096]{1,0:T(8,128)(2,1)S(1)} custom-call(bf16[32,4096]{1,0:T(8,128)(2,1)S(1)} %choose.12.rows_ref.refs_0_, bf16[1,4096,384]{2,1,0:T(8,128)(2,1)S(1)} %copy-done.3, bf16[1,4096,384]{2,1,0:T(8,128)(2,1)S(1)} %copy-done, bf16[1,384,4096]{2,1,0:T(8,128)(2,1)S(1)} %copy-done.1, bf16[32,4096]{1,0:T(8,128)(2,1)S(1)} %choose.12.rows_ref.refs_0_), custom_call_target="tpu_custom_call" | custom-call | flops 301989888 | bytes 9437184 | tf_op jit(solution)/shard_map/expert/pallas_call | solution.py:362
  33.8 6.1 %collective-permute-start.15 = (bf16[32,4096]{1,0:T(8,128)(2,1)S(1)}, bf16[32,4096]{1,0:T(8,128)(2,1)S(1)}, u32[]{:S(2)}, u32[]{:S(2)}) collective-permute-start(bf16[32,4096]{1,0:T(8,128)(2,1)S(1)} %choose.13.refs_2_), channel_id=1, source_target_pairs={{0,4},{1,5},{2,6},{3,7},{4,0},{5,1},{6,2},{7,3},{8,12},{9,13},{10,... | collective-permute-start | bytes 786440 | tf_op jit(solution)/shard_map/three_b/ppermute | solution.py:400
  39.9 0.0 collective-permute-done.9.refs_1_.ours_ref
  39.9 0.1 mix.4.refs_0_
  40.0 0.1 collective-permute-start.14
  40.1 1.6 %expert.14.refs_1_.ours_ref.refs_0_ = bf16[32,4096]{1,0:T(8,128)(2,1)S(1)} custom-call(bf16[32,4096]{1,0:T(8,128)(2,1)S(1)} %choose.14.rows_ref.refs_0_, bf16[1,4096,384]{2,1,0:T(8,128)(2,1)S(1)} %copy-done.3, bf16[1,4096,384]{2,1,0:T(8,128)(2,1)S(1)} %copy-done, bf16[1,384,4096]{2,1,0:T(8,128)(2,1)S(1)} %copy-done.1, ...), custom_call_target="tpu_custom_call" | custom-call | flops 301989888 | bytes 9437184 | tf_op jit(solution)/shard_map/expert/pallas_call | solution.py:362
  41.7 0.0 collective-permute-done.12.refs_0_.refs_1_
  41.8 3.9 %collective-permute-start.13 = (bf16[32,4096]{1,0:T(8,128)(2,1)S(1)}, bf16[32,4096]{1,0:T(8,128)(2,1)S(1)}, u32[]{:S(2)}, u32[]{:S(2)}) collective-permute-start(bf16[32,4096]{1,0:T(8,128)(2,1)S(1)} %choose.15.refs_2_), channel_id=1, source_target_pairs={{0,4},{1,5},{2,6},{3,7},{4,0},{5,1},{6,2},{7,3},{8,12},{9,13},{10,... | collective-permute-start | bytes 786440 | tf_op jit(solution)/shard_map/four/ppermute | solution.py:400
  45.7 0.5 collective-permute-done.15.refs_1_.refs_0_
  46.1 0.1 mix.5.refs_2_
  46.2 0.1 mix.6.refs_4_
  46.3 0.0 copy-start.4
  46.3 1.7 %expert.15.refs_1_ = bf16[32,4096]{1,0:T(8,128)(2,1)S(1)} custom-call(s32[1]{0:T(128)} %bitcast.3.outer_ref.flag_ref, bf16[32,4096]{1,0:T(8,128)(2,1)S(1)} %collective-permute-done.15.refs_1_.refs_0_, bf16[1,4096,384]{2,1,0:T(8,128)(2,1)S(1)} %copy-done.3, bf16[1,4096,384]{2,1,0:T(8,128)(2,1)S(1)} %copy-done, bf16[1,384,4096]{2,1,0:T(8,128)(2,1)S(1)} %copy-done.1, ...), custom_call_target="tpu_custom_call" | custom-call | flops 301989888 | bytes 9437184 | tf_op jit(solution)/shard_map/expert/pallas_call | solution.py:362
  47.9 2.3 %collective-permute-start.18 = (bf16[32,4096]{1,0:T(8,128)(2,1)S(1)}, bf16[32,4096]{1,0:T(8,128)(2,1)S(1)}, u32[]{:S(2)}, u32[]{:S(2)}) collective-permute-start(bf16[32,4096]{1,0:T(8,128)(2,1)S(1)} %expert.15.refs_1_), channel_id=1, source_target_pairs={{0,12},{1,13},{2,14},{3,15},{4,5},{5,4},{6,7},{7,6},{8,9},{9,8},{1... | collective-permute-start | bytes 786440 | tf_op jit(solution)/shard_map/direct_b/ppermute | solution.py:409
  50.2 1.3 %collective-permute-start.17 = (bf16[32,4096]{1,0:T(8,128)(2,1)S(1)}, bf16[32,4096]{1,0:T(8,128)(2,1)S(1)}, u32[]{:S(2)}, u32[]{:S(2)}) collective-permute-start(bf16[32,4096]{1,0:T(8,128)(2,1)S(1)} %mix.6.refs_4_), channel_id=1, source_target_pairs={{4,0},{5,1},{6,2},{7,3},{8,12},{9,13},{10,14},{11,15},{20,16},{21,... | collective-permute-start | bytes 786440 | tf_op jit(solution)/shard_map/sum_b/ppermute | solution.py:415
  51.5 0.1 collective-permute-start.19
  51.6 0.0 collective-permute-done.14.refs_0_.refs_3_
  51.6 0.8 %collective-permute-done.13.refs_1_.refs_0_ = bf16[32,4096]{1,0:T(8,128)(2,1)S(1)} collective-permute-done((bf16[32,4096]{1,0:T(8,128)(2,1)S(1)}, bf16[32,4096]{1,0:T(8,128)(2,1)S(1)}, u32[]{:S(2)}, u32[]{:S(2)}) %collective-permute-start.13) | collective-permute-done | bytes 262176 | tf_op jit(solution)/shard_map/four/ppermute | solution.py:400
  52.4 0.1 mix.7.refs_4_
  52.5 1.5 %collective-permute-start.16 = (bf16[32,4096]{1,0:T(8,128)(2,1)S(1)}, bf16[32,4096]{1,0:T(8,128)(2,1)S(1)}, u32[]{:S(2)}, u32[]{:S(2)}) collective-permute-start(bf16[32,4096]{1,0:T(8,128)(2,1)S(1)} %mix.7.refs_4_), channel_id=1, source_target_pairs={{4,12},{5,13},{6,14},{7,15},{8,0},{9,1},{10,2},{11,3},{20,28},{21,... | collective-permute-start | bytes 786440 | tf_op jit(solution)/shard_map/across_a/ppermute | solution.py:415
  54.0 2.4 %shares.1.refs_0_.weight_ref = bf16[128,128]{1,0:T(8,128)(2,1)S(1)} custom-call(s32[1]{0:T(128)} %bitcast.me_ref, bf16[128,4096]{1,0:T(8,128)(2,1)} %refs_0_.9, bf16[32,128]{1,0:T(8,128)(2,1)} %bitcast.6, s32[8,128]{1,0:T(8,128)} %bitcast.8, bf16[4096,128]{1,0:T(8,128)(2,1)S(1)} %copy-done.4, bf16[32,4096]{1,0:T(8,128)(2,1)S(1)} %mix.7.refs_4_), custom_call_target="tpu_custom_call" | custom-call | flops 134217728 | bytes 2097152 | tf_op jit(solution)/shard_map/shares/pallas_call | solution.py:286
  56.4 1.7 %expert.16.refs_0_.own_ref = bf16[32,4096]{1,0:T(8,128)(2,1)S(1)} custom-call(bf16[32,4096]{1,0:T(8,128)(2,1)S(1)} %join.3.refs_0_.rows_ref, bf16[1,4096,384]{2,1,0:T(8,128)(2,1)S(1)} %copy-done.3, bf16[1,4096,384]{2,1,0:T(8,128)(2,1)S(1)} %copy-done, bf16[1,384,4096]{2,1,0:T(8,128)(2,1)S(1)} %copy-done.1, bf16[128,128]{1,0:T(8,128)(2,1)S(1)} %shares.1.refs_0_.weight_ref), custom_call_target="tpu_custom_call" | custom-call | flops 301989888 | bytes 9437184 | tf_op jit(solution)/shard_map/expert/pallas_call | solution.py:362
  58.0 1.7 %expert.17.refs_4_.own_ref = bf16[32,4096]{1,0:T(8,128)(2,1)S(1)} custom-call(bf16[32,4096]{1,0:T(8,128)(2,1)S(1)} %join.2.refs_1_.rows_ref, bf16[1,4096,384]{2,1,0:T(8,128)(2,1)S(1)} %copy-done.3, bf16[1,4096,384]{2,1,0:T(8,128)(2,1)S(1)} %copy-done, bf16[1,384,4096]{2,1,0:T(8,128)(2,1)S(1)} %copy-done.1, bf16[32,4096]{1,0:T(8,128)(2,1)S(1)} %expert.16.refs_0_.own_ref), custom_call_target="tpu_custom_call" | custom-call | flops 301989888 | bytes 9437184 | tf_op jit(solution)/shard_map/expert/pallas_call | solution.py:362
  59.7 0.0 collective-permute-done.18.refs_1_
  59.7 3.1 %collective-permute-done.17.refs_0_ = bf16[32,4096]{1,0:T(8,128)(2,1)S(1)} collective-permute-done((bf16[32,4096]{1,0:T(8,128)(2,1)S(1)}, bf16[32,4096]{1,0:T(8,128)(2,1)S(1)}, u32[]{:S(2)}, u32[]{:S(2)}) %collective-permute-start.17) | collective-permute-done | bytes 262176 | tf_op jit(solution)/shard_map/sum_b/ppermute | solution.py:415
  62.9 0.0 collective-permute-done.19.refs_3_
  62.9 0.1 finish.2
  63.0 1.6 %collective-permute-start.21 = (bf16[16,4096]{1,0:T(8,128)(2,1)S(1)}, bf16[16,4096]{1,0:T(8,128)(2,1)S(1)}, u32[]{:S(2)}, u32[]{:S(2)}) collective-permute-start(bf16[16,4096]{1,0:T(8,128)(2,1)S(1)} %get-tuple-element.17.refs_4_), channel_id=1, source_target_pairs={{0,2},{1,3},{2,0},{3,1},{4,6},{5,7},{6,4},{7,5},{8,10},{9,11},{10,... | collective-permute-start | bytes 393224 | tf_op jit(solution)/shard_map/plane2/ppermute | solution.py:395
  64.6 4.1 %collective-permute-done.16.refs_1_ = bf16[32,4096]{1,0:T(8,128)(2,1)S(1)} collective-permute-done((bf16[32,4096]{1,0:T(8,128)(2,1)S(1)}, bf16[32,4096]{1,0:T(8,128)(2,1)S(1)}, u32[]{:S(2)}, u32[]{:S(2)}) %collective-permute-start.16) | collective-permute-done | bytes 262176 | tf_op jit(solution)/shard_map/across_a/ppermute | solution.py:415
  68.7 0.1 finish.3
  68.8 0.1 collective-permute-start.20
  68.9 0.0 collective-permute-done.21.refs_2_
  68.9 1.5 %collective-permute-done.22.refs_3_ = bf16[16,4096]{1,0:T(8,128)(2,1)S(1)} collective-permute-done((bf16[16,4096]{1,0:T(8,128)(2,1)S(1)}, bf16[16,4096]{1,0:T(8,128)(2,1)S(1)}, u32[]{:S(2)}, u32[]{:S(2)}) %collective-permute-start.22) | collective-permute-done | bytes 131104 | tf_op jit(solution)/shard_map/plane3/ppermute | solution.py:395
  70.3 1.2 %combine.1 = bf16[128,4096]{1,0:T(8,128)(2,1)} custom-call(bf16[128,128]{1,0:T(8,128)(2,1)S(1)} %shares.1.refs_0_.weight_ref, bf16[16,4096]{1,0:T(8,128)(2,1)S(1)} %get-tuple-element.18.refs_0_, bf16[16,4096]{1,0:T(8,128)(2,1)S(1)} %collective-permute-done.20.refs_1_, bf16[16,4096]{1,0:T(8,128)(2,1)S(1)} %collective-permute-done.21.refs_2_, ...), custom_call_target="tpu_custom_call" | custom-call | tf_op jit(solution)/shard_map/combine/pallas_call | solution.py:376
  (26 shorter events, 0.3 us)
Async XLA Ops:
  0.0 9.1 %copy-start = (bf16[1,4096,384]{2,1,0:T(8,128)(2,1)S(1)}, bf16[1,4096,384]{2,1,0:T(8,128)(2,1)}, u32[]{:S(2)}) copy-start(bf16[1,4096,384]{2,1,0:T(8,128)(2,1)} %up_ref.13) | copy-start | bytes 9437188
  2.1 3.2 %collective-permute-start = (bf16[16,4096]{1,0:T(8,128)(2,1)S(1)}, bf16[16,4096]{1,0:T(8,128)(2,1)S(1)}, u32[]{:S(2)}, u32[]{:S(2)}) collective-permute-start(bf16[16,4096]{1,0:T(8,128)(2,1)S(1)} %get-tuple-element.14), channel_id=1, source_target_pairs={{0,1},{1,0},{2,3},{3,2},{4,5},{5,4},{6,7},{7,6},{8,9},{9,8},{10,11... | collective-permute-start | bytes 393224 | tf_op jit(solution)/shard_map/plane1/ppermute | solution.py:395
  2.6 6.9 %collective-permute-start.2 = (bf16[16,4096]{1,0:T(8,128)(2,1)S(1)}, bf16[16,4096]{1,0:T(8,128)(2,1)S(1)}, u32[]{:S(2)}, u32[]{:S(2)}) collective-permute-start(bf16[16,4096]{1,0:T(8,128)(2,1)S(1)} %get-tuple-element.15), channel_id=1, source_target_pairs={{0,2},{1,3},{2,0},{3,1},{4,6},{5,7},{6,4},{7,5},{8,10},{9,11},{10,... | collective-permute-start | bytes 393224 | tf_op jit(solution)/shard_map/plane2/ppermute | solution.py:395
  5.2 6.6 %collective-permute-start.3 = (bf16[16,4096]{1,0:T(8,128)(2,1)S(1)}, bf16[16,4096]{1,0:T(8,128)(2,1)S(1)}, u32[]{:S(2)}, u32[]{:S(2)}) collective-permute-start(bf16[16,4096]{1,0:T(8,128)(2,1)S(1)} %get-tuple-element.16), channel_id=1, source_target_pairs={{0,3},{1,2},{2,1},{3,0},{4,7},{5,6},{6,5},{7,4},{8,11},{9,10},{10,... | collective-permute-start | bytes 393224 | tf_op jit(solution)/shard_map/plane3/ppermute | solution.py:395
  5.3 3.8 %copy-start.1 = (bf16[1,384,4096]{2,1,0:T(8,128)(2,1)S(1)}, bf16[1,384,4096]{2,1,0:T(8,128)(2,1)}, u32[]{:S(2)}) copy-start(bf16[1,384,4096]{2,1,0:T(8,128)(2,1)} %down_ref.13) | copy-start | bytes 9437188
  5.3 8.7 %collective-permute-start.1 = (bf16[32,4096]{1,0:T(8,128)(2,1)S(1)}, bf16[32,4096]{1,0:T(8,128)(2,1)S(1)}, u32[]{:S(2)}, u32[]{:S(2)}) collective-permute-start(bf16[32,4096]{1,0:T(8,128)(2,1)S(1)} %join.2.refs_1_.rows_ref), channel_id=1, source_target_pairs={{0,4},{1,5},{2,6},{3,7},{4,0},{5,1},{6,2},{7,3},{8,12},{9,13},{10,... | collective-permute-start | bytes 786440 | tf_op jit(solution)/shard_map/near_a/ppermute | solution.py:400
  7.2 8.6 %collective-permute-start.4 = (bf16[32,4096]{1,0:T(8,128)(2,1)S(1)}, bf16[32,4096]{1,0:T(8,128)(2,1)S(1)}, u32[]{:S(2)}, u32[]{:S(2)}) collective-permute-start(bf16[32,4096]{1,0:T(8,128)(2,1)S(1)} %join.2.refs_1_.rows_ref), channel_id=1, source_target_pairs={{0,1},{1,0},{2,3},{3,2},{4,8},{5,9},{6,10},{7,11},{8,4},{9,5},{10,... | collective-permute-start | bytes 786440 | tf_op jit(solution)/shard_map/far_in_a/ppermute | solution.py:409
  7.2 1.9 %copy-start.2 = (bf16[1,4096,384]{2,1,0:T(8,128)(2,1)S(1)}, bf16[1,4096,384]{2,1,0:T(8,128)(2,1)}, u32[]{:S(2)}) copy-start(bf16[1,4096,384]{2,1,0:T(8,128)(2,1)} %gate_ref.13) | copy-start | bytes 9437188
  9.1 4.9 %copy-start.3 = (bf16[1,4096,384]{2,1,0:T(8,128)(2,1)S(1)}, bf16[1,4096,384]{2,1,0:T(8,128)(2,1)}, u32[]{:S(2)}) copy-start(bf16[1,4096,384]{2,1,0:T(8,128)(2,1)} %gate_ref.13) | copy-start | bytes 9437188
  11.9 9.2 %collective-permute-start.7 = (bf16[32,4096]{1,0:T(8,128)(2,1)S(1)}, bf16[32,4096]{1,0:T(8,128)(2,1)S(1)}, u32[]{:S(2)}, u32[]{:S(2)}) collective-permute-start(bf16[32,4096]{1,0:T(8,128)(2,1)S(1)} %join.3.refs_0_.rows_ref), channel_id=1, source_target_pairs={{0,4},{1,5},{2,6},{3,7},{4,0},{5,1},{6,2},{7,3},{8,12},{9,13},{10,... | collective-permute-start | bytes 786440 | tf_op jit(solution)/shard_map/near_b/ppermute | solution.py:400
  13.5 9.2 %collective-permute-start.8 = (bf16[32,4096]{1,0:T(8,128)(2,1)S(1)}, bf16[32,4096]{1,0:T(8,128)(2,1)S(1)}, u32[]{:S(2)}, u32[]{:S(2)}) collective-permute-start(bf16[32,4096]{1,0:T(8,128)(2,1)S(1)} %join.3.refs_0_.rows_ref), channel_id=1, source_target_pairs={{0,1},{1,0},{2,3},{3,2},{4,8},{5,9},{6,10},{7,11},{8,4},{9,5},{10,... | collective-permute-start | bytes 786440 | tf_op jit(solution)/shard_map/far_in_b/ppermute | solution.py:409
  15.6 10.4 %collective-permute-start.6 = (bf16[32,4096]{1,0:T(8,128)(2,1)S(1)}, bf16[32,4096]{1,0:T(8,128)(2,1)S(1)}, u32[]{:S(2)}, u32[]{:S(2)}) collective-permute-start(bf16[32,4096]{1,0:T(8,128)(2,1)S(1)} %collective-permute-done.1.rows_ref), channel_id=1, source_target_pairs={{0,1},{1,0},{2,3},{3,2},{4,8},{5,9},{6,10},{7,11},{8,4},{9,5},{10,... | collective-permute-start | bytes 786440 | tf_op jit(solution)/shard_map/last_in_a/ppermute | solution.py:409
  15.8 10.5 %collective-permute-start.5 = (bf16[32,4096]{1,0:T(8,128)(2,1)S(1)}, bf16[32,4096]{1,0:T(8,128)(2,1)S(1)}, u32[]{:S(2)}, u32[]{:S(2)}) collective-permute-start(bf16[32,4096]{1,0:T(8,128)(2,1)S(1)} %choose.8.refs_0_), channel_id=1, source_target_pairs={{0,4},{1,5},{2,6},{3,7},{4,0},{5,1},{6,2},{7,3},{8,12},{9,13},{10,... | collective-permute-start | bytes 786440 | tf_op jit(solution)/shard_map/two_a/ppermute | solution.py:400
  21.1 10.1 %collective-permute-start.11 = (bf16[32,4096]{1,0:T(8,128)(2,1)S(1)}, bf16[32,4096]{1,0:T(8,128)(2,1)S(1)}, u32[]{:S(2)}, u32[]{:S(2)}) collective-permute-start(bf16[32,4096]{1,0:T(8,128)(2,1)S(1)} %collective-permute-done.7.rows_ref), channel_id=1, source_target_pairs={{0,1},{1,0},{2,3},{3,2},{4,8},{5,9},{6,10},{7,11},{8,4},{9,5},{10,... | collective-permute-start | bytes 786440 | tf_op jit(solution)/shard_map/last_in_b/ppermute | solution.py:409
  22.8 9.3 %collective-permute-start.10 = (bf16[32,4096]{1,0:T(8,128)(2,1)S(1)}, bf16[32,4096]{1,0:T(8,128)(2,1)S(1)}, u32[]{:S(2)}, u32[]{:S(2)}) collective-permute-start(bf16[32,4096]{1,0:T(8,128)(2,1)S(1)} %choose.9.refs_1_), channel_id=1, source_target_pairs={{0,4},{1,5},{2,6},{3,7},{4,0},{5,1},{6,2},{7,3},{8,12},{9,13},{10,... | collective-permute-start | bytes 786440 | tf_op jit(solution)/shard_map/two_b/ppermute | solution.py:400
  28.0 11.9 %collective-permute-start.9 = (bf16[32,4096]{1,0:T(8,128)(2,1)S(1)}, bf16[32,4096]{1,0:T(8,128)(2,1)S(1)}, u32[]{:S(2)}, u32[]{:S(2)}) collective-permute-start(bf16[32,4096]{1,0:T(8,128)(2,1)S(1)} %choose.11.refs_4_), channel_id=1, source_target_pairs={{0,4},{1,5},{2,6},{3,7},{4,0},{5,1},{6,2},{7,3},{8,12},{9,13},{10,... | collective-permute-start | bytes 786440 | tf_op jit(solution)/shard_map/three_a/ppermute | solution.py:400
  31.2 10.6 %collective-permute-start.12 = (bf16[32,4096]{1,0:T(8,128)(2,1)S(1)}, bf16[32,4096]{1,0:T(8,128)(2,1)S(1)}, u32[]{:S(2)}, u32[]{:S(2)}) collective-permute-start(bf16[32,4096]{1,0:T(8,128)(2,1)S(1)} %expert.12.refs_0_), channel_id=1, source_target_pairs={{0,1},{1,0},{2,3},{3,2},{4,8},{5,9},{6,10},{7,11},{8,4},{9,5},{10,... | collective-permute-start | bytes 786440 | tf_op jit(solution)/shard_map/across_b/ppermute | solution.py:409
  33.8 12.3 %collective-permute-start.15 = (bf16[32,4096]{1,0:T(8,128)(2,1)S(1)}, bf16[32,4096]{1,0:T(8,128)(2,1)S(1)}, u32[]{:S(2)}, u32[]{:S(2)}) collective-permute-start(bf16[32,4096]{1,0:T(8,128)(2,1)S(1)} %choose.13.refs_2_), channel_id=1, source_target_pairs={{0,4},{1,5},{2,6},{3,7},{4,0},{5,1},{6,2},{7,3},{8,12},{9,13},{10,... | collective-permute-start | bytes 786440 | tf_op jit(solution)/shard_map/three_b/ppermute | solution.py:400
  40.0 11.6 %collective-permute-start.14 = (bf16[32,4096]{1,0:T(8,128)(2,1)S(1)}, bf16[32,4096]{1,0:T(8,128)(2,1)S(1)}, u32[]{:S(2)}, u32[]{:S(2)}) collective-permute-start(bf16[32,4096]{1,0:T(8,128)(2,1)S(1)} %mix.4.refs_0_), channel_id=1, source_target_pairs={{0,1},{1,0},{2,3},{3,2},{4,8},{5,9},{6,10},{7,11},{8,4},{9,5},{10,... | collective-permute-start | bytes 786440 | tf_op jit(solution)/shard_map/mid_a/ppermute | solution.py:409
  41.8 10.6 %collective-permute-start.13 = (bf16[32,4096]{1,0:T(8,128)(2,1)S(1)}, bf16[32,4096]{1,0:T(8,128)(2,1)S(1)}, u32[]{:S(2)}, u32[]{:S(2)}) collective-permute-start(bf16[32,4096]{1,0:T(8,128)(2,1)S(1)} %choose.15.refs_2_), channel_id=1, source_target_pairs={{0,4},{1,5},{2,6},{3,7},{4,0},{5,1},{6,2},{7,3},{8,12},{9,13},{10,... | collective-permute-start | bytes 786440 | tf_op jit(solution)/shard_map/four/ppermute | solution.py:400
  46.3 7.7 %copy-start.4 = (bf16[4096,128]{1,0:T(8,128)(2,1)S(1)}, bf16[4096,128]{1,0:T(8,128)(2,1)}, u32[]{:S(2)}) copy-start(bf16[4096,128]{1,0:T(8,128)(2,1)} %refs_3_.5) | copy-start | bytes 3145732
  47.9 11.8 %collective-permute-start.18 = (bf16[32,4096]{1,0:T(8,128)(2,1)S(1)}, bf16[32,4096]{1,0:T(8,128)(2,1)S(1)}, u32[]{:S(2)}, u32[]{:S(2)}) collective-permute-start(bf16[32,4096]{1,0:T(8,128)(2,1)S(1)} %expert.15.refs_1_), channel_id=1, source_target_pairs={{0,12},{1,13},{2,14},{3,15},{4,5},{5,4},{6,7},{7,6},{8,9},{9,8},{1... | collective-permute-start | bytes 786440 | tf_op jit(solution)/shard_map/direct_b/ppermute | solution.py:409
  50.2 12.6 %collective-permute-start.17 = (bf16[32,4096]{1,0:T(8,128)(2,1)S(1)}, bf16[32,4096]{1,0:T(8,128)(2,1)S(1)}, u32[]{:S(2)}, u32[]{:S(2)}) collective-permute-start(bf16[32,4096]{1,0:T(8,128)(2,1)S(1)} %mix.6.refs_4_), channel_id=1, source_target_pairs={{4,0},{5,1},{6,2},{7,3},{8,12},{9,13},{10,14},{11,15},{20,16},{21,... | collective-permute-start | bytes 786440 | tf_op jit(solution)/shard_map/sum_b/ppermute | solution.py:415
  51.5 11.3 %collective-permute-start.19 = (bf16[32,4096]{1,0:T(8,128)(2,1)S(1)}, bf16[32,4096]{1,0:T(8,128)(2,1)S(1)}, u32[]{:S(2)}, u32[]{:S(2)}) collective-permute-start(bf16[32,4096]{1,0:T(8,128)(2,1)S(1)} %mix.5.refs_2_), channel_id=1, source_target_pairs={{0,1},{1,0},{2,3},{3,2},{4,8},{5,9},{6,10},{7,11},{8,4},{9,5},{10,... | collective-permute-start | bytes 786440 | tf_op jit(solution)/shard_map/mid_b/ppermute | solution.py:409
  52.5 16.2 %collective-permute-start.16 = (bf16[32,4096]{1,0:T(8,128)(2,1)S(1)}, bf16[32,4096]{1,0:T(8,128)(2,1)S(1)}, u32[]{:S(2)}, u32[]{:S(2)}) collective-permute-start(bf16[32,4096]{1,0:T(8,128)(2,1)S(1)} %mix.7.refs_4_), channel_id=1, source_target_pairs={{4,12},{5,13},{6,14},{7,15},{8,0},{9,1},{10,2},{11,3},{20,28},{21,... | collective-permute-start | bytes 786440 | tf_op jit(solution)/shard_map/across_a/ppermute | solution.py:415
  63.0 5.9 %collective-permute-start.21 = (bf16[16,4096]{1,0:T(8,128)(2,1)S(1)}, bf16[16,4096]{1,0:T(8,128)(2,1)S(1)}, u32[]{:S(2)}, u32[]{:S(2)}) collective-permute-start(bf16[16,4096]{1,0:T(8,128)(2,1)S(1)} %get-tuple-element.17.refs_4_), channel_id=1, source_target_pairs={{0,2},{1,3},{2,0},{3,1},{4,6},{5,7},{6,4},{7,5},{8,10},{9,11},{10,... | collective-permute-start | bytes 393224 | tf_op jit(solution)/shard_map/plane2/ppermute | solution.py:395
  64.5 5.8 %collective-permute-start.22 = (bf16[16,4096]{1,0:T(8,128)(2,1)S(1)}, bf16[16,4096]{1,0:T(8,128)(2,1)S(1)}, u32[]{:S(2)}, u32[]{:S(2)}) collective-permute-start(bf16[16,4096]{1,0:T(8,128)(2,1)S(1)} %get-tuple-element.20), channel_id=1, source_target_pairs={{0,3},{1,2},{2,1},{3,0},{4,7},{5,6},{6,5},{7,4},{8,11},{9,10},{10,... | collective-permute-start | bytes 393224 | tf_op jit(solution)/shard_map/plane3/ppermute | solution.py:395
  68.8 1.6 %collective-permute-start.20 = (bf16[16,4096]{1,0:T(8,128)(2,1)S(1)}, bf16[16,4096]{1,0:T(8,128)(2,1)S(1)}, u32[]{:S(2)}, u32[]{:S(2)}) collective-permute-start(bf16[16,4096]{1,0:T(8,128)(2,1)S(1)} %get-tuple-element.19), channel_id=1, source_target_pairs={{0,1},{1,0},{2,3},{3,2},{4,5},{5,4},{6,7},{7,6},{8,9},{9,8},{10,11... | collective-permute-start | bytes 393224 | tf_op jit(solution)/shard_map/plane1/ppermute | solution.py:395

commit v6 on v5

--- a/solution.py
+++ b/solution.py
@@ -11,7 +11,8 @@
 CAP = 16
 EPS = 1e-06
 PIECE = 512
-COLUMNS = 512
+COLUMNS = 256
+PARTS = 4
 VMEM_LIMIT = 16 * 1024 * 1024
 
 
@@ -85,12 +86,31 @@
 def dispatch_kernel(flight, me_ref, outer_ref, inner_ref, *refs):
     out_refs = refs[3:-4]
     hidden_ref, gain_ref, ids_ref, sems = refs[-4:]
-    fetch(refs[:3], (hidden_ref, gain_ref, ids_ref), sems)
     width = hidden_ref.shape[1]
     piece = min(width, PIECE)
-    inv_rms = inv_rms_of(hidden_ref)
+    step = width // PARTS
+    copies = [
+        pltpu.make_async_copy(refs[2], ids_ref, sems.at[0]),
+        pltpu.make_async_copy(refs[1], gain_ref, sems.at[1]),
+    ]
+    for i in range(PARTS):
+        cols = pl.ds(i * step, step)
+        copies.append(
+            pltpu.make_async_copy(refs[0].at[:, cols], hidden_ref.at[:, cols], sems.at[2 + i])
+        )
+    for copy in copies:
+        copy.start()
+    copies[0].wait()
     named, place = slots_of(ids_ref[...], me_ref[0], flight)
     select = spread(named, place, named, flight).astype(jnp.bfloat16)
+    squares = jnp.zeros((hidden_ref.shape[0], 128), jnp.float32)
+    for i in range(PARTS):
+        copies[2 + i].wait()
+        for first in range(i * step, (i + 1) * step, 128):
+            x = hidden_ref[:, first : first + 128].astype(jnp.float32)
+            squares = squares + x * x
+    inv_rms = lax.rsqrt(jnp.sum(squares, axis=1, keepdims=True) / width + EPS)
+    copies[1].wait()
     for i in range(width // piece):
         cols = pl.ds(i * piece, piece)
         normed = normed_piece(hidden_ref, gain_ref, inv_rms, cols)
@@ -274,7 +294,7 @@
         in_specs=smem(len(scalars)) + anywhere(3),
         out_specs=vmem(flight),
         scratch_shapes=[pltpu.VMEM(x.shape, x.dtype) for x in (hidden, gain, ids)]
-        + [pltpu.SemaphoreType.DMA((3,))],
+        + [pltpu.SemaphoreType.DMA((2 + PARTS,))],
         compiler_params=params(),
         cost_estimate=cost(hidden.size // 4, 128),
         name="dispatch",

time: 71.9 us -> 71.9 us (level)
  no operation moved by 1% of the time
where the time goes in v6:
time: 71.9 us; the launch traced here: 71.7 us
  starting transfers between devices  33.8 us (47%)
  Pallas kernels  19.7 us (27%)
  waiting for transfers between devices  15.9 us (22%)
  local copies, waits for them, and re-layouts  1.91 us (3%)
    ppermute x7, starting transfers between devices, end_pair(): return lax.ppermute(rows, 'expert', pairs)  23.2 us
    pallas_call x9, Pallas kernels, expert(): pl.pallas_call(expert_kernel if flag is None else expert_if_kernel, out_s...  13.2 us
    ppermute x2, waiting for transfers between devices, inward_shift(): return lax.ppermute(rows, 'expert', pairs)  7.26 us
    ppermute x6, starting transfers between devices, in_plane(): return lax.ppermute(rows, 'expert', pairs)  4.84 us
    ppermute x7, waiting for transfers between devices, end_pair(): return lax.ppermute(rows, 'expert', pairs)  4.49 us
    ppermute x6, waiting for transfers between devices, in_plane(): return lax.ppermute(rows, 'expert', pairs)  4.15 us
    ppermute x8, starting transfers between devices, mirror_pair(): return lax.ppermute(rows, 'expert', pairs)  2.96 us
    ppermute x2, starting transfers between devices, inward_shift(): return lax.ppermute(rows, 'expert', pairs)  2.75 us
  transfers between devices with their start and end apart: 23, of which 11 were waited for; matrix products, arithmetic and copies ran while one was open for 0% of the time, Pallas kernels for 23%

profile of v6, /device:TPU:0, one launch (start us, length us, event | category | flops | bytes accessed | tf_op | source)
XLA Modules:
  0.0 71.7 jit_solution(5134184230364554765)
XLA Ops:
  0.0 2.0 %dispatch.1 = (bf16[16,4096]{1,0:T(8,128)(2,1)S(1)}, bf16[16,4096]{1,0:T(8,128)(2,1)S(1)}, bf16[16,4096]{1,0:T(8,128)(2,1)S(1)}, bf16[16,4096]{1,0:T(8,128)(2,1)S(1)}) custom-call(s32[1]{0:T(128)} %bitcast.me_ref, s32[1]{0:T(128)} %bitcast.3.outer_ref.flag_ref, s32[1]{0:T(128)} %bitcast.4.inner_ref.flag_ref, bf16[128,4096]{1,0:T(8,128)(2,1)} %refs_0_.9, ...), custom_call_target="tpu_custom_call" | custom-call | flops 131072 | bytes 128 | tf_op jit(solution)/shard_map/dispatch/pallas_call | solution.py:291
  2.0 0.5 collective-permute-start
  2.6 2.6 %collective-permute-start.2 = (bf16[16,4096]{1,0:T(8,128)(2,1)S(1)}, bf16[16,4096]{1,0:T(8,128)(2,1)S(1)}, u32[]{:S(2)}, u32[]{:S(2)}) collective-permute-start(bf16[16,4096]{1,0:T(8,128)(2,1)S(1)} %get-tuple-element.15), channel_id=1, source_target_pairs={{0,2},{1,3},{2,0},{3,1},{4,6},{5,7},{6,4},{7,5},{8,10},{9,11},{10,... | collective-permute-start | bytes 393224 | tf_op jit(solution)/shard_map/plane2/ppermute | solution.py:415
  5.1 0.1 collective-permute-start.3
  5.2 0.0 collective-permute-done.refs_1_
  5.2 0.0 copy-start.1
  5.3 1.8 %collective-permute-start.1 = (bf16[32,4096]{1,0:T(8,128)(2,1)S(1)}, bf16[32,4096]{1,0:T(8,128)(2,1)S(1)}, u32[]{:S(2)}, u32[]{:S(2)}) collective-permute-start(bf16[32,4096]{1,0:T(8,128)(2,1)S(1)} %join.2.refs_1_.rows_ref), channel_id=1, source_target_pairs={{0,4},{1,5},{2,6},{3,7},{4,0},{5,1},{6,2},{7,3},{8,12},{9,13},{10,... | collective-permute-start | bytes 786440 | tf_op jit(solution)/shard_map/near_a/ppermute | solution.py:420
  7.1 0.1 collective-permute-start.4
  7.2 1.9 %copy-done.2 = bf16[1,4096,384]{2,1,0:T(8,128)(2,1)S(1)} copy-done((bf16[1,4096,384]{2,1,0:T(8,128)(2,1)S(1)}, bf16[1,4096,384]{2,1,0:T(8,128)(2,1)}, u32[]{:S(2)}) %copy-start.2) | copy-done | bytes 3145752
  9.1 0.4 collective-permute-done.2.refs_0_
  9.5 2.3 %collective-permute-done.3.refs_1_ = bf16[16,4096]{1,0:T(8,128)(2,1)S(1)} collective-permute-done((bf16[16,4096]{1,0:T(8,128)(2,1)S(1)}, bf16[16,4096]{1,0:T(8,128)(2,1)S(1)}, u32[]{:S(2)}, u32[]{:S(2)}) %collective-permute-start.3) | collective-permute-done | bytes 131104 | tf_op jit(solution)/shard_map/plane3/ppermute | solution.py:415
  11.8 1.7 %collective-permute-start.7 = (bf16[32,4096]{1,0:T(8,128)(2,1)S(1)}, bf16[32,4096]{1,0:T(8,128)(2,1)S(1)}, u32[]{:S(2)}, u32[]{:S(2)}) collective-permute-start(bf16[32,4096]{1,0:T(8,128)(2,1)S(1)} %join.3.refs_0_.rows_ref), channel_id=1, source_target_pairs={{0,4},{1,5},{2,6},{3,7},{4,0},{5,1},{6,2},{7,3},{8,12},{9,13},{10,... | collective-permute-start | bytes 786440 | tf_op jit(solution)/shard_map/near_b/ppermute | solution.py:420
  13.5 0.3 collective-permute-start.8
  13.8 0.1 collective-permute-done.1.rows_ref
  13.9 1.6 %expert.9.ours_ref.refs_0_.theirs_ref = bf16[32,4096]{1,0:T(8,128)(2,1)S(1)} custom-call(bf16[32,4096]{1,0:T(8,128)(2,1)S(1)} %collective-permute-done.1.rows_ref, bf16[1,4096,384]{2,1,0:T(8,128)(2,1)S(1)} %copy-done.3, bf16[1,4096,384]{2,1,0:T(8,128)(2,1)S(1)} %copy-done, bf16[1,384,4096]{2,1,0:T(8,128)(2,1)S(1)} %copy-done.1, ...), custom_call_target="tpu_custom_call" | custom-call | flops 301989888 | bytes 9437184 | tf_op jit(solution)/shard_map/expert/pallas_call | solution.py:382
  15.6 0.1 collective-permute-start.6
  15.7 0.0 collective-permute-done.4.theirs_ref
  15.7 3.3 %collective-permute-start.5 = (bf16[32,4096]{1,0:T(8,128)(2,1)S(1)}, bf16[32,4096]{1,0:T(8,128)(2,1)S(1)}, u32[]{:S(2)}, u32[]{:S(2)}) collective-permute-start(bf16[32,4096]{1,0:T(8,128)(2,1)S(1)} %choose.8.refs_0_), channel_id=1, source_target_pairs={{0,4},{1,5},{2,6},{3,7},{4,0},{5,1},{6,2},{7,3},{8,12},{9,13},{10,... | collective-permute-start | bytes 786440 | tf_op jit(solution)/shard_map/two_a/ppermute | solution.py:420
  19.0 2.0 %collective-permute-done.7.rows_ref = bf16[32,4096]{1,0:T(8,128)(2,1)S(1)} collective-permute-done((bf16[32,4096]{1,0:T(8,128)(2,1)S(1)}, bf16[32,4096]{1,0:T(8,128)(2,1)S(1)}, u32[]{:S(2)}, u32[]{:S(2)}) %collective-permute-start.7) | collective-permute-done | bytes 262176 | tf_op jit(solution)/shard_map/near_b/ppermute | solution.py:420
  21.0 0.0 collective-permute-start.11
  21.0 1.7 %expert.10.ours_ref.refs_0_ = bf16[32,4096]{1,0:T(8,128)(2,1)S(1)} custom-call(bf16[32,4096]{1,0:T(8,128)(2,1)S(1)} %collective-permute-done.7.rows_ref, bf16[1,4096,384]{2,1,0:T(8,128)(2,1)S(1)} %copy-done.3, bf16[1,4096,384]{2,1,0:T(8,128)(2,1)S(1)} %copy-done, bf16[1,384,4096]{2,1,0:T(8,128)(2,1)S(1)} %copy-done.1, bf16[32,4096]{1,0:T(8,128)(2,1)S(1)} %choose.8.refs_0_), custom_call_target="tpu_custom_call" | custom-call | flops 301989888 | bytes 9437184 | tf_op jit(solution)/shard_map/expert/pallas_call | solution.py:382
  22.7 0.0 collective-permute-done.8.theirs_ref
  22.7 3.2 %collective-permute-start.10 = (bf16[32,4096]{1,0:T(8,128)(2,1)S(1)}, bf16[32,4096]{1,0:T(8,128)(2,1)S(1)}, u32[]{:S(2)}, u32[]{:S(2)}) collective-permute-start(bf16[32,4096]{1,0:T(8,128)(2,1)S(1)} %choose.9.refs_1_), channel_id=1, source_target_pairs={{0,4},{1,5},{2,6},{3,7},{4,0},{5,1},{6,2},{7,3},{8,12},{9,13},{10,... | collective-permute-start | bytes 786440 | tf_op jit(solution)/shard_map/two_b/ppermute | solution.py:420
  25.9 0.0 collective-permute-done.6.refs_0_.theirs_ref
  25.9 0.3 collective-permute-done.5.ours_ref.refs_2_
  26.3 1.7 %expert.11.ours_ref.refs_0_ = bf16[32,4096]{1,0:T(8,128)(2,1)S(1)} custom-call(bf16[32,4096]{1,0:T(8,128)(2,1)S(1)} %choose.10.rows_ref.refs_0_, bf16[1,4096,384]{2,1,0:T(8,128)(2,1)S(1)} %copy-done.3, bf16[1,4096,384]{2,1,0:T(8,128)(2,1)S(1)} %copy-done, bf16[1,384,4096]{2,1,0:T(8,128)(2,1)S(1)} %copy-done.1, bf16[32,4096]{1,0:T(8,128)(2,1)S(1)} %choose.10.rows_ref.refs_0_), custom_call_target="tpu_custom_call" | custom-call | flops 301989888 | bytes 9437184 | tf_op jit(solution)/shard_map/expert/pallas_call | solution.py:382
  28.0 3.2 %collective-permute-start.9 = (bf16[32,4096]{1,0:T(8,128)(2,1)S(1)}, bf16[32,4096]{1,0:T(8,128)(2,1)S(1)}, u32[]{:S(2)}, u32[]{:S(2)}) collective-permute-start(bf16[32,4096]{1,0:T(8,128)(2,1)S(1)} %choose.11.refs_4_), channel_id=1, source_target_pairs={{0,4},{1,5},{2,6},{3,7},{4,0},{5,1},{6,2},{7,3},{8,12},{9,13},{10,... | collective-permute-start | bytes 786440 | tf_op jit(solution)/shard_map/three_a/ppermute | solution.py:420
  31.1 0.0 collective-permute-done.11.refs_0_.theirs_ref
  31.1 0.1 collective-permute-start.12
  31.2 0.8 %collective-permute-done.10.ours_ref.refs_2_ = bf16[32,4096]{1,0:T(8,128)(2,1)S(1)} collective-permute-done((bf16[32,4096]{1,0:T(8,128)(2,1)S(1)}, bf16[32,4096]{1,0:T(8,128)(2,1)S(1)}, u32[]{:S(2)}, u32[]{:S(2)}) %collective-permute-start.10) | collective-permute-done | bytes 262176 | tf_op jit(solution)/shard_map/two_b/ppermute | solution.py:420
  32.0 1.7 %expert.13.ours_ref.refs_0_ = bf16[32,4096]{1,0:T(8,128)(2,1)S(1)} custom-call(bf16[32,4096]{1,0:T(8,128)(2,1)S(1)} %choose.12.rows_ref.refs_0_, bf16[1,4096,384]{2,1,0:T(8,128)(2,1)S(1)} %copy-done.3, bf16[1,4096,384]{2,1,0:T(8,128)(2,1)S(1)} %copy-done, bf16[1,384,4096]{2,1,0:T(8,128)(2,1)S(1)} %copy-done.1, bf16[32,4096]{1,0:T(8,128)(2,1)S(1)} %choose.12.rows_ref.refs_0_), custom_call_target="tpu_custom_call" | custom-call | flops 301989888 | bytes 9437184 | tf_op jit(solution)/shard_map/expert/pallas_call | solution.py:382
  33.7 6.1 %collective-permute-start.15 = (bf16[32,4096]{1,0:T(8,128)(2,1)S(1)}, bf16[32,4096]{1,0:T(8,128)(2,1)S(1)}, u32[]{:S(2)}, u32[]{:S(2)}) collective-permute-start(bf16[32,4096]{1,0:T(8,128)(2,1)S(1)} %choose.13.refs_2_), channel_id=1, source_target_pairs={{0,4},{1,5},{2,6},{3,7},{4,0},{5,1},{6,2},{7,3},{8,12},{9,13},{10,... | collective-permute-start | bytes 786440 | tf_op jit(solution)/shard_map/three_b/ppermute | solution.py:420
  39.9 0.1 mix.4.refs_0_
  39.9 0.1 collective-permute-start.14
  40.0 1.6 %expert.14.refs_1_.ours_ref.refs_0_ = bf16[32,4096]{1,0:T(8,128)(2,1)S(1)} custom-call(bf16[32,4096]{1,0:T(8,128)(2,1)S(1)} %choose.14.rows_ref.refs_0_, bf16[1,4096,384]{2,1,0:T(8,128)(2,1)S(1)} %copy-done.3, bf16[1,4096,384]{2,1,0:T(8,128)(2,1)S(1)} %copy-done, bf16[1,384,4096]{2,1,0:T(8,128)(2,1)S(1)} %copy-done.1, ...), custom_call_target="tpu_custom_call" | custom-call | flops 301989888 | bytes 9437184 | tf_op jit(solution)/shard_map/expert/pallas_call | solution.py:382
  41.7 0.0 collective-permute-done.12.refs_0_.refs_1_
  41.7 3.9 %collective-permute-start.13 = (bf16[32,4096]{1,0:T(8,128)(2,1)S(1)}, bf16[32,4096]{1,0:T(8,128)(2,1)S(1)}, u32[]{:S(2)}, u32[]{:S(2)}) collective-permute-start(bf16[32,4096]{1,0:T(8,128)(2,1)S(1)} %choose.15.refs_2_), channel_id=1, source_target_pairs={{0,4},{1,5},{2,6},{3,7},{4,0},{5,1},{6,2},{7,3},{8,12},{9,13},{10,... | collective-permute-start | bytes 786440 | tf_op jit(solution)/shard_map/four/ppermute | solution.py:420
  45.6 0.5 collective-permute-done.15.refs_1_.refs_0_
  46.1 0.1 mix.5.refs_2_
  46.2 0.1 mix.6.refs_4_
  46.2 0.0 copy-start.4
  46.2 1.7 %expert.15.refs_1_ = bf16[32,4096]{1,0:T(8,128)(2,1)S(1)} custom-call(s32[1]{0:T(128)} %bitcast.3.outer_ref.flag_ref, bf16[32,4096]{1,0:T(8,128)(2,1)S(1)} %collective-permute-done.15.refs_1_.refs_0_, bf16[1,4096,384]{2,1,0:T(8,128)(2,1)S(1)} %copy-done.3, bf16[1,4096,384]{2,1,0:T(8,128)(2,1)S(1)} %copy-done, bf16[1,384,4096]{2,1,0:T(8,128)(2,1)S(1)} %copy-done.1, ...), custom_call_target="tpu_custom_call" | custom-call | flops 301989888 | bytes 9437184 | tf_op jit(solution)/shard_map/expert/pallas_call | solution.py:382
  47.9 2.3 %collective-permute-start.18 = (bf16[32,4096]{1,0:T(8,128)(2,1)S(1)}, bf16[32,4096]{1,0:T(8,128)(2,1)S(1)}, u32[]{:S(2)}, u32[]{:S(2)}) collective-permute-start(bf16[32,4096]{1,0:T(8,128)(2,1)S(1)} %expert.15.refs_1_), channel_id=1, source_target_pairs={{0,12},{1,13},{2,14},{3,15},{4,5},{5,4},{6,7},{7,6},{8,9},{9,8},{1... | collective-permute-start | bytes 786440 | tf_op jit(solution)/shard_map/direct_b/ppermute | solution.py:429
  50.2 1.3 %collective-permute-start.17 = (bf16[32,4096]{1,0:T(8,128)(2,1)S(1)}, bf16[32,4096]{1,0:T(8,128)(2,1)S(1)}, u32[]{:S(2)}, u32[]{:S(2)}) collective-permute-start(bf16[32,4096]{1,0:T(8,128)(2,1)S(1)} %mix.6.refs_4_), channel_id=1, source_target_pairs={{4,0},{5,1},{6,2},{7,3},{8,12},{9,13},{10,14},{11,15},{20,16},{21,... | collective-permute-start | bytes 786440 | tf_op jit(solution)/shard_map/sum_b/ppermute | solution.py:435
  51.4 0.1 collective-permute-start.19
  51.5 0.0 collective-permute-done.14.refs_0_.refs_3_
  51.5 0.8 %collective-permute-done.13.refs_1_.refs_0_ = bf16[32,4096]{1,0:T(8,128)(2,1)S(1)} collective-permute-done((bf16[32,4096]{1,0:T(8,128)(2,1)S(1)}, bf16[32,4096]{1,0:T(8,128)(2,1)S(1)}, u32[]{:S(2)}, u32[]{:S(2)}) %collective-permute-start.13) | collective-permute-done | bytes 262176 | tf_op jit(solution)/shard_map/four/ppermute | solution.py:420
  52.4 0.1 mix.7.refs_4_
  52.5 1.5 %collective-permute-start.16 = (bf16[32,4096]{1,0:T(8,128)(2,1)S(1)}, bf16[32,4096]{1,0:T(8,128)(2,1)S(1)}, u32[]{:S(2)}, u32[]{:S(2)}) collective-permute-start(bf16[32,4096]{1,0:T(8,128)(2,1)S(1)} %mix.7.refs_4_), channel_id=1, source_target_pairs={{4,12},{5,13},{6,14},{7,15},{8,0},{9,1},{10,2},{11,3},{20,28},{21,... | collective-permute-start | bytes 786440 | tf_op jit(solution)/shard_map/across_a/ppermute | solution.py:435
  53.9 2.4 %shares.1.refs_0_.weight_ref = bf16[128,128]{1,0:T(8,128)(2,1)S(1)} custom-call(s32[1]{0:T(128)} %bitcast.me_ref, bf16[128,4096]{1,0:T(8,128)(2,1)} %refs_0_.9, bf16[32,128]{1,0:T(8,128)(2,1)} %bitcast.6, s32[8,128]{1,0:T(8,128)} %bitcast.8, bf16[4096,128]{1,0:T(8,128)(2,1)S(1)} %copy-done.4, bf16[32,4096]{1,0:T(8,128)(2,1)S(1)} %mix.7.refs_4_), custom_call_target="tpu_custom_call" | custom-call | flops 134217728 | bytes 2097152 | tf_op jit(solution)/shard_map/shares/pallas_call | solution.py:306
  56.3 1.7 %expert.16.refs_0_.own_ref = bf16[32,4096]{1,0:T(8,128)(2,1)S(1)} custom-call(bf16[32,4096]{1,0:T(8,128)(2,1)S(1)} %join.3.refs_0_.rows_ref, bf16[1,4096,384]{2,1,0:T(8,128)(2,1)S(1)} %copy-done.3, bf16[1,4096,384]{2,1,0:T(8,128)(2,1)S(1)} %copy-done, bf16[1,384,4096]{2,1,0:T(8,128)(2,1)S(1)} %copy-done.1, bf16[128,128]{1,0:T(8,128)(2,1)S(1)} %shares.1.refs_0_.weight_ref), custom_call_target="tpu_custom_call" | custom-call | flops 301989888 | bytes 9437184 | tf_op jit(solution)/shard_map/expert/pallas_call | solution.py:382
  58.0 1.7 %expert.17.refs_4_.own_ref = bf16[32,4096]{1,0:T(8,128)(2,1)S(1)} custom-call(bf16[32,4096]{1,0:T(8,128)(2,1)S(1)} %join.2.refs_1_.rows_ref, bf16[1,4096,384]{2,1,0:T(8,128)(2,1)S(1)} %copy-done.3, bf16[1,4096,384]{2,1,0:T(8,128)(2,1)S(1)} %copy-done, bf16[1,384,4096]{2,1,0:T(8,128)(2,1)S(1)} %copy-done.1, bf16[32,4096]{1,0:T(8,128)(2,1)S(1)} %expert.16.refs_0_.own_ref), custom_call_target="tpu_custom_call" | custom-call | flops 301989888 | bytes 9437184 | tf_op jit(solution)/shard_map/expert/pallas_call | solution.py:382
  59.7 0.0 collective-permute-done.18.refs_1_
  59.7 3.1 %collective-permute-done.17.refs_0_ = bf16[32,4096]{1,0:T(8,128)(2,1)S(1)} collective-permute-done((bf16[32,4096]{1,0:T(8,128)(2,1)S(1)}, bf16[32,4096]{1,0:T(8,128)(2,1)S(1)}, u32[]{:S(2)}, u32[]{:S(2)}) %collective-permute-start.17) | collective-permute-done | bytes 262176 | tf_op jit(solution)/shard_map/sum_b/ppermute | solution.py:435
  62.8 0.0 collective-permute-done.19.refs_3_
  62.8 0.1 finish.2
  62.9 1.6 %collective-permute-start.21 = (bf16[16,4096]{1,0:T(8,128)(2,1)S(1)}, bf16[16,4096]{1,0:T(8,128)(2,1)S(1)}, u32[]{:S(2)}, u32[]{:S(2)}) collective-permute-start(bf16[16,4096]{1,0:T(8,128)(2,1)S(1)} %get-tuple-element.17.refs_4_), channel_id=1, source_target_pairs={{0,2},{1,3},{2,0},{3,1},{4,6},{5,7},{6,4},{7,5},{8,10},{9,11},{10,... | collective-permute-start | bytes 393224 | tf_op jit(solution)/shard_map/plane2/ppermute | solution.py:415
  64.5 0.0 collective-permute-start.22
  64.5 4.1 %collective-permute-done.16.refs_1_ = bf16[32,4096]{1,0:T(8,128)(2,1)S(1)} collective-permute-done((bf16[32,4096]{1,0:T(8,128)(2,1)S(1)}, bf16[32,4096]{1,0:T(8,128)(2,1)S(1)}, u32[]{:S(2)}, u32[]{:S(2)}) %collective-permute-start.16) | collective-permute-done | bytes 262176 | tf_op jit(solution)/shard_map/across_a/ppermute | solution.py:435
  68.6 0.1 finish.3
  68.7 0.1 collective-permute-start.20
  68.8 0.0 collective-permute-done.21.refs_2_
  68.8 1.4 %collective-permute-done.22.refs_3_ = bf16[16,4096]{1,0:T(8,128)(2,1)S(1)} collective-permute-done((bf16[16,4096]{1,0:T(8,128)(2,1)S(1)}, bf16[16,4096]{1,0:T(8,128)(2,1)S(1)}, u32[]{:S(2)}, u32[]{:S(2)}) %collective-permute-start.22) | collective-permute-done | bytes 131104 | tf_op jit(solution)/shard_map/plane3/ppermute | solution.py:415
  70.3 1.3 %combine.1 = bf16[128,4096]{1,0:T(8,128)(2,1)} custom-call(bf16[128,128]{1,0:T(8,128)(2,1)S(1)} %shares.1.refs_0_.weight_ref, bf16[16,4096]{1,0:T(8,128)(2,1)S(1)} %get-tuple-element.18.refs_0_, bf16[16,4096]{1,0:T(8,128)(2,1)S(1)} %collective-permute-done.20.refs_1_, bf16[16,4096]{1,0:T(8,128)(2,1)S(1)} %collective-permute-done.21.refs_2_, ...), custom_call_target="tpu_custom_call" | custom-call | tf_op jit(solution)/shard_map/combine/pallas_call | solution.py:396
  (26 shorter events, 0.3 us)
Async XLA Ops:
  0.0 9.1 %copy-start = (bf16[1,4096,384]{2,1,0:T(8,128)(2,1)S(1)}, bf16[1,4096,384]{2,1,0:T(8,128)(2,1)}, u32[]{:S(2)}) copy-start(bf16[1,4096,384]{2,1,0:T(8,128)(2,1)} %up_ref.13) | copy-start | bytes 9437188
  2.0 3.2 %collective-permute-start = (bf16[16,4096]{1,0:T(8,128)(2,1)S(1)}, bf16[16,4096]{1,0:T(8,128)(2,1)S(1)}, u32[]{:S(2)}, u32[]{:S(2)}) collective-permute-start(bf16[16,4096]{1,0:T(8,128)(2,1)S(1)} %get-tuple-element.14), channel_id=1, source_target_pairs={{0,1},{1,0},{2,3},{3,2},{4,5},{5,4},{6,7},{7,6},{8,9},{9,8},{10,11... | collective-permute-start | bytes 393224 | tf_op jit(solution)/shard_map/plane1/ppermute | solution.py:415
  2.6 6.9 %collective-permute-start.2 = (bf16[16,4096]{1,0:T(8,128)(2,1)S(1)}, bf16[16,4096]{1,0:T(8,128)(2,1)S(1)}, u32[]{:S(2)}, u32[]{:S(2)}) collective-permute-start(bf16[16,4096]{1,0:T(8,128)(2,1)S(1)} %get-tuple-element.15), channel_id=1, source_target_pairs={{0,2},{1,3},{2,0},{3,1},{4,6},{5,7},{6,4},{7,5},{8,10},{9,11},{10,... | collective-permute-start | bytes 393224 | tf_op jit(solution)/shard_map/plane2/ppermute | solution.py:415
  5.1 6.6 %collective-permute-start.3 = (bf16[16,4096]{1,0:T(8,128)(2,1)S(1)}, bf16[16,4096]{1,0:T(8,128)(2,1)S(1)}, u32[]{:S(2)}, u32[]{:S(2)}) collective-permute-start(bf16[16,4096]{1,0:T(8,128)(2,1)S(1)} %get-tuple-element.16), channel_id=1, source_target_pairs={{0,3},{1,2},{2,1},{3,0},{4,7},{5,6},{6,5},{7,4},{8,11},{9,10},{10,... | collective-permute-start | bytes 393224 | tf_op jit(solution)/shard_map/plane3/ppermute | solution.py:415
  5.2 3.8 %copy-start.1 = (bf16[1,384,4096]{2,1,0:T(8,128)(2,1)S(1)}, bf16[1,384,4096]{2,1,0:T(8,128)(2,1)}, u32[]{:S(2)}) copy-start(bf16[1,384,4096]{2,1,0:T(8,128)(2,1)} %down_ref.13) | copy-start | bytes 9437188
  5.3 8.7 %collective-permute-start.1 = (bf16[32,4096]{1,0:T(8,128)(2,1)S(1)}, bf16[32,4096]{1,0:T(8,128)(2,1)S(1)}, u32[]{:S(2)}, u32[]{:S(2)}) collective-permute-start(bf16[32,4096]{1,0:T(8,128)(2,1)S(1)} %join.2.refs_1_.rows_ref), channel_id=1, source_target_pairs={{0,4},{1,5},{2,6},{3,7},{4,0},{5,1},{6,2},{7,3},{8,12},{9,13},{10,... | collective-permute-start | bytes 786440 | tf_op jit(solution)/shard_map/near_a/ppermute | solution.py:420
  7.1 8.6 %collective-permute-start.4 = (bf16[32,4096]{1,0:T(8,128)(2,1)S(1)}, bf16[32,4096]{1,0:T(8,128)(2,1)S(1)}, u32[]{:S(2)}, u32[]{:S(2)}) collective-permute-start(bf16[32,4096]{1,0:T(8,128)(2,1)S(1)} %join.2.refs_1_.rows_ref), channel_id=1, source_target_pairs={{0,1},{1,0},{2,3},{3,2},{4,8},{5,9},{6,10},{7,11},{8,4},{9,5},{10,... | collective-permute-start | bytes 786440 | tf_op jit(solution)/shard_map/far_in_a/ppermute | solution.py:429
  7.2 1.9 %copy-start.2 = (bf16[1,4096,384]{2,1,0:T(8,128)(2,1)S(1)}, bf16[1,4096,384]{2,1,0:T(8,128)(2,1)}, u32[]{:S(2)}) copy-start(bf16[1,4096,384]{2,1,0:T(8,128)(2,1)} %gate_ref.13) | copy-start | bytes 9437188
  9.1 4.9 %copy-start.3 = (bf16[1,4096,384]{2,1,0:T(8,128)(2,1)S(1)}, bf16[1,4096,384]{2,1,0:T(8,128)(2,1)}, u32[]{:S(2)}) copy-start(bf16[1,4096,384]{2,1,0:T(8,128)(2,1)} %gate_ref.13) | copy-start | bytes 9437188
  11.8 9.2 %collective-permute-start.7 = (bf16[32,4096]{1,0:T(8,128)(2,1)S(1)}, bf16[32,4096]{1,0:T(8,128)(2,1)S(1)}, u32[]{:S(2)}, u32[]{:S(2)}) collective-permute-start(bf16[32,4096]{1,0:T(8,128)(2,1)S(1)} %join.3.refs_0_.rows_ref), channel_id=1, source_target_pairs={{0,4},{1,5},{2,6},{3,7},{4,0},{5,1},{6,2},{7,3},{8,12},{9,13},{10,... | collective-permute-start | bytes 786440 | tf_op jit(solution)/shard_map/near_b/ppermute | solution.py:420
  13.5 9.2 %collective-permute-start.8 = (bf16[32,4096]{1,0:T(8,128)(2,1)S(1)}, bf16[32,4096]{1,0:T(8,128)(2,1)S(1)}, u32[]{:S(2)}, u32[]{:S(2)}) collective-permute-start(bf16[32,4096]{1,0:T(8,128)(2,1)S(1)} %join.3.refs_0_.rows_ref), channel_id=1, source_target_pairs={{0,1},{1,0},{2,3},{3,2},{4,8},{5,9},{6,10},{7,11},{8,4},{9,5},{10,... | collective-permute-start | bytes 786440 | tf_op jit(solution)/shard_map/far_in_b/ppermute | solution.py:429
  15.6 10.4 %collective-permute-start.6 = (bf16[32,4096]{1,0:T(8,128)(2,1)S(1)}, bf16[32,4096]{1,0:T(8,128)(2,1)S(1)}, u32[]{:S(2)}, u32[]{:S(2)}) collective-permute-start(bf16[32,4096]{1,0:T(8,128)(2,1)S(1)} %collective-permute-done.1.rows_ref), channel_id=1, source_target_pairs={{0,1},{1,0},{2,3},{3,2},{4,8},{5,9},{6,10},{7,11},{8,4},{9,5},{10,... | collective-permute-start | bytes 786440 | tf_op jit(solution)/shard_map/last_in_a/ppermute | solution.py:429
  15.7 10.5 %collective-permute-start.5 = (bf16[32,4096]{1,0:T(8,128)(2,1)S(1)}, bf16[32,4096]{1,0:T(8,128)(2,1)S(1)}, u32[]{:S(2)}, u32[]{:S(2)}) collective-permute-start(bf16[32,4096]{1,0:T(8,128)(2,1)S(1)} %choose.8.refs_0_), channel_id=1, source_target_pairs={{0,4},{1,5},{2,6},{3,7},{4,0},{5,1},{6,2},{7,3},{8,12},{9,13},{10,... | collective-permute-start | bytes 786440 | tf_op jit(solution)/shard_map/two_a/ppermute | solution.py:420
  21.0 10.1 %collective-permute-start.11 = (bf16[32,4096]{1,0:T(8,128)(2,1)S(1)}, bf16[32,4096]{1,0:T(8,128)(2,1)S(1)}, u32[]{:S(2)}, u32[]{:S(2)}) collective-permute-start(bf16[32,4096]{1,0:T(8,128)(2,1)S(1)} %collective-permute-done.7.rows_ref), channel_id=1, source_target_pairs={{0,1},{1,0},{2,3},{3,2},{4,8},{5,9},{6,10},{7,11},{8,4},{9,5},{10,... | collective-permute-start | bytes 786440 | tf_op jit(solution)/shard_map/last_in_b/ppermute | solution.py:429
  22.7 9.3 %collective-permute-start.10 = (bf16[32,4096]{1,0:T(8,128)(2,1)S(1)}, bf16[32,4096]{1,0:T(8,128)(2,1)S(1)}, u32[]{:S(2)}, u32[]{:S(2)}) collective-permute-start(bf16[32,4096]{1,0:T(8,128)(2,1)S(1)} %choose.9.refs_1_), channel_id=1, source_target_pairs={{0,4},{1,5},{2,6},{3,7},{4,0},{5,1},{6,2},{7,3},{8,12},{9,13},{10,... | collective-permute-start | bytes 786440 | tf_op jit(solution)/shard_map/two_b/ppermute | solution.py:420
  28.0 11.9 %collective-permute-start.9 = (bf16[32,4096]{1,0:T(8,128)(2,1)S(1)}, bf16[32,4096]{1,0:T(8,128)(2,1)S(1)}, u32[]{:S(2)}, u32[]{:S(2)}) collective-permute-start(bf16[32,4096]{1,0:T(8,128)(2,1)S(1)} %choose.11.refs_4_), channel_id=1, source_target_pairs={{0,4},{1,5},{2,6},{3,7},{4,0},{5,1},{6,2},{7,3},{8,12},{9,13},{10,... | collective-permute-start | bytes 786440 | tf_op jit(solution)/shard_map/three_a/ppermute | solution.py:420
  31.1 10.6 %collective-permute-start.12 = (bf16[32,4096]{1,0:T(8,128)(2,1)S(1)}, bf16[32,4096]{1,0:T(8,128)(2,1)S(1)}, u32[]{:S(2)}, u32[]{:S(2)}) collective-permute-start(bf16[32,4096]{1,0:T(8,128)(2,1)S(1)} %expert.12.refs_0_), channel_id=1, source_target_pairs={{0,1},{1,0},{2,3},{3,2},{4,8},{5,9},{6,10},{7,11},{8,4},{9,5},{10,... | collective-permute-start | bytes 786440 | tf_op jit(solution)/shard_map/across_b/ppermute | solution.py:429
  33.7 12.4 %collective-permute-start.15 = (bf16[32,4096]{1,0:T(8,128)(2,1)S(1)}, bf16[32,4096]{1,0:T(8,128)(2,1)S(1)}, u32[]{:S(2)}, u32[]{:S(2)}) collective-permute-start(bf16[32,4096]{1,0:T(8,128)(2,1)S(1)} %choose.13.refs_2_), channel_id=1, source_target_pairs={{0,4},{1,5},{2,6},{3,7},{4,0},{5,1},{6,2},{7,3},{8,12},{9,13},{10,... | collective-permute-start | bytes 786440 | tf_op jit(solution)/shard_map/three_b/ppermute | solution.py:420
  39.9 11.6 %collective-permute-start.14 = (bf16[32,4096]{1,0:T(8,128)(2,1)S(1)}, bf16[32,4096]{1,0:T(8,128)(2,1)S(1)}, u32[]{:S(2)}, u32[]{:S(2)}) collective-permute-start(bf16[32,4096]{1,0:T(8,128)(2,1)S(1)} %mix.4.refs_0_), channel_id=1, source_target_pairs={{0,1},{1,0},{2,3},{3,2},{4,8},{5,9},{6,10},{7,11},{8,4},{9,5},{10,... | collective-permute-start | bytes 786440 | tf_op jit(solution)/shard_map/mid_a/ppermute | solution.py:429
  41.7 10.6 %collective-permute-start.13 = (bf16[32,4096]{1,0:T(8,128)(2,1)S(1)}, bf16[32,4096]{1,0:T(8,128)(2,1)S(1)}, u32[]{:S(2)}, u32[]{:S(2)}) collective-permute-start(bf16[32,4096]{1,0:T(8,128)(2,1)S(1)} %choose.15.refs_2_), channel_id=1, source_target_pairs={{0,4},{1,5},{2,6},{3,7},{4,0},{5,1},{6,2},{7,3},{8,12},{9,13},{10,... | collective-permute-start | bytes 786440 | tf_op jit(solution)/shard_map/four/ppermute | solution.py:420
  46.2 7.7 %copy-start.4 = (bf16[4096,128]{1,0:T(8,128)(2,1)S(1)}, bf16[4096,128]{1,0:T(8,128)(2,1)}, u32[]{:S(2)}) copy-start(bf16[4096,128]{1,0:T(8,128)(2,1)} %refs_3_.5) | copy-start | bytes 3145732
  47.9 11.8 %collective-permute-start.18 = (bf16[32,4096]{1,0:T(8,128)(2,1)S(1)}, bf16[32,4096]{1,0:T(8,128)(2,1)S(1)}, u32[]{:S(2)}, u32[]{:S(2)}) collective-permute-start(bf16[32,4096]{1,0:T(8,128)(2,1)S(1)} %expert.15.refs_1_), channel_id=1, source_target_pairs={{0,12},{1,13},{2,14},{3,15},{4,5},{5,4},{6,7},{7,6},{8,9},{9,8},{1... | collective-permute-start | bytes 786440 | tf_op jit(solution)/shard_map/direct_b/ppermute | solution.py:429
  50.2 12.6 %collective-permute-start.17 = (bf16[32,4096]{1,0:T(8,128)(2,1)S(1)}, bf16[32,4096]{1,0:T(8,128)(2,1)S(1)}, u32[]{:S(2)}, u32[]{:S(2)}) collective-permute-start(bf16[32,4096]{1,0:T(8,128)(2,1)S(1)} %mix.6.refs_4_), channel_id=1, source_target_pairs={{4,0},{5,1},{6,2},{7,3},{8,12},{9,13},{10,14},{11,15},{20,16},{21,... | collective-permute-start | bytes 786440 | tf_op jit(solution)/shard_map/sum_b/ppermute | solution.py:435
  51.4 11.3 %collective-permute-start.19 = (bf16[32,4096]{1,0:T(8,128)(2,1)S(1)}, bf16[32,4096]{1,0:T(8,128)(2,1)S(1)}, u32[]{:S(2)}, u32[]{:S(2)}) collective-permute-start(bf16[32,4096]{1,0:T(8,128)(2,1)S(1)} %mix.5.refs_2_), channel_id=1, source_target_pairs={{0,1},{1,0},{2,3},{3,2},{4,8},{5,9},{6,10},{7,11},{8,4},{9,5},{10,... | collective-permute-start | bytes 786440 | tf_op jit(solution)/shard_map/mid_b/ppermute | solution.py:429
  52.5 16.2 %collective-permute-start.16 = (bf16[32,4096]{1,0:T(8,128)(2,1)S(1)}, bf16[32,4096]{1,0:T(8,128)(2,1)S(1)}, u32[]{:S(2)}, u32[]{:S(2)}) collective-permute-start(bf16[32,4096]{1,0:T(8,128)(2,1)S(1)} %mix.7.refs_4_), channel_id=1, source_target_pairs={{4,12},{5,13},{6,14},{7,15},{8,0},{9,1},{10,2},{11,3},{20,28},{21,... | collective-permute-start | bytes 786440 | tf_op jit(solution)/shard_map/across_a/ppermute | solution.py:435
  62.9 5.9 %collective-permute-start.21 = (bf16[16,4096]{1,0:T(8,128)(2,1)S(1)}, bf16[16,4096]{1,0:T(8,128)(2,1)S(1)}, u32[]{:S(2)}, u32[]{:S(2)}) collective-permute-start(bf16[16,4096]{1,0:T(8,128)(2,1)S(1)} %get-tuple-element.17.refs_4_), channel_id=1, source_target_pairs={{0,2},{1,3},{2,0},{3,1},{4,6},{5,7},{6,4},{7,5},{8,10},{9,11},{10,... | collective-permute-start | bytes 393224 | tf_op jit(solution)/shard_map/plane2/ppermute | solution.py:415
  64.5 5.8 %collective-permute-start.22 = (bf16[16,4096]{1,0:T(8,128)(2,1)S(1)}, bf16[16,4096]{1,0:T(8,128)(2,1)S(1)}, u32[]{:S(2)}, u32[]{:S(2)}) collective-permute-start(bf16[16,4096]{1,0:T(8,128)(2,1)S(1)} %get-tuple-element.20), channel_id=1, source_target_pairs={{0,3},{1,2},{2,1},{3,0},{4,7},{5,6},{6,5},{7,4},{8,11},{9,10},{10,... | collective-permute-start | bytes 393224 | tf_op jit(solution)/shard_map/plane3/ppermute | solution.py:415
  68.7 1.5 %collective-permute-start.20 = (bf16[16,4096]{1,0:T(8,128)(2,1)S(1)}, bf16[16,4096]{1,0:T(8,128)(2,1)S(1)}, u32[]{:S(2)}, u32[]{:S(2)}) collective-permute-start(bf16[16,4096]{1,0:T(8,128)(2,1)S(1)} %get-tuple-element.19), channel_id=1, source_target_pairs={{0,1},{1,0},{2,3},{3,2},{4,5},{5,4},{6,7},{7,6},{8,9},{9,8},{10,11... | collective-permute-start | bytes 393224 | tf_op jit(solution)/shard_map/plane1/ppermute | solution.py:415
